TPU v7x, 512 devices: a whole 4x4x16 slice. The times are simulated.
512 devices in a mesh: row: 32 (over y, x, core), col: 16 (over z).
Axes of the slice: x: 4, y: 4, z: 16, core: 2. Of those that a mesh axis runs over, the one named last changes fastest.
Arguments:
- x_start: bfloat16 [64, 131072], P(None, ('row', 'col')), may hold values from -6 to 6
- weights: float32 [131072], P(('row', 'col')), may hold values from 1 to 10
- blocks: bfloat16 [4608, 512, 512], P(('row', 'col')), may hold values from -0.25 to 0.25
- block_rows: int32 [4608], P(('row', 'col')), may hold values from 0 to 7
- block_cols: int32 [4608], P(('row', 'col')), may hold values from 0 to 15
- live_blocks: int32 [512], P(('row', 'col')), may hold values from 1 to 9, as said below
Outputs:
- embedding: bfloat16 [64, 131072], P(None, ('row', 'col'))
Inputs may be any that keep to these rules, and one draw needn't show every extreme that they name: `live_blocks`: some cell has all 9 slots live.
All inputs are finite; a program needn't handle non-finite values.
Results may differ from a plain program's by a relative error of at most 0.023.
Values may be sent and summed in bfloat16 or wider, within the bound.
No kernel may reach another device: no remote copies, remote signals or barrier semaphores. Data moves between devices by JAX's collectives and lax.ppermute only.
A program may use at most 64 MiB of HBM per device.

v0:
```python
import jax
import jax.numpy as jnp
from jax import lax
from jax.sharding import PartitionSpec as P

ITERS = 2


def scale_columns(panel, gains):
    return (panel.astype(jnp.float32) * gains[None, :]).astype(jnp.bfloat16)


def whiten(lower_inverse, panel, level):
    return jnp.dot(lower_inverse, panel.astype(jnp.float32), precision=level).astype(jnp.bfloat16)


def cell_products(row_panel, col_panel, blocks, block_rows, block_cols, live_count):
    vector_count = row_panel.shape[0]
    tile_size = blocks.shape[1]
    slot_count = blocks.shape[0]
    row_tiles = row_panel.shape[1] // tile_size
    col_tiles = col_panel.shape[1] // tile_size
    live_mask = (jnp.arange(slot_count, dtype=jnp.int32) < live_count).astype(jnp.float32)
    picked_cols = jnp.take(
        col_panel.reshape(vector_count, col_tiles, tile_size), block_cols, axis=1
    )
    picked_rows = jnp.take(
        row_panel.reshape(vector_count, row_tiles, tile_size), block_rows, axis=1
    )
    direct = jnp.einsum("ksj,sij->ksi", picked_cols, blocks, preferred_element_type=jnp.float32)
    mirror = jnp.einsum("ksi,sij->ksj", picked_rows, blocks, preferred_element_type=jnp.float32)
    row_hot = (block_rows[:, None] == jnp.arange(row_tiles, dtype=jnp.int32)[None, :]).astype(
        jnp.float32
    ) * live_mask[:, None]
    col_hot = (block_cols[:, None] == jnp.arange(col_tiles, dtype=jnp.int32)[None, :]).astype(
        jnp.float32
    ) * live_mask[:, None]
    direct_sum = jnp.einsum("sa,ksi->kai", row_hot, direct, precision=lax.Precision.HIGH).reshape(
        vector_count, row_tiles * tile_size
    )
    mirror_sum = jnp.einsum("sb,ksj->kbj", col_hot, mirror, precision=lax.Precision.HIGH).reshape(
        vector_count, col_tiles * tile_size
    )
    return (direct_sum, mirror_sum)


def body(x_start, weights, blocks, block_rows, block_cols, live_blocks):
    vector_count, shard_rows = x_start.shape
    row_devices = lax.axis_size("row")
    total_rows = float(shard_rows * row_devices * lax.axis_size("col"))
    identity = jnp.eye(vector_count, dtype=jnp.float32)
    live_count = live_blocks[0]
    current = x_start
    fresh_panel = x_start
    lower_inverse = identity
    for sweep_index in range(ITERS):
        scaled = scale_columns(current, weights)
        row_panel = lax.all_gather(scaled, "col", axis=1, tiled=True)
        col_panel = lax.all_gather(scaled, "row", axis=1, tiled=True)
        direct_sum, mirror_sum = cell_products(
            row_panel, col_panel, blocks, block_rows, block_cols, live_count
        )
        own_direct = lax.psum_scatter(
            direct_sum.astype(jnp.bfloat16), "col", scatter_dimension=1, tiled=True
        ).astype(jnp.float32)
        outgoing = mirror_sum.astype(jnp.bfloat16).reshape(vector_count, row_devices, shard_rows)
        arrived = lax.all_to_all(outgoing, "row", split_axis=1, concat_axis=1, tiled=True)
        own_mirror = jnp.sum(arrived, axis=1, dtype=jnp.float32)
        fresh_panel = ((own_direct + own_mirror) * weights[None, :]).astype(jnp.bfloat16)
        gram_part = lax.dot_general(
            fresh_panel, fresh_panel, (((1,), (1,)), ((), ())), preferred_element_type=jnp.float32
        )
        gram_matrix = lax.psum(gram_part, ("row", "col")) / total_rows + 1e-06 * identity
        lower_factor = jnp.linalg.cholesky(gram_matrix)
        lower_inverse = lax.linalg.triangular_solve(
            lower_factor, identity, left_side=True, lower=True
        )
        current = whiten(lower_inverse, fresh_panel, lax.Precision.HIGHEST)
    return current


def solution(mesh):
    in_specs = (
        P(None, ("row", "col")),
        P(("row", "col")),
        P(("row", "col"), None, None),
        P(("row", "col")),
        P(("row", "col")),
        P(("row", "col")),
    )
    out_specs = P(None, ("row", "col"))
    return jax.shard_map(body, mesh=mesh, in_specs=in_specs, out_specs=out_specs, check_vma=False)
```

profile of v0, /device:TPU:1, one launch (start us, length us, event | category | flops | bytes accessed | tf_op | source)
XLA Modules:
  0.0 534.0 jit_solution(11481595839486044659)
XLA Ops:
  6.5 1.4 multiply_convert_fusion.2
  8.0 32.1 %all_gather.13 = bf16[64,4096]{1,0:T(8,128)(2,1)S(1)} all-gather(bf16[64,256]{1,0:T(8,128)(2,1)} %multiply_convert_fusion.2), channel_id=1, replica_groups=mesh['row'=32,'col'=16] {'col'}, dimensions={1}, use_global_device_ids=true | all-gather | bytes 557056 | tf_op jit(solution)/shard_map/all_gather | solution.py:58
  40.7 0.7 compare_select_fusion.1
  41.4 0.6 gather_fusion.1
  42.0 3.3 convolution_bitcast_fusion.2
  45.4 1.8 fusion.17
  47.1 0.4 convert_element_type.102
  47.5 1.6 copy.23
  49.1 15.3 %all-to-all-start = ((bf16[64,32,256]{2,0,1:T(8,128)(2,1)}), bf16[64,32,256]{2,0,1:T(8,128)(2,1)S(1)}, u32[]{:S(2)}, u32[]{:S(2)}) async-start(bf16[64,32,256]{2,0,1:T(8,128)(2,1)} %copy.23), calls=%async_computation.1 | async-start | bytes 2097152 | tf_op jit(solution)/shard_map/all_to_all | solution.py:67
  64.6 12.7 %all-gather.3.cloned.1.call-done = bf16[64,8192]{1,0:T(8,128)(2,1)} async-done(((bf16[64,256]{1,0:T(8,128)(2,1)}), bf16[64,8192]{1,0:T(8,128)(2,1)}) %all-gather.3.cloned.1.call-update) | async-done | bytes 1048592 | tf_op jit(solution)/shard_map/all_gather | solution.py:59
  77.2 1.3 copy.66
  78.5 0.6 gather_fusion
  79.1 3.9 convolution_bitcast_fusion.3
  83.0 1.6 fusion.20
  84.7 1.0 copy.39
  85.7 0.2 convert_reduce_fusion.1
  85.9 61.8 %reduce-scatter.3.cloned.1.call-done = bf16[64,256]{1,0:T(8,128)(2,1)} async-done(((bf16[64,4096]{1,0:T(8,128)(2,1)}), bf16[64,256]{1,0:T(8,128)(2,1)}) %reduce-scatter.3.cloned.1.call-update) | async-done | bytes 32784 | tf_op jit(solution)/shard_map/reduce_scatter | solution.py:63
  147.6 1.0 fusion.85
  148.6 111.5 %psum.14 = f32[64,64]{0,1:T(8,128)S(1)} all-reduce(f32[64,64]{0,1:T(8,128)S(1)} %fusion.85), channel_id=1, replica_groups=mesh['row'=32,'col'=16] {'row','col'}, use_global_device_ids=true, to_apply=%region_2.5 | all-reduce | flops 4096 | bytes 32768 | tf_op jit(solution)/shard_map/psum | solution.py:73
  260.2 5.8 %cholesky.44 = f32[64,64]{1,0:T(8,128)S(1)} custom-call(f32[64,64]{1,0:T(8,128)S(1)} %fusion.54), custom_call_target="Cholesky" | custom-call | tf_op jit(solution)/shard_map/jit(cholesky)/cholesky | solution.py:74
  266.1 0.6 compare_reduce_fusion.1
  266.8 0.7 fusion.49
  267.4 4.9 custom-call.6
  272.3 0.3 fusion.47
  272.6 1.5 fusion.28
  274.2 24.3 %all_gather.15 = bf16[64,4096]{1,0:T(8,128)(2,1)S(1)} all-gather(bf16[64,256]{1,0:T(8,128)(2,1)} %fusion.28), channel_id=1, replica_groups=mesh['row'=32,'col'=16] {'col'}, dimensions={1}, use_global_device_ids=true | all-gather | bytes 557056 | tf_op jit(solution)/shard_map/all_gather | solution.py:58
  298.5 0.6 gather_fusion.3
  299.1 3.3 convolution_bitcast_fusion
  302.4 1.8 fusion.14
  304.2 0.4 convert_element_type.115
  304.6 1.6 copy.30
  306.2 11.7 %all-to-all-start.1 = ((bf16[64,32,256]{2,0,1:T(8,128)(2,1)}), bf16[64,32,256]{2,0,1:T(8,128)(2,1)S(1)}, u32[]{:S(2)}, u32[]{:S(2)}) async-start(bf16[64,32,256]{2,0,1:T(8,128)(2,1)} %copy.30), calls=%async_computation.3 | async-start | bytes 2097152 | tf_op jit(solution)/shard_map/all_to_all | solution.py:67
  317.9 13.2 %all-gather.5.cloned.1.call-done = bf16[64,8192]{1,0:T(8,128)(2,1)} async-done(((bf16[64,256]{1,0:T(8,128)(2,1)}), bf16[64,8192]{1,0:T(8,128)(2,1)}) %all-gather.5.cloned.1.call-update) | async-done | bytes 1048592 | tf_op jit(solution)/shard_map/all_gather | solution.py:59
  331.2 1.3 copy.65
  332.5 0.6 gather_fusion.2
  333.1 3.9 convolution_bitcast_fusion.1
  337.0 1.6 fusion.23
  338.6 1.0 copy.40
  339.7 0.2 convert_reduce_fusion
  339.8 61.7 %reduce-scatter.5.cloned.1.call-done = bf16[64,256]{1,0:T(8,128)(2,1)} async-done(((bf16[64,4096]{1,0:T(8,128)(2,1)}), bf16[64,256]{1,0:T(8,128)(2,1)}) %reduce-scatter.5.cloned.1.call-update) | async-done | bytes 32784 | tf_op jit(solution)/shard_map/reduce_scatter | solution.py:63
  401.5 0.8 multiply_convert_fusion
  402.4 111.9 %psum.15 = f32[64,64]{0,1:T(8,128)S(1)} all-reduce(f32[64,64]{0,1:T(8,128)S(1)} %fusion.86), channel_id=1, replica_groups=mesh['row'=32,'col'=16] {'row','col'}, use_global_device_ids=true, to_apply=%region_7.0 | all-reduce | flops 4096 | bytes 32768 | tf_op jit(solution)/shard_map/psum | solution.py:73
  514.4 5.8 %cholesky.55 = f32[64,64]{1,0:T(8,128)S(1)} custom-call(f32[64,64]{1,0:T(8,128)S(1)} %fusion.52), custom_call_target="Cholesky" | custom-call | tf_op jit(solution)/shard_map/jit(cholesky)/cholesky | solution.py:74
  520.3 0.6 compare_reduce_fusion
  520.9 0.7 fusion.50
  521.6 4.9 custom-call.7
  526.5 0.3 fusion.45
  526.7 0.8 convolution_convert_fusion
  (33 shorter events, 0.7 us)
Async XLA Ops:
  6.5 35.5 %copy-start.2 = (s32[9]{0:T(128)S(1)}, s32[9]{0:T(128)}, u32[]{:S(2)}) copy-start(s32[9]{0:T(128)} %param.16) | copy-start | bytes 112
  6.5 70.7 %all-gather.3.cloned.1.call-start = ((), (), s32[]{:S(2)}) async-start(), calls=%async_computation.4 | async-start | bytes 1081344 | tf_op jit(solution)/shard_map/all_gather | solution.py:59
  42.0 3.3 copy-start.1
  49.1 36.6 %all-to-all-start = ((bf16[64,32,256]{2,0,1:T(8,128)(2,1)}), bf16[64,32,256]{2,0,1:T(8,128)(2,1)S(1)}, u32[]{:S(2)}, u32[]{:S(2)}) async-start(bf16[64,32,256]{2,0,1:T(8,128)(2,1)} %copy.23), calls=%async_computation.1 | async-start | bytes 2097152 | tf_op jit(solution)/shard_map/all_to_all | solution.py:67
  64.5 83.2 %reduce-scatter.3.cloned.1.call-start = ((), (), s32[]{:S(2)}) async-start(), calls=%async_computation.5 | async-start | bytes 557056 | tf_op jit(solution)/shard_map/reduce_scatter | solution.py:63
  83.0 64.6 %copy-start = (f32[256]{0:T(256)S(1)}, f32[256]{0:T(256)}, u32[]{:S(2)}) copy-start(f32[256]{0:T(256)} %param.14) | copy-start | bytes 3076
  85.7 245.5 %all-gather.5.cloned.1.call-start = ((), (), s32[]{:S(2)}) async-start(), calls=%async_computation.6 | async-start | bytes 1081344 | tf_op jit(solution)/shard_map/all_gather | solution.py:59
  306.2 33.5 %all-to-all-start.1 = ((bf16[64,32,256]{2,0,1:T(8,128)(2,1)}), bf16[64,32,256]{2,0,1:T(8,128)(2,1)S(1)}, u32[]{:S(2)}, u32[]{:S(2)}) async-start(bf16[64,32,256]{2,0,1:T(8,128)(2,1)} %copy.30), calls=%async_computation.3 | async-start | bytes 2097152 | tf_op jit(solution)/shard_map/all_to_all | solution.py:67
  317.9 83.6 %reduce-scatter.5.cloned.1.call-start = ((), (), s32[]{:S(2)}) async-start(), calls=%async_computation.7 | async-start | bytes 557056 | tf_op jit(solution)/shard_map/reduce_scatter | solution.py:63
Sparse Core Ops, SparseCore 0:
  10.4 66.7 all-gather.2
  85.8 61.8 reduce-scatter.2
  274.3 56.8 all-gather.4
  339.8 61.6 reduce-scatter.4
where the time goes:
time: 535 us; the launch traced here: 534 us
  blocking collectives  280 us (52%)
  waiting for transfers between devices  149 us (28%)
  other arithmetic  27.4 us (5%)
  starting transfers between devices  27.2 us (5%)
  matrix products  25.1 us (5%)
  between operations  14.1 us (3%)
  local copies, waits for them, and re-layouts  11.2 us (2%)
    psum x2, blocking collectives, body(): lax.psum(gram_part, ('row', 'col')) / total_rows + 1e-06 * identity  223 us
    reduce_scatter x2, waiting for transfers between devices, body(): lax.psum_scatter(direct_sum.astype(jnp.bfloat16), 'col', scatter_dimensio...  123 us
    all_gather x2, blocking collectives, body(): row_panel = lax.all_gather(scaled, 'col', axis=1, tiled=True)  56.4 us
    all_to_all x2, starting transfers between devices, body(): lax.all_to_all(outgoing, 'row', split_axis=1, concat_axis=1, tiled=True)  27 us
    all_gather x2, waiting for transfers between devices, body(): col_panel = lax.all_gather(scaled, 'row', axis=1, tiled=True)  25.9 us
    another operation x6, other arithmetic, body(): lower_factor = jnp.linalg.cholesky(gram_matrix)  13 us
    another operation x4, other arithmetic, body(): lax.linalg.triangular_solve(lower_factor, identity, left_side=True, lower...  11.1 us
  transfers between devices with their start and end apart: 6, of which 4 were waited for; matrix products, arithmetic and copies ran while one was open for 6% of the time, Pallas kernels for 0%

commit v1 on v0

v1 whole, which is shorter than its diff:
```python
import functools

import jax
import jax.numpy as jnp
from jax import lax
from jax.experimental import pallas as pl
from jax.experimental.pallas import tpu as pltpu
from jax.sharding import Mesh, PartitionSpec as P

F32 = jnp.float32
BF16 = jnp.bfloat16
ROW = ("y", "x", "core")
RIDGE = 1e-06
VMEM = pl.BlockSpec(memory_space=pltpu.VMEM)
SMEM = pl.BlockSpec(memory_space=pltpu.SMEM)
PARAMS = pltpu.CompilerParams(vmem_limit_bytes=48 * 1024 * 1024)
NT = (((1,), (1,)), ((), ()))
NN = (((1,), (0,)), ((), ()))


def call(kernel, outs, ins, scratch=(), flops=0, moved=0):
    return pl.pallas_call(
        kernel,
        out_shape=[jax.ShapeDtypeStruct(s, d) for s, d in outs],
        in_specs=ins,
        out_specs=[VMEM] * len(outs),
        scratch_shapes=list(scratch),
        compiler_params=PARAMS,
        cost_estimate=pl.CostEstimate(flops=flops, bytes_accessed=moved, transcendentals=0),
    )


def start_tiles(blocks, held, sems):
    slots = held.shape[0]
    copies = [pltpu.make_async_copy(blocks.at[s], held.at[s], sems.at[s]) for s in range(slots)]
    for copy in copies:
        copy.start()
    return copies


def direct_kernel(rows, cols, live, panel, blocks, out, held, total, sems):
    copies = start_tiles(blocks, held, sems)
    total[...] = jnp.zeros_like(total)
    half = panel.shape[2]
    for s, copy in enumerate(copies):
        copy.wait()

        @pl.when(s < live[0])
        def _():
            r, c = rows[s], cols[s]
            part = lax.dot_general(
                panel[2 * c], held[s, :, :half], NT, preferred_element_type=F32
            ) + lax.dot_general(panel[2 * c + 1], held[s, :, half:], NT, preferred_element_type=F32)
            total[2 * r] += part[:, :half]
            total[2 * r + 1] += part[:, half:]

    out[...] = total[...].astype(BF16)


def mirror_kernel(rows, cols, live, panel, blocks, keep, send, held, total, sems):
    copies = start_tiles(blocks, held, sems)
    total[...] = jnp.zeros_like(total)
    half = panel.shape[2]
    for s, copy in enumerate(copies):
        copy.wait()

        @pl.when(s < live[0])
        def _():
            r, c = rows[s], cols[s]
            part = lax.dot_general(
                panel[2 * r], held[s, :half, :], NN, preferred_element_type=F32
            ) + lax.dot_general(panel[2 * r + 1], held[s, half:, :], NN, preferred_element_type=F32)
            total[2 * c] += part[:, :half]
            total[2 * c + 1] += part[:, half:]

    me = lax.axis_index("core")
    for chip in range(keep.shape[0]):
        keep[chip] = total[2 * chip + me].astype(BF16)
        send[chip] = total[2 * chip + 1 - me].astype(BF16)


def merge_x_kernel(keep, got, *pieces):
    me = lax.axis_index("x")
    n = len(pieces)
    for k, piece in enumerate(pieces):
        to = lax.rem(me + k, n)
        for y in range(piece.shape[0]):
            piece[y] = (keep[y * n + to].astype(F32) + got[y * n + to].astype(F32)).astype(BF16)


def merge_y_kernel(own, *refs):
    n = own.shape[0]
    got, pieces = refs[: n - 1], refs[n - 1 :]
    me = lax.axis_index("y")
    for k, piece in enumerate(pieces):
        to = lax.rem(me + k, n)
        sums = own[to].astype(F32)
        for g in got:
            sums += g[to].astype(F32)
        piece[...] = sums.astype(BF16)


def spread(value, scaled, copies):
    scaled[...] = value
    for k in range(copies.shape[0]):
        copies[k] = value


def prepare_kernel(x, weights, scaled, copies):
    spread((x[...].astype(F32) * weights[...]).astype(BF16), scaled, copies)


def add_up(arrived, own, others, weights):
    sums = own[...].astype(F32)
    for other in others:
        sums += other[...].astype(F32)
    for k in range(arrived.shape[0]):
        sums += arrived[k].astype(F32)
    return sums * weights[...]


def between_kernel(arrived, weights, own, s1, s2, s3, scaled, copies, gram):
    fresh = add_up(arrived, own, (s1, s2, s3), weights)
    spread((fresh * weights[...]).astype(BF16), scaled, copies)
    rounded = fresh.astype(BF16)
    gram[...] = lax.dot_general(rounded, rounded, NT, preferred_element_type=F32)


def fold(matrix):
    h = matrix.shape[0] // 2
    return jnp.concatenate([matrix[:h], matrix[h:]], axis=1)


def last_kernel(scale, arrived, weights, own, s1, s2, s3, first, fresh, keep, send):
    rounded = add_up(arrived, own, (s1, s2, s3), weights).astype(BF16)
    fresh[...] = rounded
    gram = lax.dot_general(rounded, rounded, NT, preferred_element_type=F32)
    gram = (gram + RIDGE * first[...]) * scale
    h = gram.shape[0] // 2
    low, high = fold(gram[:h]), fold(gram[h:])
    second = lax.axis_index("core") == 1
    keep[...] = jnp.where(second, high, low)
    send[...] = jnp.where(second, low, high)


def whiten_kernel(parts, fresh, out, factor):
    n = fresh.shape[0]
    halves = [parts[0], parts[1]]
    matrix = jnp.concatenate([p for h in halves for p in (h[:, :n], h[:, n:])], axis=0)
    eye = (
        lax.broadcasted_iota(jnp.int32, (n, n), 0) == lax.broadcasted_iota(jnp.int32, (n, n), 1)
    ).astype(F32)
    left = jnp.concatenate([matrix + RIDGE * RIDGE * eye, eye], axis=1)
    base = 0
    for j in range(0, n, 2):
        if j - base == 8:
            left = left[8:]
            base = j
        i = j - base
        row0, row1 = left[i : i + 1], left[i + 1 : i + 2]
        col0, col1 = left[:, j : j + 1], left[:, j + 1 : j + 2]
        p0, q = row0[:, j : j + 1], row0[:, j + 1 : j + 2]
        inv0 = 1.0 / p0
        t = q * inv0
        p1 = row1[:, j + 1 : j + 2] - q * t
        inv1 = 1.0 / p1
        row1 = row1 - t * row0
        col1 = col1 - t * col0
        factor[j : j + 1] = row0 * (1.0 / jnp.sqrt(p0))
        factor[j + 1 : j + 2] = row1 * (1.0 / jnp.sqrt(p1))
        left = left - (col0 * inv0) * row0 - (col1 * inv1) * row1
    inverse = factor[:, n:]
    out[...] = lax.dot_general(
        inverse,
        fresh[...].astype(F32),
        NN,
        precision=lax.Precision.HIGHEST,
        preferred_element_type=F32,
    ).astype(BF16)


def swap(value, axis, shift, size):
    return lax.ppermute(value, axis, [(i, (i + shift) % size) for i in range(size)])


def exchange(value, axes):
    return lax.all_to_all(value, axes, split_axis=0, concat_axis=0, tiled=True)


def body(x_start, weights, blocks, block_rows, block_cols, live_blocks):
    k, own = x_start.shape
    slots, tile, _ = blocks.shape
    ny, nx, nz = lax.axis_size("y"), lax.axis_size("x"), lax.axis_size("z")
    rows = 2 * ny * nx
    vertices = float(own * rows * nz)
    gains = weights.reshape(1, own)
    any_spec = pl.BlockSpec(memory_space=pl.ANY)
    flops = 2 * slots * k * tile * tile
    held = pltpu.VMEM((slots, tile, tile), BF16)
    sems = pltpu.SemaphoreType.DMA((slots,))
    panel_in = [SMEM] * 3 + [VMEM, any_spec]

    scaled, copies = call(
        prepare_kernel, [((k, own), BF16), ((rows, k, own), BF16)], [VMEM] * 2
    )(x_start, gains)
    gram = None
    for sweep in range(2):
        with jax.named_scope("gather_plane"):
            col_panel = exchange(copies, ROW)
        with jax.named_scope("gather_line"):
            row_panel = lax.all_gather(scaled, "z", axis=0)
        col_panel, row_panel = lax.optimization_barrier((col_panel, row_panel))
        with jax.named_scope("mirror"):
            keep, send = call(
                mirror_kernel,
                [((ny * nx, k, own), BF16)] * 2,
                panel_in,
                [held, pltpu.VMEM((rows, k, own), F32), sems],
                flops,
                blocks.size * 2,
            )(block_rows, block_cols, live_blocks, row_panel, blocks)
        with jax.named_scope("core_swap"):
            got = swap(send, "core", 1, 2)
        col_panel, send = lax.optimization_barrier((col_panel, send))
        with jax.named_scope("direct"):
            (direct,) = call(
                direct_kernel,
                [((nz, k, own), BF16)],
                panel_in,
                [held, pltpu.VMEM((nz, k, own), F32), sems],
                flops,
                blocks.size * 2,
            )(block_rows, block_cols, live_blocks, col_panel, blocks)
        with jax.named_scope("reduce_line"):
            arrived = exchange(direct, "z")
        with jax.named_scope("reduce_x"):
            pieces = call(merge_x_kernel, [((ny, k, own), BF16)] * nx, [VMEM] * 2)(keep, got)
            moved = [pieces[0]] + [swap(pieces[s], "x", s, nx) for s in range(1, nx)]
        with jax.named_scope("reduce_y"):
            pieces = call(merge_y_kernel, [((k, own), BF16)] * ny, [VMEM] * nx)(*moved)
            moved = [pieces[0]] + [swap(pieces[s], "y", s, ny) for s in range(1, ny)]
        if sweep == 0:
            with jax.named_scope("between"):
                scaled, copies, gram = call(
                    between_kernel,
                    [((k, own), BF16), ((rows, k, own), BF16), ((k, k), F32)],
                    [VMEM] * 6,
                )(arrived, gains, *moved)
        else:
            with jax.named_scope("last"):
                fresh, keep, send = call(
                    functools.partial(last_kernel, 1.0 / vertices),
                    [((k, own), BF16)] + [((k // 4, 2 * k), F32)] * 2,
                    [VMEM] * 7,
                )(arrived, gains, *moved, gram)
    with jax.named_scope("gram_core"):
        part = keep + swap(send, "core", 1, 2)
    with jax.named_scope("gram_plane"):
        copies = jnp.broadcast_to(part[None], (ny * nx,) + part.shape)
        part = jnp.sum(exchange(copies, ("y", "x")), axis=0)
    with jax.named_scope("gram_line"):
        copies = jnp.broadcast_to(part[None], (nz,) + part.shape)
        part = jnp.sum(exchange(copies, "z"), axis=0)
    with jax.named_scope("gram_pair"):
        parts = lax.all_gather(part, "core", axis=0)
    with jax.named_scope("whiten"):
        (out,) = call(
            whiten_kernel,
            [((k, own), BF16)],
            [VMEM] * 2,
            [pltpu.VMEM((k, 2 * k), F32)],
        )(parts, fresh)
    return out


def solution(mesh):
    fine = Mesh(mesh.devices.reshape(4, 4, 2, 16), ("y", "x", "core", "z"))
    cells = ("y", "x", "core", "z")
    return jax.shard_map(
        body,
        mesh=fine,
        in_specs=(P(None, cells), P(cells), P(cells, None, None), P(cells), P(cells), P(cells)),
        out_specs=P(None, cells),
        check_vma=False,
    )
```

time: 535 us -> 239 us (0.45)
  blocking collectives: 280 us -> 99 us
  waiting for transfers between devices: 149 us -> 13.3 us
  starting transfers between devices: 27.2 us -> 98.8 us
  other arithmetic: 27.4 us -> 0.04 us
  matrix products: 25.1 us -> 0 us
  Pallas kernels: 0 us -> 23.1 us
  between operations: 14.1 us -> 0.95 us
  local copies, waits for them, and re-layouts: 11.2 us -> 2.79 us
    psum x2 -> x0, blocking collectives: 223 us -> none  [body(): lax.psum(gram_part, ('row', 'col')) / total_rows + 1e-06 * identity]
    reduce_scatter x2 -> x0, waiting for transfers between devices: 123 us -> none  [body(): lax.psum_scatter(direct_sum.astype(jnp.bfloat16), 'col', scatter_dimensio...]
    ppermute x0 -> x15, starting transfers between devices: none -> 63.6 us  [swap(): lax.ppermute(value, axis, [(i, (i + shift) % size) for i in range(size)])]
    all_to_all x0 -> x2, blocking collectives: none -> 35.9 us  [exchange(): return lax.all_to_all(value, axes, split_axis=0, concat_axis=0, tiled=True)]
    all_gather x2 -> x0, waiting for transfers between devices: 25.9 us -> none  [body(): col_panel = lax.all_gather(scaled, 'row', axis=1, tiled=True)]
    dot_general x12 -> x0, matrix products: 24.6 us -> none  [the longest x2 7.76 us: cell_products(): jnp.einsum('ksj,sij->ksi', picked_cols, blocks, preferred_element_type=jn...]
    another operation x10 -> x0, other arithmetic: 24.1 us -> none  [the longest x6 13 us: body(): lower_factor = jnp.linalg.cholesky(gram_matrix)]
    pallas_call x0 -> x12, Pallas kernels: none -> 23.1 us  [the longest x2 7.93 us: body(): call(direct_kernel, [((nz, k, own), BF16)], panel_in, [held, pltpu.VMEM((...]
  transfers between devices with their start and end apart: 6 -> 19, of which waited for: 4 -> 9; matrix products, arithmetic and copies ran while one was open for 6% -> 0% of each run, Pallas kernels for 0% -> 0%
where the time goes in v1:
time: 239 us; the launch traced here: 238 us
  blocking collectives  99 us (41%)
  starting transfers between devices  98.8 us (41%)
  Pallas kernels  23.1 us (10%)
  waiting for transfers between devices  13.3 us (6%)
  local copies, waits for them, and re-layouts  2.79 us (1%)
    ppermute x15, starting transfers between devices, swap(): lax.ppermute(value, axis, [(i, (i + shift) % size) for i in range(size)])  63.6 us
    all_gather x2, blocking collectives, body(): row_panel = lax.all_gather(scaled, 'z', axis=0)  57.7 us
    all_to_all x2, blocking collectives, exchange(): return lax.all_to_all(value, axes, split_axis=0, concat_axis=0, tiled=True)  35.9 us
    all_to_all x4, starting transfers between devices, exchange(): return lax.all_to_all(value, axes, split_axis=0, concat_axis=0, tiled=True)  35.1 us
    ppermute x15, waiting for transfers between devices, swap(): lax.ppermute(value, axis, [(i, (i + shift) % size) for i in range(size)])  13.3 us
    pallas_call x2, Pallas kernels, body(): call(direct_kernel, [((nz, k, own), BF16)], panel_in, [held, pltpu.VMEM((...  7.93 us
    pallas_call x1, Pallas kernels, body(): call(whiten_kernel, [((k, own), BF16)], [VMEM] * 2, [pltpu.VMEM((k, 2 * k...  6.22 us
    pallas_call x2, Pallas kernels, body(): call(mirror_kernel, [((ny * nx, k, own), BF16)] * 2, panel_in, [held, plt...  6.06 us
  transfers between devices with their start and end apart: 19, of which 9 were waited for; matrix products, arithmetic and copies ran while one was open for 0% of the time, Pallas kernels for 0%

profile of v1, /device:TPU:1, one launch (start us, length us, event | category | flops | bytes accessed | tf_op | source)
XLA Modules:
  0.0 238.1 jit_solution(7168376253610245445)
XLA Ops:
  0.0 0.8 copy-done
  0.8 0.7 copy-done.1
  1.4 1.1 shard_map.64
  2.5 10.5 %all-to-all-start = ((bf16[32,64,256]{2,1,0:T(8,128)(2,1)}), bf16[32,64,256]{2,1,0:T(8,128)(2,1)S(1)}, u32[]{:S(2)}, u32[]{:S(2)}) async-start(bf16[32,64,256]{2,1,0:T(8,128)(2,1)} %get-tuple-element.39), calls=%async_computation | async-start | bytes 2097152 | tf_op jit(solution)/shard_map/gather_plane/all_to_all | solution.py:187
  13.7 30.5 %all-gather = bf16[1024,256]{1,0:T(8,128)(2,1)S(1)} all-gather(bf16[64,256]{1,0:T(8,128)(2,1)S(1)} %get-tuple-element.40), channel_id=2, replica_groups=mesh['y'=4,'x'=4,'core'=2,'z'=16] {'z'}, dimensions={0}, use_global_device_ids=true | all-gather | bytes 557056 | tf_op jit(solution)/shard_map/gather_line/all_gather | solution.py:211
  44.1 0.7 copy-done.3
  44.8 0.7 copy-done.5
  45.5 3.0 %mirror.2 = (bf16[16,64,256]{2,1,0:T(8,128)(2,1)S(1)}, bf16[16,64,256]{2,1,0:T(8,128)(2,1)S(1)}) custom-call(s32[9]{0:T(128)S(1)} %copy-done.3, s32[9]{0:T(128)S(1)} %copy-done.5, s32[1]{0:T(128)S(6)} %copy.7.live, bf16[16,64,256]{2,1,0:T(8,128)(2,1)S(1)} %bitcast.4, bf16[9,512,512]{2,1,0:T(8,128)(2,1)} %blocks.7), custom_call_target="tpu_custom_call" | custom-call | flops 301989888 | bytes 4718592 | tf_op jit(solution)/shard_map/mirror/pallas_call | solution.py:214
  48.5 4.0 %direct.2 = bf16[16,64,256]{2,1,0:T(8,128)(2,1)} custom-call(s32[9]{0:T(128)S(1)} %copy-done.3, s32[9]{0:T(128)S(1)} %copy-done.5, s32[1]{0:T(128)S(6)} %copy.7.live, bf16[32,64,256]{2,1,0:T(8,128)(2,1)S(1)} %all-to-all-done.panel, bf16[9,512,512]{2,1,0:T(8,128)(2,1)} %blocks.7), custom_call_target="tpu_custom_call" | custom-call | flops 301989888 | bytes 4718592 | tf_op jit(solution)/shard_map/direct/pallas_call | solution.py:226
  52.5 6.6 %all-to-all-start.1 = ((bf16[16,64,256]{2,1,0:T(8,128)(2,1)}), bf16[16,64,256]{2,1,0:T(8,128)(2,1)S(1)}, u32[]{:S(2)}, u32[]{:S(2)}) async-start(bf16[16,64,256]{2,1,0:T(8,128)(2,1)} %direct.2), calls=%async_computation.1 | async-start | bytes 1048576 | tf_op jit(solution)/shard_map/reduce_line/all_to_all | solution.py:187
  59.1 8.0 %collective-permute-start = (bf16[16,64,256]{2,1,0:T(8,128)(2,1)S(1)}, bf16[16,64,256]{2,1,0:T(8,128)(2,1)S(1)}, u32[]{:S(2)}, u32[]{:S(2)}) collective-permute-start(bf16[16,64,256]{2,1,0:T(8,128)(2,1)S(1)} %get-tuple-element.43), channel_id=1, source_target_pairs={{0,16},{16,0},{1,17},{17,1},{2,18},{18,2},{3,19},{19,3},{4,20},{20... | collective-permute-start | bytes 1572872 | tf_op jit(solution)/shard_map/core_swap/ppermute | solution.py:183
  67.1 1.5 collective-permute-done.got
  68.6 0.1 reduce_x.2
  68.7 4.4 %collective-permute-start.1 = (bf16[4,64,256]{2,1,0:T(8,128)(2,1)S(1)}, bf16[4,64,256]{2,1,0:T(8,128)(2,1)S(1)}, u32[]{:S(2)}, u32[]{:S(2)}) collective-permute-start(bf16[4,64,256]{2,1,0:T(8,128)(2,1)S(1)} %get-tuple-element.47), channel_id=1, source_target_pairs={{0,32},{32,64},{64,96},{96,0},{1,33},{33,65},{65,97},{97,1},{2,34}... | collective-permute-start | bytes 393224 | tf_op jit(solution)/shard_map/reduce_x/ppermute | solution.py:183
  73.1 3.5 %collective-permute-start.2 = (bf16[4,64,256]{2,1,0:T(8,128)(2,1)S(1)}, bf16[4,64,256]{2,1,0:T(8,128)(2,1)S(1)}, u32[]{:S(2)}, u32[]{:S(2)}) collective-permute-start(bf16[4,64,256]{2,1,0:T(8,128)(2,1)S(1)} %get-tuple-element.48), channel_id=1, source_target_pairs={{0,64},{32,96},{64,0},{96,32},{1,65},{33,97},{65,1},{97,33},{2,66}... | collective-permute-start | bytes 393224 | tf_op jit(solution)/shard_map/reduce_x/ppermute | solution.py:183
  76.6 3.1 %collective-permute-start.3 = (bf16[4,64,256]{2,1,0:T(8,128)(2,1)S(1)}, bf16[4,64,256]{2,1,0:T(8,128)(2,1)S(1)}, u32[]{:S(2)}, u32[]{:S(2)}) collective-permute-start(bf16[4,64,256]{2,1,0:T(8,128)(2,1)S(1)} %get-tuple-element.49), channel_id=1, source_target_pairs={{0,96},{32,0},{64,32},{96,64},{1,97},{33,1},{65,33},{97,65},{2,98}... | collective-permute-start | bytes 393224 | tf_op jit(solution)/shard_map/reduce_x/ppermute | solution.py:183
  79.7 1.2 collective-permute-done.2.refs_1_
  80.9 1.7 collective-permute-done.3.refs_2_
  82.6 0.1 reduce_y.2
  82.7 3.1 %collective-permute-start.4 = (bf16[64,256]{1,0:T(8,128)(2,1)S(1)}, bf16[64,256]{1,0:T(8,128)(2,1)S(1)}, u32[]{:S(2)}, u32[]{:S(2)}) collective-permute-start(bf16[64,256]{1,0:T(8,128)(2,1)S(1)} %get-tuple-element.51), channel_id=1, source_target_pairs={{0,128},{128,256},{256,384},{384,0},{1,129},{129,257},{257,385},{3... | collective-permute-start | bytes 98312 | tf_op jit(solution)/shard_map/reduce_y/ppermute | solution.py:183
  85.8 4.4 %collective-permute-start.5 = (bf16[64,256]{1,0:T(8,128)(2,1)S(1)}, bf16[64,256]{1,0:T(8,128)(2,1)S(1)}, u32[]{:S(2)}, u32[]{:S(2)}) collective-permute-start(bf16[64,256]{1,0:T(8,128)(2,1)S(1)} %get-tuple-element.52), channel_id=1, source_target_pairs={{0,256},{128,384},{256,0},{384,128},{1,257},{129,385},{257,1},{385... | collective-permute-start | bytes 98312 | tf_op jit(solution)/shard_map/reduce_y/ppermute | solution.py:183
  90.2 2.9 %collective-permute-start.6 = (bf16[64,256]{1,0:T(8,128)(2,1)S(1)}, bf16[64,256]{1,0:T(8,128)(2,1)S(1)}, u32[]{:S(2)}, u32[]{:S(2)}) collective-permute-start(bf16[64,256]{1,0:T(8,128)(2,1)S(1)} %get-tuple-element.53), channel_id=1, source_target_pairs={{0,384},{128,0},{256,128},{384,256},{1,385},{129,1},{257,129},{385... | collective-permute-start | bytes 98312 | tf_op jit(solution)/shard_map/reduce_y/ppermute | solution.py:183
  93.1 1.8 collective-permute-done.6.s3
  94.8 1.2 between.1
  96.0 9.6 %all-to-all-start.2 = ((bf16[32,64,256]{2,1,0:T(8,128)(2,1)}), bf16[32,64,256]{2,1,0:T(8,128)(2,1)S(1)}, u32[]{:S(2)}, u32[]{:S(2)}) async-start(bf16[32,64,256]{2,1,0:T(8,128)(2,1)} %get-tuple-element.54), calls=%async_computation.2 | async-start | bytes 2097152 | tf_op jit(solution)/shard_map/gather_plane/all_to_all | solution.py:187
  105.7 27.2 %all-gather.1 = bf16[1024,256]{1,0:T(8,128)(2,1)S(1)} all-gather(bf16[64,256]{1,0:T(8,128)(2,1)S(1)} %get-tuple-element.55), channel_id=3, replica_groups=mesh['y'=4,'x'=4,'core'=2,'z'=16] {'z'}, dimensions={0}, use_global_device_ids=true | all-gather | bytes 557056 | tf_op jit(solution)/shard_map/gather_line/all_gather | solution.py:211
  132.8 3.0 %mirror.3 = (bf16[16,64,256]{2,1,0:T(8,128)(2,1)S(1)}, bf16[16,64,256]{2,1,0:T(8,128)(2,1)S(1)}) custom-call(s32[9]{0:T(128)S(1)} %copy-done.4, s32[9]{0:T(128)S(1)} %copy-done.6, s32[1]{0:T(128)S(6)} %copy.7.live, bf16[16,64,256]{2,1,0:T(8,128)(2,1)S(1)} %bitcast.5, bf16[9,512,512]{2,1,0:T(8,128)(2,1)} %blocks.7), custom_call_target="tpu_custom_call" | custom-call | flops 301989888 | bytes 4718592 | tf_op jit(solution)/shard_map/mirror/pallas_call | solution.py:214
  135.9 4.0 %direct.3 = bf16[16,64,256]{2,1,0:T(8,128)(2,1)} custom-call(s32[9]{0:T(128)S(1)} %copy-done.4, s32[9]{0:T(128)S(1)} %copy-done.6, s32[1]{0:T(128)S(6)} %copy.7.live, bf16[32,64,256]{2,1,0:T(8,128)(2,1)S(1)} %all-to-all-done.2.panel, bf16[9,512,512]{2,1,0:T(8,128)(2,1)} %blocks.7), custom_call_target="tpu_custom_call" | custom-call | flops 301989888 | bytes 4718592 | tf_op jit(solution)/shard_map/direct/pallas_call | solution.py:226
  139.8 8.4 %all-to-all-start.3 = ((bf16[16,64,256]{2,1,0:T(8,128)(2,1)}), bf16[16,64,256]{2,1,0:T(8,128)(2,1)S(1)}, u32[]{:S(2)}, u32[]{:S(2)}) async-start(bf16[16,64,256]{2,1,0:T(8,128)(2,1)} %direct.3), calls=%async_computation.3 | async-start | bytes 1048576 | tf_op jit(solution)/shard_map/reduce_line/all_to_all | solution.py:187
  148.3 8.2 %collective-permute-start.7 = (bf16[16,64,256]{2,1,0:T(8,128)(2,1)S(1)}, bf16[16,64,256]{2,1,0:T(8,128)(2,1)S(1)}, u32[]{:S(2)}, u32[]{:S(2)}) collective-permute-start(bf16[16,64,256]{2,1,0:T(8,128)(2,1)S(1)} %get-tuple-element.58), channel_id=1, source_target_pairs={{0,16},{16,0},{1,17},{17,1},{2,18},{18,2},{3,19},{19,3},{4,20},{20... | collective-permute-start | bytes 1572872 | tf_op jit(solution)/shard_map/core_swap/ppermute | solution.py:183
  156.5 1.5 collective-permute-done.7.got
  158.0 0.1 reduce_x.3
  158.1 4.6 %collective-permute-start.8 = (bf16[4,64,256]{2,1,0:T(8,128)(2,1)S(1)}, bf16[4,64,256]{2,1,0:T(8,128)(2,1)S(1)}, u32[]{:S(2)}, u32[]{:S(2)}) collective-permute-start(bf16[4,64,256]{2,1,0:T(8,128)(2,1)S(1)} %get-tuple-element.62), channel_id=1, source_target_pairs={{0,32},{32,64},{64,96},{96,0},{1,33},{33,65},{65,97},{97,1},{2,34}... | collective-permute-start | bytes 393224 | tf_op jit(solution)/shard_map/reduce_x/ppermute | solution.py:183
  162.7 3.3 %collective-permute-start.9 = (bf16[4,64,256]{2,1,0:T(8,128)(2,1)S(1)}, bf16[4,64,256]{2,1,0:T(8,128)(2,1)S(1)}, u32[]{:S(2)}, u32[]{:S(2)}) collective-permute-start(bf16[4,64,256]{2,1,0:T(8,128)(2,1)S(1)} %get-tuple-element.63), channel_id=1, source_target_pairs={{0,64},{32,96},{64,0},{96,32},{1,65},{33,97},{65,1},{97,33},{2,66}... | collective-permute-start | bytes 393224 | tf_op jit(solution)/shard_map/reduce_x/ppermute | solution.py:183
  166.1 2.9 %collective-permute-start.10 = (bf16[4,64,256]{2,1,0:T(8,128)(2,1)S(1)}, bf16[4,64,256]{2,1,0:T(8,128)(2,1)S(1)}, u32[]{:S(2)}, u32[]{:S(2)}) collective-permute-start(bf16[4,64,256]{2,1,0:T(8,128)(2,1)S(1)} %get-tuple-element.64), channel_id=1, source_target_pairs={{0,96},{32,0},{64,32},{96,64},{1,97},{33,1},{65,33},{97,65},{2,98}... | collective-permute-start | bytes 393224 | tf_op jit(solution)/shard_map/reduce_x/ppermute | solution.py:183
  169.0 1.5 collective-permute-done.9.refs_1_
  170.5 1.6 collective-permute-done.10.refs_2_
  172.1 2.7 %collective-permute-start.11 = (bf16[64,256]{1,0:T(8,128)(2,1)S(1)}, bf16[64,256]{1,0:T(8,128)(2,1)S(1)}, u32[]{:S(2)}, u32[]{:S(2)}) collective-permute-start(bf16[64,256]{1,0:T(8,128)(2,1)S(1)} %get-tuple-element.66), channel_id=1, source_target_pairs={{0,128},{128,256},{256,384},{384,0},{1,129},{129,257},{257,385},{3... | collective-permute-start | bytes 98312 | tf_op jit(solution)/shard_map/reduce_y/ppermute | solution.py:183
  174.8 4.4 %collective-permute-start.12 = (bf16[64,256]{1,0:T(8,128)(2,1)S(1)}, bf16[64,256]{1,0:T(8,128)(2,1)S(1)}, u32[]{:S(2)}, u32[]{:S(2)}) collective-permute-start(bf16[64,256]{1,0:T(8,128)(2,1)S(1)} %get-tuple-element.67), channel_id=1, source_target_pairs={{0,256},{128,384},{256,0},{384,128},{1,257},{129,385},{257,1},{385... | collective-permute-start | bytes 98312 | tf_op jit(solution)/shard_map/reduce_y/ppermute | solution.py:183
  179.2 2.9 %collective-permute-start.13 = (bf16[64,256]{1,0:T(8,128)(2,1)S(1)}, bf16[64,256]{1,0:T(8,128)(2,1)S(1)}, u32[]{:S(2)}, u32[]{:S(2)}) collective-permute-start(bf16[64,256]{1,0:T(8,128)(2,1)S(1)} %get-tuple-element.68), channel_id=1, source_target_pairs={{0,384},{128,0},{256,128},{384,256},{1,385},{129,1},{257,129},{385... | collective-permute-start | bytes 98312 | tf_op jit(solution)/shard_map/reduce_y/ppermute | solution.py:183
  182.1 1.7 collective-permute-done.13.s3
  183.9 0.3 last.1
  184.2 5.4 %collective-permute-start.14 = (f32[16,128]{1,0:T(8,128)S(1)}, f32[16,128]{1,0:T(8,128)S(1)}, u32[]{:S(2)}, u32[]{:S(2)}) collective-permute-start(f32[16,128]{1,0:T(8,128)S(1)} %get-tuple-element.71), channel_id=1, source_target_pairs={{0,16},{16,0},{1,17},{17,1},{2,18},{18,2},{3,19},{19,3},{4,20},{20... | collective-permute-start | bytes 24584 | tf_op jit(solution)/shard_map/gram_core/ppermute | solution.py:183
  189.6 0.8 collective-permute-done.14
  190.4 12.4 %all_to_all.30 = f32[16,16,128]{2,1,0:T(8,128)S(1)} all-to-all(f32[16,16,128]{2,1,0:T(8,128)S(1)} %broadcast_in_dim.4), channel_id=1, replica_groups=mesh['y'=4,'x'=4,'core'=2,'z'=16] {'y','x'}, dimensions={0} | all-to-all | bytes 262144 | tf_op jit(solution)/shard_map/gram_plane/all_to_all | solution.py:187
  202.8 23.5 %all_to_all.31 = f32[16,16,128]{2,1,0:T(8,128)S(1)} all-to-all(f32[16,16,128]{2,1,0:T(8,128)S(1)} %broadcast_in_dim.5), channel_id=1, replica_groups=mesh['y'=4,'x'=4,'core'=2,'z'=16] {'z'}, dimensions={0} | all-to-all | bytes 262144 | tf_op jit(solution)/shard_map/gram_line/all_to_all | solution.py:187
  226.3 5.5 %all-gather.2 = f32[32,128]{1,0:T(8,128)S(1)} all-gather(f32[16,128]{1,0:T(8,128)S(1)} %reduce_sum.19), channel_id=4, replica_groups=mesh['y'=4,'x'=4,'core'=2,'z'=16] {'core'}, dimensions={0}, use_global_device_ids=true | all-gather | bytes 24576 | tf_op jit(solution)/shard_map/gram_pair/all_gather | solution.py:265
  231.8 6.2 %whiten.1 = bf16[64,256]{1,0:T(8,128)(2,1)} custom-call(f32[2,16,128]{2,1,0:T(8,128)S(1)} %bitcast.6, bf16[64,256]{1,0:T(8,128)(2,1)S(1)} %get-tuple-element.72.fresh), custom_call_target="tpu_custom_call" | custom-call | tf_op jit(solution)/shard_map/whiten/pallas_call | solution.py:267
  (26 shorter events, 0.2 us)
Async XLA Ops:
  0.0 0.8 copy-start
  0.8 0.7 copy-start.1
  2.5 41.6 %all-to-all-start = ((bf16[32,64,256]{2,1,0:T(8,128)(2,1)}), bf16[32,64,256]{2,1,0:T(8,128)(2,1)S(1)}, u32[]{:S(2)}, u32[]{:S(2)}) async-start(bf16[32,64,256]{2,1,0:T(8,128)(2,1)} %get-tuple-element.39), calls=%async_computation | async-start | bytes 2097152 | tf_op jit(solution)/shard_map/gather_plane/all_to_all | solution.py:187
  44.1 0.7 copy-start.3
  44.8 0.7 copy-start.5
  48.5 46.3 %copy-start.2 = (f32[256]{0:T(256)S(1)}, f32[256]{0:T(256)}, u32[]{:S(2)}) copy-start(f32[256]{0:T(256)} %param.7) | copy-start | bytes 3076
  48.5 84.3 %copy-start.4 = (s32[9]{0:T(128)S(1)}, s32[9]{0:T(128)}, u32[]{:S(2)}) copy-start(s32[9]{0:T(128)} %rows.7) | copy-start | bytes 112
  48.5 84.3 %copy-start.6 = (s32[9]{0:T(128)S(1)}, s32[9]{0:T(128)}, u32[]{:S(2)}) copy-start(s32[9]{0:T(128)} %cols.7) | copy-start | bytes 112
  52.5 42.3 %all-to-all-start.1 = ((bf16[16,64,256]{2,1,0:T(8,128)(2,1)}), bf16[16,64,256]{2,1,0:T(8,128)(2,1)S(1)}, u32[]{:S(2)}, u32[]{:S(2)}) async-start(bf16[16,64,256]{2,1,0:T(8,128)(2,1)} %direct.2), calls=%async_computation.1 | async-start | bytes 1048576 | tf_op jit(solution)/shard_map/reduce_line/all_to_all | solution.py:187
  59.1 9.5 %collective-permute-start = (bf16[16,64,256]{2,1,0:T(8,128)(2,1)S(1)}, bf16[16,64,256]{2,1,0:T(8,128)(2,1)S(1)}, u32[]{:S(2)}, u32[]{:S(2)}) collective-permute-start(bf16[16,64,256]{2,1,0:T(8,128)(2,1)S(1)} %get-tuple-element.43), channel_id=1, source_target_pairs={{0,16},{16,0},{1,17},{17,1},{2,18},{18,2},{3,19},{19,3},{4,20},{20... | collective-permute-start | bytes 1572872 | tf_op jit(solution)/shard_map/core_swap/ppermute | solution.py:183
  68.7 11.0 %collective-permute-start.1 = (bf16[4,64,256]{2,1,0:T(8,128)(2,1)S(1)}, bf16[4,64,256]{2,1,0:T(8,128)(2,1)S(1)}, u32[]{:S(2)}, u32[]{:S(2)}) collective-permute-start(bf16[4,64,256]{2,1,0:T(8,128)(2,1)S(1)} %get-tuple-element.47), channel_id=1, source_target_pairs={{0,32},{32,64},{64,96},{96,0},{1,33},{33,65},{65,97},{97,1},{2,34}... | collective-permute-start | bytes 393224 | tf_op jit(solution)/shard_map/reduce_x/ppermute | solution.py:183
  73.1 7.8 %collective-permute-start.2 = (bf16[4,64,256]{2,1,0:T(8,128)(2,1)S(1)}, bf16[4,64,256]{2,1,0:T(8,128)(2,1)S(1)}, u32[]{:S(2)}, u32[]{:S(2)}) collective-permute-start(bf16[4,64,256]{2,1,0:T(8,128)(2,1)S(1)} %get-tuple-element.48), channel_id=1, source_target_pairs={{0,64},{32,96},{64,0},{96,32},{1,65},{33,97},{65,1},{97,33},{2,66}... | collective-permute-start | bytes 393224 | tf_op jit(solution)/shard_map/reduce_x/ppermute | solution.py:183
  76.6 6.0 %collective-permute-start.3 = (bf16[4,64,256]{2,1,0:T(8,128)(2,1)S(1)}, bf16[4,64,256]{2,1,0:T(8,128)(2,1)S(1)}, u32[]{:S(2)}, u32[]{:S(2)}) collective-permute-start(bf16[4,64,256]{2,1,0:T(8,128)(2,1)S(1)} %get-tuple-element.49), channel_id=1, source_target_pairs={{0,96},{32,0},{64,32},{96,64},{1,97},{33,1},{65,33},{97,65},{2,98}... | collective-permute-start | bytes 393224 | tf_op jit(solution)/shard_map/reduce_x/ppermute | solution.py:183
  82.7 10.4 %collective-permute-start.4 = (bf16[64,256]{1,0:T(8,128)(2,1)S(1)}, bf16[64,256]{1,0:T(8,128)(2,1)S(1)}, u32[]{:S(2)}, u32[]{:S(2)}) collective-permute-start(bf16[64,256]{1,0:T(8,128)(2,1)S(1)} %get-tuple-element.51), channel_id=1, source_target_pairs={{0,128},{128,256},{256,384},{384,0},{1,129},{129,257},{257,385},{3... | collective-permute-start | bytes 98312 | tf_op jit(solution)/shard_map/reduce_y/ppermute | solution.py:183
  85.8 7.3 %collective-permute-start.5 = (bf16[64,256]{1,0:T(8,128)(2,1)S(1)}, bf16[64,256]{1,0:T(8,128)(2,1)S(1)}, u32[]{:S(2)}, u32[]{:S(2)}) collective-permute-start(bf16[64,256]{1,0:T(8,128)(2,1)S(1)} %get-tuple-element.52), channel_id=1, source_target_pairs={{0,256},{128,384},{256,0},{384,128},{1,257},{129,385},{257,1},{385... | collective-permute-start | bytes 98312 | tf_op jit(solution)/shard_map/reduce_y/ppermute | solution.py:183
  90.2 4.7 %collective-permute-start.6 = (bf16[64,256]{1,0:T(8,128)(2,1)S(1)}, bf16[64,256]{1,0:T(8,128)(2,1)S(1)}, u32[]{:S(2)}, u32[]{:S(2)}) collective-permute-start(bf16[64,256]{1,0:T(8,128)(2,1)S(1)} %get-tuple-element.53), channel_id=1, source_target_pairs={{0,384},{128,0},{256,128},{384,256},{1,385},{129,1},{257,129},{385... | collective-permute-start | bytes 98312 | tf_op jit(solution)/shard_map/reduce_y/ppermute | solution.py:183
  96.0 36.8 %all-to-all-start.2 = ((bf16[32,64,256]{2,1,0:T(8,128)(2,1)}), bf16[32,64,256]{2,1,0:T(8,128)(2,1)S(1)}, u32[]{:S(2)}, u32[]{:S(2)}) async-start(bf16[32,64,256]{2,1,0:T(8,128)(2,1)} %get-tuple-element.54), calls=%async_computation.2 | async-start | bytes 2097152 | tf_op jit(solution)/shard_map/gather_plane/all_to_all | solution.py:187
  139.8 44.0 %all-to-all-start.3 = ((bf16[16,64,256]{2,1,0:T(8,128)(2,1)}), bf16[16,64,256]{2,1,0:T(8,128)(2,1)S(1)}, u32[]{:S(2)}, u32[]{:S(2)}) async-start(bf16[16,64,256]{2,1,0:T(8,128)(2,1)} %direct.3), calls=%async_computation.3 | async-start | bytes 1048576 | tf_op jit(solution)/shard_map/reduce_line/all_to_all | solution.py:187
  148.3 9.8 %collective-permute-start.7 = (bf16[16,64,256]{2,1,0:T(8,128)(2,1)S(1)}, bf16[16,64,256]{2,1,0:T(8,128)(2,1)S(1)}, u32[]{:S(2)}, u32[]{:S(2)}) collective-permute-start(bf16[16,64,256]{2,1,0:T(8,128)(2,1)S(1)} %get-tuple-element.58), channel_id=1, source_target_pairs={{0,16},{16,0},{1,17},{17,1},{2,18},{18,2},{3,19},{19,3},{4,20},{20... | collective-permute-start | bytes 1572872 | tf_op jit(solution)/shard_map/core_swap/ppermute | solution.py:183
  158.1 10.8 %collective-permute-start.8 = (bf16[4,64,256]{2,1,0:T(8,128)(2,1)S(1)}, bf16[4,64,256]{2,1,0:T(8,128)(2,1)S(1)}, u32[]{:S(2)}, u32[]{:S(2)}) collective-permute-start(bf16[4,64,256]{2,1,0:T(8,128)(2,1)S(1)} %get-tuple-element.62), channel_id=1, source_target_pairs={{0,32},{32,64},{64,96},{96,0},{1,33},{33,65},{65,97},{97,1},{2,34}... | collective-permute-start | bytes 393224 | tf_op jit(solution)/shard_map/reduce_x/ppermute | solution.py:183
  162.7 7.8 %collective-permute-start.9 = (bf16[4,64,256]{2,1,0:T(8,128)(2,1)S(1)}, bf16[4,64,256]{2,1,0:T(8,128)(2,1)S(1)}, u32[]{:S(2)}, u32[]{:S(2)}) collective-permute-start(bf16[4,64,256]{2,1,0:T(8,128)(2,1)S(1)} %get-tuple-element.63), channel_id=1, source_target_pairs={{0,64},{32,96},{64,0},{96,32},{1,65},{33,97},{65,1},{97,33},{2,66}... | collective-permute-start | bytes 393224 | tf_op jit(solution)/shard_map/reduce_x/ppermute | solution.py:183
  166.1 6.0 %collective-permute-start.10 = (bf16[4,64,256]{2,1,0:T(8,128)(2,1)S(1)}, bf16[4,64,256]{2,1,0:T(8,128)(2,1)S(1)}, u32[]{:S(2)}, u32[]{:S(2)}) collective-permute-start(bf16[4,64,256]{2,1,0:T(8,128)(2,1)S(1)} %get-tuple-element.64), channel_id=1, source_target_pairs={{0,96},{32,0},{64,32},{96,64},{1,97},{33,1},{65,33},{97,65},{2,98}... | collective-permute-start | bytes 393224 | tf_op jit(solution)/shard_map/reduce_x/ppermute | solution.py:183
  172.1 10.0 %collective-permute-start.11 = (bf16[64,256]{1,0:T(8,128)(2,1)S(1)}, bf16[64,256]{1,0:T(8,128)(2,1)S(1)}, u32[]{:S(2)}, u32[]{:S(2)}) collective-permute-start(bf16[64,256]{1,0:T(8,128)(2,1)S(1)} %get-tuple-element.66), channel_id=1, source_target_pairs={{0,128},{128,256},{256,384},{384,0},{1,129},{129,257},{257,385},{3... | collective-permute-start | bytes 98312 | tf_op jit(solution)/shard_map/reduce_y/ppermute | solution.py:183
  174.8 7.3 %collective-permute-start.12 = (bf16[64,256]{1,0:T(8,128)(2,1)S(1)}, bf16[64,256]{1,0:T(8,128)(2,1)S(1)}, u32[]{:S(2)}, u32[]{:S(2)}) collective-permute-start(bf16[64,256]{1,0:T(8,128)(2,1)S(1)} %get-tuple-element.67), channel_id=1, source_target_pairs={{0,256},{128,384},{256,0},{384,128},{1,257},{129,385},{257,1},{385... | collective-permute-start | bytes 98312 | tf_op jit(solution)/shard_map/reduce_y/ppermute | solution.py:183
  179.2 4.7 %collective-permute-start.13 = (bf16[64,256]{1,0:T(8,128)(2,1)S(1)}, bf16[64,256]{1,0:T(8,128)(2,1)S(1)}, u32[]{:S(2)}, u32[]{:S(2)}) collective-permute-start(bf16[64,256]{1,0:T(8,128)(2,1)S(1)} %get-tuple-element.68), channel_id=1, source_target_pairs={{0,384},{128,0},{256,128},{384,256},{1,385},{129,1},{257,129},{385... | collective-permute-start | bytes 98312 | tf_op jit(solution)/shard_map/reduce_y/ppermute | solution.py:183
  184.2 6.2 %collective-permute-start.14 = (f32[16,128]{1,0:T(8,128)S(1)}, f32[16,128]{1,0:T(8,128)S(1)}, u32[]{:S(2)}, u32[]{:S(2)}) collective-permute-start(f32[16,128]{1,0:T(8,128)S(1)} %get-tuple-element.71), channel_id=1, source_target_pairs={{0,16},{16,0},{1,17},{17,1},{2,18},{18,2},{3,19},{19,3},{4,20},{20... | collective-permute-start | bytes 24584 | tf_op jit(solution)/shard_map/gram_core/ppermute | solution.py:183

commit v2 on v1

v2 whole, which is shorter than its diff:
```python
import functools

import jax
import jax.numpy as jnp
from jax import lax
from jax.experimental import pallas as pl
from jax.experimental.pallas import tpu as pltpu
from jax.sharding import Mesh, PartitionSpec as P

F32 = jnp.float32
BF16 = jnp.bfloat16
ROW = ("y", "x", "core")
LINE = ("far", "near")
RIDGE = 1e-06
STEP = 8
VMEM = pl.BlockSpec(memory_space=pltpu.VMEM)
SMEM = pl.BlockSpec(memory_space=pltpu.SMEM)
PARAMS = pltpu.CompilerParams(vmem_limit_bytes=48 * 1024 * 1024)
NT = (((1,), (1,)), ((), ()))
NN = (((1,), (0,)), ((), ()))


def call(kernel, outs, ins, scratch=(), flops=0, moved=0):
    return pl.pallas_call(
        kernel,
        out_shape=[jax.ShapeDtypeStruct(s, d) for s, d in outs],
        in_specs=ins,
        out_specs=[VMEM] * len(outs),
        scratch_shapes=list(scratch),
        compiler_params=PARAMS,
        cost_estimate=pl.CostEstimate(flops=flops, bytes_accessed=moved, transcendentals=0),
    )


def products_kernel(
    places, row_panel, col_panel, tiles, direct, keep, send, blocks, row_sum, col_sum, tile_sems
):
    slots = tiles.shape[0]
    copies = [pltpu.make_async_copy(tiles.at[s], blocks.at[s], tile_sems.at[s]) for s in range(slots)]
    for copy in copies:
        copy.start()
    row_sum[...] = jnp.zeros_like(row_sum)
    col_sum[...] = jnp.zeros_like(col_sum)
    half = row_panel.shape[2]
    for s, copy in enumerate(copies):
        copy.wait()

        @pl.when(s < places[2 * slots])
        def _():
            r, c = places[s], places[slots + s]
            low, high = 2 * r, 2 * r + 1
            left, right = 2 * c, 2 * c + 1
            part = lax.dot_general(
                row_panel[low], blocks[s, :half, :], NN, preferred_element_type=F32
            ) + lax.dot_general(row_panel[high], blocks[s, half:, :], NN, preferred_element_type=F32)
            col_sum[left] += part[:, :half]
            col_sum[right] += part[:, half:]
            part = lax.dot_general(
                col_panel[left], blocks[s, :, :half], NT, preferred_element_type=F32
            ) + lax.dot_general(col_panel[right], blocks[s, :, half:], NT, preferred_element_type=F32)
            row_sum[low] += part[:, :half]
            row_sum[high] += part[:, half:]

    direct[...] = row_sum[...].astype(BF16)
    me = lax.axis_index("core")
    for chip in range(keep.shape[0]):
        keep[chip] = col_sum[2 * chip + me].astype(BF16)
        send[chip] = col_sum[2 * chip + 1 - me].astype(BF16)


def merge_x_kernel(keep, got, *pieces):
    me = lax.axis_index("x")
    n = len(pieces)
    for k, piece in enumerate(pieces):
        to = lax.rem(me + k, n)
        for y in range(piece.shape[0]):
            piece[y] = (keep[y * n + to].astype(F32) + got[y * n + to].astype(F32)).astype(BF16)


def merge_y_kernel(own, *refs):
    n = own.shape[0]
    got, pieces = refs[: n - 1], refs[n - 1 :]
    me = lax.axis_index("y")
    for k, piece in enumerate(pieces):
        to = lax.rem(me + k, n)
        sums = own[to].astype(F32)
        for g in got:
            sums += g[to].astype(F32)
        piece[...] = sums.astype(BF16)


def spread(value, scaled, copies):
    scaled[...] = value
    for k in range(copies.shape[0]):
        copies[k] = value


def add_up(arrived, own, others, weights):
    sums = own[...].astype(F32)
    for other in others:
        sums += other[...].astype(F32)
    for k in range(arrived.shape[0]):
        sums += arrived[k].astype(F32)
    return sums * weights[...]


def between_kernel(arrived, own, s1, s2, s3, weights, scaled, copies, gram):
    fresh = add_up(arrived, own, (s1, s2, s3), weights)
    spread((fresh * weights[...]).astype(BF16), scaled, copies)
    rounded = fresh.astype(BF16)
    gram[...] = lax.dot_general(rounded, rounded, NT, preferred_element_type=F32)


def masks(h):
    i = lax.broadcasted_iota(jnp.int32, (h, h), 0)
    j = lax.broadcasted_iota(jnp.int32, (h, h), 1)
    return (i >= j).astype(F32), (i == j).astype(F32)


def pack(gram):
    h = gram.shape[0] // 2
    lower, eye = masks(h)
    mixed = gram[:h, :h] * lower + gram[h:, h:] * (1.0 - lower)
    diagonal = jnp.sum(gram[h:, h:] * eye, axis=0, keepdims=True)
    lines = []
    for block in (mixed, gram[h:, :h]):
        wide = jnp.concatenate([block[8 * i : 8 * i + 8] for i in range(h // 8)], axis=1)
        lines += [wide[i : i + 1] for i in range(8)]
    lines.append(jnp.concatenate([diagonal] * (128 // h), axis=1))
    lines.append(jnp.zeros_like(lines[-1]))
    return jnp.concatenate(lines, axis=1)


def unpack(row, n):
    h = n // 2
    lower, eye = masks(h)
    blocks = []
    for b in range(2):
        at = [row[:, 128 * (8 * b + i) : 128 * (8 * b + i + 1)] for i in range(8)]
        wide = jnp.concatenate(at, axis=0)
        blocks.append(jnp.concatenate([wide[:, h * i : h * i + h] for i in range(h // 8)], axis=0))
    mixed, corner = blocks
    diagonal = row[:, 2048 : 2048 + h] * eye
    upper = mixed * (1.0 - lower)
    strict = mixed * (lower - eye)
    first = strict + strict.T + mixed * eye
    second = upper + upper.T + diagonal
    return jnp.concatenate(
        [jnp.concatenate([first, corner.T], axis=1), jnp.concatenate([corner, second], axis=1)],
        axis=0,
    )


def last_kernel(scale, arrived, own, s1, s2, s3, weights, first, fresh, keep, send):
    rounded = add_up(arrived, own, (s1, s2, s3), weights).astype(BF16)
    fresh[...] = rounded
    gram = lax.dot_general(rounded, rounded, NT, preferred_element_type=F32)
    packed = pack((gram + RIDGE * first[...]) * scale)
    h = packed.shape[1] // 2
    second = lax.axis_index("core") == 1
    keep[...] = jnp.where(second, packed[:, h:], packed[:, :h])
    send[...] = jnp.where(second, packed[:, :h], packed[:, h:])


def whiten_kernel(parts, fresh, out, factor):
    packed = jnp.concatenate([parts[0], parts[1]], axis=1)
    n = fresh.shape[0]
    matrix = unpack(packed, n)
    eye = masks(n)[1]
    left = jnp.concatenate([matrix + RIDGE * RIDGE * eye, eye], axis=1)
    base = 0
    for j in range(0, n, STEP):
        if j - base == 8:
            left = left[8:]
            base = j
        i = j - base
        wide = (left.shape[0], 2 * n)
        cols = [jnp.broadcast_to(left[:, j + a : j + a + 1], wide) for a in range(STEP)]
        rows = [left[i + a : i + a + 1] for a in range(STEP)]
        block = [[cols[b][i + a : i + a + 1] for b in range(STEP)] for a in range(STEP)]
        for a in range(STEP):
            pivot = block[a][a]
            inverse = 1.0 / pivot
            for b in range(a + 1, STEP):
                ratio = block[a][b] * inverse
                for c in range(b, STEP):
                    block[b][c] = block[b][c] - ratio * block[a][c]
                rows[b] = rows[b] - ratio * rows[a]
                cols[b] = cols[b] - ratio * cols[a]
            factor[j + a : j + a + 1] = rows[a] * (1.0 / jnp.sqrt(pivot))
            rows[a] = rows[a] * inverse
        for a in range(STEP):
            left = left - cols[a] * rows[a]
    inverse = factor[:, n:]
    out[...] = lax.dot_general(
        inverse,
        fresh[...].astype(F32),
        NN,
        precision=lax.Precision.HIGHEST,
        preferred_element_type=F32,
    ).astype(BF16)


def shift(value, axis, step, size):
    return lax.ppermute(value, axis, [(i, (i + step) % size) for i in range(size)])


def exchange(value, axes):
    return lax.all_to_all(value, axes, split_axis=0, concat_axis=0, tiled=True)


def body(x_start, weights, blocks, block_rows, block_cols, live_blocks):
    k, own = x_start.shape
    slots, tile, _ = blocks.shape
    ny, nx, nz = lax.axis_size("y"), lax.axis_size("x"), lax.axis_size("far") * lax.axis_size("near")
    rows = 2 * ny * nx
    vertices = float(own * rows * nz)
    gains = weights.reshape(1, own)
    any_spec = pl.BlockSpec(memory_space=pl.ANY)
    any_in = pl.BlockSpec(memory_space=pltpu.HBM)
    places = jnp.concatenate([block_rows, block_cols, live_blocks])
    scaled = (x_start.astype(F32) * gains).astype(BF16)
    copies = jnp.broadcast_to(scaled[None], (rows, k, own))
    gram = None
    for sweep in range(2):
        with jax.named_scope("gather_plane"):
            col_panel = exchange(copies, ROW)
        with jax.named_scope("gather_line"):
            row_panel = lax.all_gather(scaled, LINE, axis=0)
        col_panel, row_panel = lax.optimization_barrier((col_panel, row_panel))
        with jax.named_scope("products"):
            direct, keep, send = call(
                products_kernel,
                [((nz, k, own), BF16)] + [((ny * nx, k, own), BF16)] * 2,
                [SMEM] + [VMEM] * 2 + [any_in],
                [pltpu.VMEM((slots, tile, tile), BF16)]
                + [pltpu.VMEM((nz, k, own), F32), pltpu.VMEM((rows, k, own), F32)]
                + [pltpu.SemaphoreType.DMA((slots,))],
                4 * slots * k * tile * tile,
                blocks.size * 2,
            )(places, row_panel, col_panel, blocks)
        with jax.named_scope("reduce_core"):
            got = shift(send, "core", 1, 2)
        direct, got = lax.optimization_barrier((direct, got))
        with jax.named_scope("reduce_line"):
            arrived = exchange(direct, LINE)
        with jax.named_scope("reduce_x"):
            pieces = call(merge_x_kernel, [((ny, k, own), BF16)] * nx, [VMEM] * 2)(keep, got)
            moved = [pieces[0]] + [shift(pieces[s], "x", s, nx) for s in range(1, nx)]
        with jax.named_scope("reduce_y"):
            pieces = call(merge_y_kernel, [((k, own), BF16)] * ny, [VMEM] * nx)(*moved)
            moved = [pieces[0]] + [shift(pieces[s], "y", s, ny) for s in range(1, ny)]
        if sweep == 0:
            with jax.named_scope("between"):
                scaled, copies, gram = call(
                    between_kernel,
                    [((k, own), BF16), ((rows, k, own), BF16), ((k, k), F32)],
                    [VMEM] * 6,
                )(arrived, *moved, gains)
        else:
            with jax.named_scope("last"):
                fresh, keep, send = call(
                    functools.partial(last_kernel, 1.0 / vertices),
                    [((k, own), BF16)] + [((1, 9 * 128), F32)] * 2,
                    [VMEM] * 7,
                )(arrived, *moved, gains, gram)
    with jax.named_scope("gram_core"):
        part = keep + shift(send, "core", 1, 2)
    with jax.named_scope("gram_plane"):
        copies = jnp.broadcast_to(part[None], (ny * nx,) + part.shape)
        part = jnp.sum(exchange(copies, ("y", "x")), axis=0)
    with jax.named_scope("gram_line"):
        copies = jnp.broadcast_to(part[None], (nz,) + part.shape)
        part = jnp.sum(exchange(copies, LINE), axis=0)
    with jax.named_scope("gram_pair"):
        parts = lax.all_gather(part, "core", axis=0)
    with jax.named_scope("whiten"):
        (out,) = call(
            whiten_kernel,
            [((k, own), BF16)],
            [VMEM] * 2,
            [pltpu.VMEM((k, 2 * k), F32)],
        )(parts, fresh)
    return out


def solution(mesh):
    cells = ROW + LINE
    fine = Mesh(mesh.devices.reshape(4, 4, 2, 8, 2), cells)
    return jax.shard_map(
        body,
        mesh=fine,
        in_specs=(P(None, cells), P(cells), P(cells, None, None), P(cells), P(cells), P(cells)),
        out_specs=P(None, cells),
        check_vma=False,
    )
```

time: 239 us -> 229 us (0.958)
  Pallas kernels: 23.1 us -> 12.9 us
  waiting for transfers between devices: 13.3 us -> 17 us
    pallas_call x5 -> x2, Pallas kernels: 15.1 us -> 8.27 us  [body(): call(products_kernel, [((nz, k, own), BF16)] + [((ny * nx, k, own), BF16)...]
    ppermute x15, starting transfers between devices: 63.6 us -> 59.5 us  [shift(): lax.ppermute(value, axis, [(i, (i + step) % size) for i in range(size)])]
    ppermute x15, waiting for transfers between devices: 13.3 us -> 16.9 us  [shift(): lax.ppermute(value, axis, [(i, (i + step) % size) for i in range(size)])]
    pallas_call x1, Pallas kernels: 6.22 us -> 2.67 us  [body(): call(whiten_kernel, [((k, own), BF16)], [VMEM] * 2, [pltpu.VMEM((k, 2 * k...]
    unnamed x14 -> x3, local copies, waits for them, and re-layouts: 2.77 us -> 0.01 us
    all_to_all x4, starting transfers between devices: 35.1 us -> 37.5 us  [exchange(): return lax.all_to_all(value, axes, split_axis=0, concat_axis=0, tiled=True)]
where the time goes in v2:
time: 229 us; the launch traced here: 227 us
  starting transfers between devices  97.1 us (42%)
  blocking collectives  96.7 us (42%)
  waiting for transfers between devices  17 us (7%)
  Pallas kernels  12.9 us (6%)
    ppermute x15, starting transfers between devices, shift(): lax.ppermute(value, axis, [(i, (i + step) % size) for i in range(size)])  59.5 us
    all_gather x2, blocking collectives, body(): row_panel = lax.all_gather(scaled, LINE, axis=0)  58.1 us
    all_to_all x4, starting transfers between devices, exchange(): return lax.all_to_all(value, axes, split_axis=0, concat_axis=0, tiled=True)  37.5 us
    all_to_all x2, blocking collectives, exchange(): return lax.all_to_all(value, axes, split_axis=0, concat_axis=0, tiled=True)  33.9 us
    ppermute x15, waiting for transfers between devices, shift(): lax.ppermute(value, axis, [(i, (i + step) % size) for i in range(size)])  16.9 us
    pallas_call x2, Pallas kernels, body(): call(products_kernel, [((nz, k, own), BF16)] + [((ny * nx, k, own), BF16)...  8.27 us
    all_gather x1, blocking collectives, body(): parts = lax.all_gather(part, 'core', axis=0)  4.71 us
  transfers between devices with their start and end apart: 19, of which 9 were waited for; matrix products, arithmetic and copies ran while one was open for 0% of the time, Pallas kernels for 0%

profile of v2, /device:TPU:1, one launch (start us, length us, event | category | flops | bytes accessed | tf_op | source)
XLA Modules:
  0.0 227.4 jit_solution(13774732280650956660)
XLA Ops:
  0.0 0.8 multiply_convert_fusion
  0.8 1.1 broadcast_in_dim.10
  1.9 10.5 %all-to-all-start = ((bf16[32,64,256]{2,1,0:T(8,128)(2,1)}), bf16[32,64,256]{2,1,0:T(8,128)(2,1)S(1)}, u32[]{:S(2)}, u32[]{:S(2)}) async-start(bf16[32,64,256]{2,1,0:T(8,128)(2,1)} %broadcast_in_dim.10), calls=%async_computation | async-start | bytes 2097152 | tf_op jit(solution)/shard_map/gather_plane/all_to_all | solution.py:209
  13.0 0.7 pad_add_fusion.places
  13.8 30.1 %all-gather = bf16[1024,256]{1,0:T(8,128)(2,1)S(1)} all-gather(bf16[64,256]{1,0:T(8,128)(2,1)S(1)} %multiply_convert_fusion), channel_id=2, replica_groups=mesh['y'=4,'x'=4,'core'=2,'far'=8,'near'=2] {'far','near'}, dimensions={0}, use_global_device_ids=true | all-gather | bytes 557056 | tf_op jit(solution)/shard_map/gather_line/all_gather | solution.py:229
  43.9 4.1 %products.2 = (bf16[16,64,256]{2,1,0:T(8,128)(2,1)}, bf16[16,64,256]{2,1,0:T(8,128)(2,1)S(1)}, bf16[16,64,256]{2,1,0:T(8,128)(2,1)S(1)}) custom-call(s32[19]{0:T(128)S(1)} %pad_add_fusion.places, bf16[16,64,256]{2,1,0:T(8,128)(2,1)S(1)} %bitcast.4, bf16[32,64,256]{2,1,0:T(8,128)(2,1)S(1)} %all-to-all-done.col_panel, bf16[9,512,512]{2,1,0:T(8,128)(2,1)} %tiles.3), custom_call_target="tpu_custom_call" | custom-call | flops 603979776 | bytes 4718592 | tf_op jit(solution)/shard_map/products/pallas_call | solution.py:232
  48.0 8.4 %collective-permute-start = (bf16[16,64,256]{2,1,0:T(8,128)(2,1)S(1)}, bf16[16,64,256]{2,1,0:T(8,128)(2,1)S(1)}, u32[]{:S(2)}, u32[]{:S(2)}) collective-permute-start(bf16[16,64,256]{2,1,0:T(8,128)(2,1)S(1)} %get-tuple-element.44), channel_id=1, source_target_pairs={{0,16},{16,0},{1,17},{17,1},{2,18},{18,2},{3,19},{19,3},{4,20},{20... | collective-permute-start | bytes 1572872 | tf_op jit(solution)/shard_map/reduce_core/ppermute | solution.py:205
  56.4 1.5 collective-permute-done.got
  57.9 8.5 %all-to-all-start.1 = ((bf16[16,64,256]{2,1,0:T(8,128)(2,1)}), bf16[16,64,256]{2,1,0:T(8,128)(2,1)S(1)}, u32[]{:S(2)}, u32[]{:S(2)}) async-start(bf16[16,64,256]{2,1,0:T(8,128)(2,1)} %get-tuple-element.45), calls=%async_computation.1 | async-start | bytes 1048576 | tf_op jit(solution)/shard_map/reduce_line/all_to_all | solution.py:209
  66.4 0.1 reduce_x.2
  66.5 1.9 collective-permute-start.1
  68.4 3.8 %collective-permute-start.2 = (bf16[4,64,256]{2,1,0:T(8,128)(2,1)S(1)}, bf16[4,64,256]{2,1,0:T(8,128)(2,1)S(1)}, u32[]{:S(2)}, u32[]{:S(2)}) collective-permute-start(bf16[4,64,256]{2,1,0:T(8,128)(2,1)S(1)} %get-tuple-element.50), channel_id=1, source_target_pairs={{0,64},{32,96},{64,0},{96,32},{1,65},{33,97},{65,1},{97,33},{2,66}... | collective-permute-start | bytes 393224 | tf_op jit(solution)/shard_map/reduce_x/ppermute | solution.py:205
  72.3 3.1 %collective-permute-start.3 = (bf16[4,64,256]{2,1,0:T(8,128)(2,1)S(1)}, bf16[4,64,256]{2,1,0:T(8,128)(2,1)S(1)}, u32[]{:S(2)}, u32[]{:S(2)}) collective-permute-start(bf16[4,64,256]{2,1,0:T(8,128)(2,1)S(1)} %get-tuple-element.51), channel_id=1, source_target_pairs={{0,96},{32,0},{64,32},{96,64},{1,97},{33,1},{65,33},{97,65},{2,98}... | collective-permute-start | bytes 393224 | tf_op jit(solution)/shard_map/reduce_x/ppermute | solution.py:205
  75.4 1.0 collective-permute-done.2.refs_1_
  76.3 3.1 %collective-permute-done.3.refs_2_ = bf16[4,64,256]{2,1,0:T(8,128)(2,1)S(1)} collective-permute-done((bf16[4,64,256]{2,1,0:T(8,128)(2,1)S(1)}, bf16[4,64,256]{2,1,0:T(8,128)(2,1)S(1)}, u32[]{:S(2)}, u32[]{:S(2)}) %collective-permute-start.3) | collective-permute-done | bytes 131104 | tf_op jit(solution)/shard_map/reduce_x/ppermute | solution.py:205
  79.5 0.1 reduce_y.2
  79.6 1.9 collective-permute-start.4
  81.5 5.6 %collective-permute-start.5 = (bf16[64,256]{1,0:T(8,128)(2,1)S(1)}, bf16[64,256]{1,0:T(8,128)(2,1)S(1)}, u32[]{:S(2)}, u32[]{:S(2)}) collective-permute-start(bf16[64,256]{1,0:T(8,128)(2,1)S(1)} %get-tuple-element.54), channel_id=1, source_target_pairs={{0,256},{128,384},{256,0},{384,128},{1,257},{129,385},{257,1},{385... | collective-permute-start | bytes 98312 | tf_op jit(solution)/shard_map/reduce_y/ppermute | solution.py:205
  87.1 2.2 collective-permute-start.6
  89.3 0.0 collective-permute-done.4.s1
  89.3 2.7 %collective-permute-done.6.s3 = bf16[64,256]{1,0:T(8,128)(2,1)S(1)} collective-permute-done((bf16[64,256]{1,0:T(8,128)(2,1)S(1)}, bf16[64,256]{1,0:T(8,128)(2,1)S(1)}, u32[]{:S(2)}, u32[]{:S(2)}) %collective-permute-start.6) | collective-permute-done | bytes 32800 | tf_op jit(solution)/shard_map/reduce_y/ppermute | solution.py:205
  92.1 1.2 between.1
  93.2 10.1 %all-to-all-start.2 = ((bf16[32,64,256]{2,1,0:T(8,128)(2,1)}), bf16[32,64,256]{2,1,0:T(8,128)(2,1)S(1)}, u32[]{:S(2)}, u32[]{:S(2)}) async-start(bf16[32,64,256]{2,1,0:T(8,128)(2,1)} %get-tuple-element.56), calls=%async_computation.2 | async-start | bytes 2097152 | tf_op jit(solution)/shard_map/gather_plane/all_to_all | solution.py:209
  103.4 28.0 %all-gather.1 = bf16[1024,256]{1,0:T(8,128)(2,1)S(1)} all-gather(bf16[64,256]{1,0:T(8,128)(2,1)S(1)} %get-tuple-element.57), channel_id=3, replica_groups=mesh['y'=4,'x'=4,'core'=2,'far'=8,'near'=2] {'far','near'}, dimensions={0}, use_global_device_ids=true | all-gather | bytes 557056 | tf_op jit(solution)/shard_map/gather_line/all_gather | solution.py:229
  131.4 4.1 %products.3 = (bf16[16,64,256]{2,1,0:T(8,128)(2,1)}, bf16[16,64,256]{2,1,0:T(8,128)(2,1)S(1)}, bf16[16,64,256]{2,1,0:T(8,128)(2,1)S(1)}) custom-call(s32[19]{0:T(128)S(1)} %pad_add_fusion.places, bf16[16,64,256]{2,1,0:T(8,128)(2,1)S(1)} %bitcast.3, bf16[32,64,256]{2,1,0:T(8,128)(2,1)S(1)} %all-to-all-done.2.col_panel, bf16[9,512,512]{2,1,0:T(8,128)(2,1)} %tiles.3), custom_call_target="tpu_custom_call" | custom-call | flops 603979776 | bytes 4718592 | tf_op jit(solution)/shard_map/products/pallas_call | solution.py:232
  135.5 7.3 %collective-permute-start.7 = (bf16[16,64,256]{2,1,0:T(8,128)(2,1)S(1)}, bf16[16,64,256]{2,1,0:T(8,128)(2,1)S(1)}, u32[]{:S(2)}, u32[]{:S(2)}) collective-permute-start(bf16[16,64,256]{2,1,0:T(8,128)(2,1)S(1)} %get-tuple-element.61), channel_id=1, source_target_pairs={{0,16},{16,0},{1,17},{17,1},{2,18},{18,2},{3,19},{19,3},{4,20},{20... | collective-permute-start | bytes 1572872 | tf_op jit(solution)/shard_map/reduce_core/ppermute | solution.py:205
  142.8 1.5 collective-permute-done.7.got
  144.4 8.5 %all-to-all-start.3 = ((bf16[16,64,256]{2,1,0:T(8,128)(2,1)}), bf16[16,64,256]{2,1,0:T(8,128)(2,1)S(1)}, u32[]{:S(2)}, u32[]{:S(2)}) async-start(bf16[16,64,256]{2,1,0:T(8,128)(2,1)} %get-tuple-element.62), calls=%async_computation.3 | async-start | bytes 1048576 | tf_op jit(solution)/shard_map/reduce_line/all_to_all | solution.py:209
  152.9 0.1 reduce_x.3
  153.0 1.9 collective-permute-start.8
  154.9 3.6 %collective-permute-start.9 = (bf16[4,64,256]{2,1,0:T(8,128)(2,1)S(1)}, bf16[4,64,256]{2,1,0:T(8,128)(2,1)S(1)}, u32[]{:S(2)}, u32[]{:S(2)}) collective-permute-start(bf16[4,64,256]{2,1,0:T(8,128)(2,1)S(1)} %get-tuple-element.67), channel_id=1, source_target_pairs={{0,64},{32,96},{64,0},{96,32},{1,65},{33,97},{65,1},{97,33},{2,66}... | collective-permute-start | bytes 393224 | tf_op jit(solution)/shard_map/reduce_x/ppermute | solution.py:205
  158.6 3.1 %collective-permute-start.10 = (bf16[4,64,256]{2,1,0:T(8,128)(2,1)S(1)}, bf16[4,64,256]{2,1,0:T(8,128)(2,1)S(1)}, u32[]{:S(2)}, u32[]{:S(2)}) collective-permute-start(bf16[4,64,256]{2,1,0:T(8,128)(2,1)S(1)} %get-tuple-element.68), channel_id=1, source_target_pairs={{0,96},{32,0},{64,32},{96,64},{1,97},{33,1},{65,33},{97,65},{2,98}... | collective-permute-start | bytes 393224 | tf_op jit(solution)/shard_map/reduce_x/ppermute | solution.py:205
  161.7 1.1 collective-permute-done.9.refs_1_
  162.8 3.2 %collective-permute-done.10.refs_2_ = bf16[4,64,256]{2,1,0:T(8,128)(2,1)S(1)} collective-permute-done((bf16[4,64,256]{2,1,0:T(8,128)(2,1)S(1)}, bf16[4,64,256]{2,1,0:T(8,128)(2,1)S(1)}, u32[]{:S(2)}, u32[]{:S(2)}) %collective-permute-start.10) | collective-permute-done | bytes 131104 | tf_op jit(solution)/shard_map/reduce_x/ppermute | solution.py:205
  166.0 0.1 reduce_y.3
  166.1 1.9 collective-permute-start.11
  168.0 5.3 %collective-permute-start.12 = (bf16[64,256]{1,0:T(8,128)(2,1)S(1)}, bf16[64,256]{1,0:T(8,128)(2,1)S(1)}, u32[]{:S(2)}, u32[]{:S(2)}) collective-permute-start(bf16[64,256]{1,0:T(8,128)(2,1)S(1)} %get-tuple-element.71), channel_id=1, source_target_pairs={{0,256},{128,384},{256,0},{384,128},{1,257},{129,385},{257,1},{385... | collective-permute-start | bytes 98312 | tf_op jit(solution)/shard_map/reduce_y/ppermute | solution.py:205
  173.3 3.0 %collective-permute-start.13 = (bf16[64,256]{1,0:T(8,128)(2,1)S(1)}, bf16[64,256]{1,0:T(8,128)(2,1)S(1)}, u32[]{:S(2)}, u32[]{:S(2)}) collective-permute-start(bf16[64,256]{1,0:T(8,128)(2,1)S(1)} %get-tuple-element.72), channel_id=1, source_target_pairs={{0,384},{128,0},{256,128},{384,256},{1,385},{129,1},{257,129},{385... | collective-permute-start | bytes 98312 | tf_op jit(solution)/shard_map/reduce_y/ppermute | solution.py:205
  176.3 1.9 collective-permute-done.13.s3
  178.3 0.4 last.1
  178.7 6.4 %collective-permute-start.14 = (f32[1,1152]{1,0:T(1,128)S(1)}, f32[1,1152]{1,0:T(1,128)S(1)}, u32[]{:S(2)}, u32[]{:S(2)}) collective-permute-start(f32[1,1152]{1,0:T(1,128)S(1)} %get-tuple-element.75), channel_id=1, source_target_pairs={{0,16},{16,0},{1,17},{17,1},{2,18},{18,2},{3,19},{19,3},{4,20},{20... | collective-permute-start | bytes 13832 | tf_op jit(solution)/shard_map/gram_core/ppermute | solution.py:205
  185.1 0.8 collective-permute-done.14
  185.9 11.6 %all_to_all.30 = f32[16,1,1152]{2,1,0:T(1,128)S(1)} all-to-all(f32[16,1,1152]{2,1,0:T(1,128)S(1)} %broadcast_in_dim.25), channel_id=1, replica_groups=mesh['y'=4,'x'=4,'core'=2,'far'=8,'near'=2] {'y','x'}, dimensions={0} | all-to-all | bytes 147456 | tf_op jit(solution)/shard_map/gram_plane/all_to_all | solution.py:209
  197.6 0.1 reduce_sum.18
  197.7 22.3 %all_to_all.31 = f32[16,1,1152]{2,1,0:T(1,128)S(1)} all-to-all(f32[16,1,1152]{2,1,0:T(1,128)S(1)} %broadcast_in_dim.26), channel_id=1, replica_groups=mesh['y'=4,'x'=4,'core'=2,'far'=8,'near'=2] {'far','near'}, dimensions={0} | all-to-all | bytes 147456 | tf_op jit(solution)/shard_map/gram_line/all_to_all | solution.py:209
  219.9 0.1 reduce_sum.19
  220.0 4.7 %all-gather.3.parts = f32[2,1,1152]{2,1,0:T(1,128)S(1)} all-gather(f32[1,1,1152]{2,1,0:T(1,128)S(1)} %reshape.19), channel_id=4, replica_groups=mesh['y'=4,'x'=4,'core'=2,'far'=8,'near'=2] {'core'}, dimensions={0}, use_global_device_ids=true | all-gather | bytes 13824 | tf_op jit(solution)/shard_map/gram_pair/all_gather | solution.py:276
  224.7 2.7 %whiten.1 = bf16[64,256]{1,0:T(8,128)(2,1)} custom-call(f32[2,1,1152]{2,1,0:T(1,128)S(1)} %all-gather.3.parts, bf16[64,256]{1,0:T(8,128)(2,1)S(1)} %get-tuple-element.76.fresh), custom_call_target="tpu_custom_call" | custom-call | tf_op jit(solution)/shard_map/whiten/pallas_call | solution.py:278
  (15 shorter events, 0.1 us)
Async XLA Ops:
  1.9 42.0 %all-to-all-start = ((bf16[32,64,256]{2,1,0:T(8,128)(2,1)}), bf16[32,64,256]{2,1,0:T(8,128)(2,1)S(1)}, u32[]{:S(2)}, u32[]{:S(2)}) async-start(bf16[32,64,256]{2,1,0:T(8,128)(2,1)} %broadcast_in_dim.10), calls=%async_computation | async-start | bytes 2097152 | tf_op jit(solution)/shard_map/gather_plane/all_to_all | solution.py:209
  13.7 78.3 %copy-start = (f32[256]{0:T(256)S(1)}, f32[256]{0:T(256)}, u32[]{:S(2)}) copy-start(f32[256]{0:T(256)} %param.7) | copy-start | bytes 3076
  48.0 9.9 %collective-permute-start = (bf16[16,64,256]{2,1,0:T(8,128)(2,1)S(1)}, bf16[16,64,256]{2,1,0:T(8,128)(2,1)S(1)}, u32[]{:S(2)}, u32[]{:S(2)}) collective-permute-start(bf16[16,64,256]{2,1,0:T(8,128)(2,1)S(1)} %get-tuple-element.44), channel_id=1, source_target_pairs={{0,16},{16,0},{1,17},{17,1},{2,18},{18,2},{3,19},{19,3},{4,20},{20... | collective-permute-start | bytes 1572872 | tf_op jit(solution)/shard_map/reduce_core/ppermute | solution.py:205
  57.9 34.1 %all-to-all-start.1 = ((bf16[16,64,256]{2,1,0:T(8,128)(2,1)}), bf16[16,64,256]{2,1,0:T(8,128)(2,1)S(1)}, u32[]{:S(2)}, u32[]{:S(2)}) async-start(bf16[16,64,256]{2,1,0:T(8,128)(2,1)} %get-tuple-element.45), calls=%async_computation.1 | async-start | bytes 1048576 | tf_op jit(solution)/shard_map/reduce_line/all_to_all | solution.py:209
  66.5 8.8 %collective-permute-start.1 = (bf16[4,64,256]{2,1,0:T(8,128)(2,1)S(1)}, bf16[4,64,256]{2,1,0:T(8,128)(2,1)S(1)}, u32[]{:S(2)}, u32[]{:S(2)}) collective-permute-start(bf16[4,64,256]{2,1,0:T(8,128)(2,1)S(1)} %get-tuple-element.49), channel_id=1, source_target_pairs={{0,32},{32,64},{64,96},{96,0},{1,33},{33,65},{65,97},{97,1},{2,34}... | collective-permute-start | bytes 393224 | tf_op jit(solution)/shard_map/reduce_x/ppermute | solution.py:205
  68.4 7.9 %collective-permute-start.2 = (bf16[4,64,256]{2,1,0:T(8,128)(2,1)S(1)}, bf16[4,64,256]{2,1,0:T(8,128)(2,1)S(1)}, u32[]{:S(2)}, u32[]{:S(2)}) collective-permute-start(bf16[4,64,256]{2,1,0:T(8,128)(2,1)S(1)} %get-tuple-element.50), channel_id=1, source_target_pairs={{0,64},{32,96},{64,0},{96,32},{1,65},{33,97},{65,1},{97,33},{2,66}... | collective-permute-start | bytes 393224 | tf_op jit(solution)/shard_map/reduce_x/ppermute | solution.py:205
  72.3 7.2 %collective-permute-start.3 = (bf16[4,64,256]{2,1,0:T(8,128)(2,1)S(1)}, bf16[4,64,256]{2,1,0:T(8,128)(2,1)S(1)}, u32[]{:S(2)}, u32[]{:S(2)}) collective-permute-start(bf16[4,64,256]{2,1,0:T(8,128)(2,1)S(1)} %get-tuple-element.51), channel_id=1, source_target_pairs={{0,96},{32,0},{64,32},{96,64},{1,97},{33,1},{65,33},{97,65},{2,98}... | collective-permute-start | bytes 393224 | tf_op jit(solution)/shard_map/reduce_x/ppermute | solution.py:205
  79.6 9.7 %collective-permute-start.4 = (bf16[64,256]{1,0:T(8,128)(2,1)S(1)}, bf16[64,256]{1,0:T(8,128)(2,1)S(1)}, u32[]{:S(2)}, u32[]{:S(2)}) collective-permute-start(bf16[64,256]{1,0:T(8,128)(2,1)S(1)} %get-tuple-element.53), channel_id=1, source_target_pairs={{0,128},{128,256},{256,384},{384,0},{1,129},{129,257},{257,385},{3... | collective-permute-start | bytes 98312 | tf_op jit(solution)/shard_map/reduce_y/ppermute | solution.py:205
  81.5 7.8 %collective-permute-start.5 = (bf16[64,256]{1,0:T(8,128)(2,1)S(1)}, bf16[64,256]{1,0:T(8,128)(2,1)S(1)}, u32[]{:S(2)}, u32[]{:S(2)}) collective-permute-start(bf16[64,256]{1,0:T(8,128)(2,1)S(1)} %get-tuple-element.54), channel_id=1, source_target_pairs={{0,256},{128,384},{256,0},{384,128},{1,257},{129,385},{257,1},{385... | collective-permute-start | bytes 98312 | tf_op jit(solution)/shard_map/reduce_y/ppermute | solution.py:205
  87.1 5.0 %collective-permute-start.6 = (bf16[64,256]{1,0:T(8,128)(2,1)S(1)}, bf16[64,256]{1,0:T(8,128)(2,1)S(1)}, u32[]{:S(2)}, u32[]{:S(2)}) collective-permute-start(bf16[64,256]{1,0:T(8,128)(2,1)S(1)} %get-tuple-element.55), channel_id=1, source_target_pairs={{0,384},{128,0},{256,128},{384,256},{1,385},{129,1},{257,129},{385... | collective-permute-start | bytes 98312 | tf_op jit(solution)/shard_map/reduce_y/ppermute | solution.py:205
  93.2 38.1 %all-to-all-start.2 = ((bf16[32,64,256]{2,1,0:T(8,128)(2,1)}), bf16[32,64,256]{2,1,0:T(8,128)(2,1)S(1)}, u32[]{:S(2)}, u32[]{:S(2)}) async-start(bf16[32,64,256]{2,1,0:T(8,128)(2,1)} %get-tuple-element.56), calls=%async_computation.2 | async-start | bytes 2097152 | tf_op jit(solution)/shard_map/gather_plane/all_to_all | solution.py:209
  135.5 8.9 %collective-permute-start.7 = (bf16[16,64,256]{2,1,0:T(8,128)(2,1)S(1)}, bf16[16,64,256]{2,1,0:T(8,128)(2,1)S(1)}, u32[]{:S(2)}, u32[]{:S(2)}) collective-permute-start(bf16[16,64,256]{2,1,0:T(8,128)(2,1)S(1)} %get-tuple-element.61), channel_id=1, source_target_pairs={{0,16},{16,0},{1,17},{17,1},{2,18},{18,2},{3,19},{19,3},{4,20},{20... | collective-permute-start | bytes 1572872 | tf_op jit(solution)/shard_map/reduce_core/ppermute | solution.py:205
  144.4 33.9 %all-to-all-start.3 = ((bf16[16,64,256]{2,1,0:T(8,128)(2,1)}), bf16[16,64,256]{2,1,0:T(8,128)(2,1)S(1)}, u32[]{:S(2)}, u32[]{:S(2)}) async-start(bf16[16,64,256]{2,1,0:T(8,128)(2,1)} %get-tuple-element.62), calls=%async_computation.3 | async-start | bytes 1048576 | tf_op jit(solution)/shard_map/reduce_line/all_to_all | solution.py:209
  153.0 8.7 %collective-permute-start.8 = (bf16[4,64,256]{2,1,0:T(8,128)(2,1)S(1)}, bf16[4,64,256]{2,1,0:T(8,128)(2,1)S(1)}, u32[]{:S(2)}, u32[]{:S(2)}) collective-permute-start(bf16[4,64,256]{2,1,0:T(8,128)(2,1)S(1)} %get-tuple-element.66), channel_id=1, source_target_pairs={{0,32},{32,64},{64,96},{96,0},{1,33},{33,65},{65,97},{97,1},{2,34}... | collective-permute-start | bytes 393224 | tf_op jit(solution)/shard_map/reduce_x/ppermute | solution.py:205
  154.9 7.9 %collective-permute-start.9 = (bf16[4,64,256]{2,1,0:T(8,128)(2,1)S(1)}, bf16[4,64,256]{2,1,0:T(8,128)(2,1)S(1)}, u32[]{:S(2)}, u32[]{:S(2)}) collective-permute-start(bf16[4,64,256]{2,1,0:T(8,128)(2,1)S(1)} %get-tuple-element.67), channel_id=1, source_target_pairs={{0,64},{32,96},{64,0},{96,32},{1,65},{33,97},{65,1},{97,33},{2,66}... | collective-permute-start | bytes 393224 | tf_op jit(solution)/shard_map/reduce_x/ppermute | solution.py:205
  158.6 7.4 %collective-permute-start.10 = (bf16[4,64,256]{2,1,0:T(8,128)(2,1)S(1)}, bf16[4,64,256]{2,1,0:T(8,128)(2,1)S(1)}, u32[]{:S(2)}, u32[]{:S(2)}) collective-permute-start(bf16[4,64,256]{2,1,0:T(8,128)(2,1)S(1)} %get-tuple-element.68), channel_id=1, source_target_pairs={{0,96},{32,0},{64,32},{96,64},{1,97},{33,1},{65,33},{97,65},{2,98}... | collective-permute-start | bytes 393224 | tf_op jit(solution)/shard_map/reduce_x/ppermute | solution.py:205
  166.1 10.2 %collective-permute-start.11 = (bf16[64,256]{1,0:T(8,128)(2,1)S(1)}, bf16[64,256]{1,0:T(8,128)(2,1)S(1)}, u32[]{:S(2)}, u32[]{:S(2)}) collective-permute-start(bf16[64,256]{1,0:T(8,128)(2,1)S(1)} %get-tuple-element.70), channel_id=1, source_target_pairs={{0,128},{128,256},{256,384},{384,0},{1,129},{129,257},{257,385},{3... | collective-permute-start | bytes 98312 | tf_op jit(solution)/shard_map/reduce_y/ppermute | solution.py:205
  168.0 8.3 %collective-permute-start.12 = (bf16[64,256]{1,0:T(8,128)(2,1)S(1)}, bf16[64,256]{1,0:T(8,128)(2,1)S(1)}, u32[]{:S(2)}, u32[]{:S(2)}) collective-permute-start(bf16[64,256]{1,0:T(8,128)(2,1)S(1)} %get-tuple-element.71), channel_id=1, source_target_pairs={{0,256},{128,384},{256,0},{384,128},{1,257},{129,385},{257,1},{385... | collective-permute-start | bytes 98312 | tf_op jit(solution)/shard_map/reduce_y/ppermute | solution.py:205
  173.3 5.0 %collective-permute-start.13 = (bf16[64,256]{1,0:T(8,128)(2,1)S(1)}, bf16[64,256]{1,0:T(8,128)(2,1)S(1)}, u32[]{:S(2)}, u32[]{:S(2)}) collective-permute-start(bf16[64,256]{1,0:T(8,128)(2,1)S(1)} %get-tuple-element.72), channel_id=1, source_target_pairs={{0,384},{128,0},{256,128},{384,256},{1,385},{129,1},{257,129},{385... | collective-permute-start | bytes 98312 | tf_op jit(solution)/shard_map/reduce_y/ppermute | solution.py:205
  178.7 7.2 %collective-permute-start.14 = (f32[1,1152]{1,0:T(1,128)S(1)}, f32[1,1152]{1,0:T(1,128)S(1)}, u32[]{:S(2)}, u32[]{:S(2)}) collective-permute-start(f32[1,1152]{1,0:T(1,128)S(1)} %get-tuple-element.75), channel_id=1, source_target_pairs={{0,16},{16,0},{1,17},{17,1},{2,18},{18,2},{3,19},{19,3},{4,20},{20... | collective-permute-start | bytes 13832 | tf_op jit(solution)/shard_map/gram_core/ppermute | solution.py:205

commit v3 on v2

--- a/solution.py
+++ b/solution.py
@@ -37,16 +37,16 @@
 ):
     slots = tiles.shape[0]
     copies = [pltpu.make_async_copy(tiles.at[s], blocks.at[s], tile_sems.at[s]) for s in range(slots)]
-    for copy in copies:
-        copy.start()
+    for s, copy in enumerate(copies):
+        pl.when(s < places[2 * slots])(copy.start)
     row_sum[...] = jnp.zeros_like(row_sum)
     col_sum[...] = jnp.zeros_like(col_sum)
     half = row_panel.shape[2]
     for s, copy in enumerate(copies):
-        copy.wait()
 
         @pl.when(s < places[2 * slots])
         def _():
+            copy.wait()
             r, c = places[s], places[slots + s]
             low, high = 2 * r, 2 * r + 1
             left, right = 2 * c, 2 * c + 1
@@ -151,15 +151,14 @@
     )
 
 
-def last_kernel(scale, arrived, own, s1, s2, s3, weights, first, fresh, keep, send):
+def last_kernel(scale, arrived, own, s1, s2, s3, weights, first, fresh, copies):
     rounded = add_up(arrived, own, (s1, s2, s3), weights).astype(BF16)
     fresh[...] = rounded
     gram = lax.dot_general(rounded, rounded, NT, preferred_element_type=F32)
     packed = pack((gram + RIDGE * first[...]) * scale)
     h = packed.shape[1] // 2
-    second = lax.axis_index("core") == 1
-    keep[...] = jnp.where(second, packed[:, h:], packed[:, :h])
-    send[...] = jnp.where(second, packed[:, :h], packed[:, h:])
+    for k in range(copies.shape[0]):
+        copies[k] = packed[:, h:] if k % 2 else packed[:, :h]
 
 
 def whiten_kernel(parts, fresh, out, factor):
@@ -259,16 +258,13 @@
                 )(arrived, *moved, gains)
         else:
             with jax.named_scope("last"):
-                fresh, keep, send = call(
+                fresh, copies = call(
                     functools.partial(last_kernel, 1.0 / vertices),
-                    [((k, own), BF16)] + [((1, 9 * 128), F32)] * 2,
+                    [((k, own), BF16), ((rows, 1, 9 * 128), F32)],
                     [VMEM] * 7,
                 )(arrived, *moved, gains, gram)
-    with jax.named_scope("gram_core"):
-        part = keep + shift(send, "core", 1, 2)
     with jax.named_scope("gram_plane"):
-        copies = jnp.broadcast_to(part[None], (ny * nx,) + part.shape)
-        part = jnp.sum(exchange(copies, ("y", "x")), axis=0)
+        part = jnp.sum(exchange(copies, ROW), axis=0)
     with jax.named_scope("gram_line"):
         copies = jnp.broadcast_to(part[None], (nz,) + part.shape)
         part = jnp.sum(exchange(copies, LINE), axis=0)

time: 229 us -> 226 us (0.987)
  blocking collectives: 96.7 us -> 102 us
  starting transfers between devices: 97.1 us -> 93.1 us
  waiting for transfers between devices: 17 us -> 14.6 us
    all_to_all x2, blocking collectives: 33.9 us -> 40.6 us  [exchange(): return lax.all_to_all(value, axes, split_axis=0, concat_axis=0, tiled=True)]
    all_to_all x4, starting transfers between devices: 37.5 us -> 33.6 us  [exchange(): return lax.all_to_all(value, axes, split_axis=0, concat_axis=0, tiled=True)]
    ppermute x15 -> x14, waiting for transfers between devices: 16.9 us -> 14.6 us  [shift(): lax.ppermute(value, axis, [(i, (i + step) % size) for i in range(size)])]
    ppermute x15 -> x14, starting transfers between devices: 59.5 us -> 59.6 us  [shift(): lax.ppermute(value, axis, [(i, (i + step) % size) for i in range(size)])]
  transfers between devices with their start and end apart: 19 -> 18, of which waited for: 9 -> 8; matrix products, arithmetic and copies ran while one was open for 0% -> 0% of each run, Pallas kernels for 0% -> 0%
where the time goes in v3:
time: 226 us; the launch traced here: 225 us
  blocking collectives  102 us (45%)
  starting transfers between devices  93.1 us (41%)
  waiting for transfers between devices  14.6 us (6%)
  Pallas kernels  11.5 us (5%)
    ppermute x14, starting transfers between devices, shift(): lax.ppermute(value, axis, [(i, (i + step) % size) for i in range(size)])  59.6 us
    all_gather x2, blocking collectives, body(): row_panel = lax.all_gather(scaled, LINE, axis=0)  58.1 us
    all_to_all x2, blocking collectives, exchange(): return lax.all_to_all(value, axes, split_axis=0, concat_axis=0, tiled=True)  40.6 us
    all_to_all x4, starting transfers between devices, exchange(): return lax.all_to_all(value, axes, split_axis=0, concat_axis=0, tiled=True)  33.6 us
    ppermute x14, waiting for transfers between devices, shift(): lax.ppermute(value, axis, [(i, (i + step) % size) for i in range(size)])  14.6 us
    pallas_call x2, Pallas kernels, body(): call(products_kernel, [((nz, k, own), BF16)] + [((ny * nx, k, own), BF16)...  6.81 us
  transfers between devices with their start and end apart: 18, of which 8 were waited for; matrix products, arithmetic and copies ran while one was open for 0% of the time, Pallas kernels for 0%

profile of v3, /device:TPU:1, one launch (start us, length us, event | category | flops | bytes accessed | tf_op | source)
XLA Modules:
  0.0 225.2 jit_solution(11631255229326470497)
XLA Ops:
  0.0 0.8 multiply_convert_fusion
  0.8 1.1 broadcast_in_dim.6
  1.9 10.5 %all-to-all-start = ((bf16[32,64,256]{2,1,0:T(8,128)(2,1)}), bf16[32,64,256]{2,1,0:T(8,128)(2,1)S(1)}, u32[]{:S(2)}, u32[]{:S(2)}) async-start(bf16[32,64,256]{2,1,0:T(8,128)(2,1)} %broadcast_in_dim.6), calls=%async_computation | async-start | bytes 2097152 | tf_op jit(solution)/shard_map/gather_plane/all_to_all | solution.py:208
  13.0 0.7 pad_add_fusion.places
  13.8 30.1 %all-gather = bf16[1024,256]{1,0:T(8,128)(2,1)S(1)} all-gather(bf16[64,256]{1,0:T(8,128)(2,1)S(1)} %multiply_convert_fusion), channel_id=2, replica_groups=mesh['y'=4,'x'=4,'core'=2,'far'=8,'near'=2] {'far','near'}, dimensions={0}, use_global_device_ids=true | all-gather | bytes 557056 | tf_op jit(solution)/shard_map/gather_line/all_gather | solution.py:228
  43.9 3.4 %products.2 = (bf16[16,64,256]{2,1,0:T(8,128)(2,1)}, bf16[16,64,256]{2,1,0:T(8,128)(2,1)S(1)}, bf16[16,64,256]{2,1,0:T(8,128)(2,1)S(1)}) custom-call(s32[19]{0:T(128)S(1)} %pad_add_fusion.places, bf16[16,64,256]{2,1,0:T(8,128)(2,1)S(1)} %bitcast.4, bf16[32,64,256]{2,1,0:T(8,128)(2,1)S(1)} %all-to-all-done.col_panel, bf16[9,512,512]{2,1,0:T(8,128)(2,1)} %tiles.3), custom_call_target="tpu_custom_call" | custom-call | flops 603979776 | bytes 4718592 | tf_op jit(solution)/shard_map/products/pallas_call | solution.py:231
  47.3 10.1 %collective-permute-start = (bf16[16,64,256]{2,1,0:T(8,128)(2,1)S(1)}, bf16[16,64,256]{2,1,0:T(8,128)(2,1)S(1)}, u32[]{:S(2)}, u32[]{:S(2)}) collective-permute-start(bf16[16,64,256]{2,1,0:T(8,128)(2,1)S(1)} %get-tuple-element.43), channel_id=1, source_target_pairs={{0,16},{16,0},{1,17},{17,1},{2,18},{18,2},{3,19},{19,3},{4,20},{20... | collective-permute-start | bytes 1572872 | tf_op jit(solution)/shard_map/reduce_core/ppermute | solution.py:204
  57.4 1.5 collective-permute-done.got
  58.9 6.0 %all-to-all-start.1 = ((bf16[16,64,256]{2,1,0:T(8,128)(2,1)}), bf16[16,64,256]{2,1,0:T(8,128)(2,1)S(1)}, u32[]{:S(2)}, u32[]{:S(2)}) async-start(bf16[16,64,256]{2,1,0:T(8,128)(2,1)} %get-tuple-element.44), calls=%async_computation.1 | async-start | bytes 1048576 | tf_op jit(solution)/shard_map/reduce_line/all_to_all | solution.py:208
  64.9 0.1 reduce_x.2
  65.1 3.1 %collective-permute-start.1 = (bf16[4,64,256]{2,1,0:T(8,128)(2,1)S(1)}, bf16[4,64,256]{2,1,0:T(8,128)(2,1)S(1)}, u32[]{:S(2)}, u32[]{:S(2)}) collective-permute-start(bf16[4,64,256]{2,1,0:T(8,128)(2,1)S(1)} %get-tuple-element.48), channel_id=1, source_target_pairs={{0,32},{32,64},{64,96},{96,0},{1,33},{33,65},{65,97},{97,1},{2,34}... | collective-permute-start | bytes 393224 | tf_op jit(solution)/shard_map/reduce_x/ppermute | solution.py:204
  68.2 4.0 %collective-permute-start.2 = (bf16[4,64,256]{2,1,0:T(8,128)(2,1)S(1)}, bf16[4,64,256]{2,1,0:T(8,128)(2,1)S(1)}, u32[]{:S(2)}, u32[]{:S(2)}) collective-permute-start(bf16[4,64,256]{2,1,0:T(8,128)(2,1)S(1)} %get-tuple-element.49), channel_id=1, source_target_pairs={{0,64},{32,96},{64,0},{96,32},{1,65},{33,97},{65,1},{97,33},{2,66}... | collective-permute-start | bytes 393224 | tf_op jit(solution)/shard_map/reduce_x/ppermute | solution.py:204
  72.2 3.1 %collective-permute-start.3 = (bf16[4,64,256]{2,1,0:T(8,128)(2,1)S(1)}, bf16[4,64,256]{2,1,0:T(8,128)(2,1)S(1)}, u32[]{:S(2)}, u32[]{:S(2)}) collective-permute-start(bf16[4,64,256]{2,1,0:T(8,128)(2,1)S(1)} %get-tuple-element.50), channel_id=1, source_target_pairs={{0,96},{32,0},{64,32},{96,64},{1,97},{33,1},{65,33},{97,65},{2,98}... | collective-permute-start | bytes 393224 | tf_op jit(solution)/shard_map/reduce_x/ppermute | solution.py:204
  75.3 0.0 collective-permute-done.1.refs_0_
  75.3 0.1 collective-permute-done.2.refs_1_
  75.5 2.8 %collective-permute-done.3.refs_2_ = bf16[4,64,256]{2,1,0:T(8,128)(2,1)S(1)} collective-permute-done((bf16[4,64,256]{2,1,0:T(8,128)(2,1)S(1)}, bf16[4,64,256]{2,1,0:T(8,128)(2,1)S(1)}, u32[]{:S(2)}, u32[]{:S(2)}) %collective-permute-start.3) | collective-permute-done | bytes 131104 | tf_op jit(solution)/shard_map/reduce_x/ppermute | solution.py:204
  78.2 0.1 reduce_y.2
  78.3 3.4 %collective-permute-start.4 = (bf16[64,256]{1,0:T(8,128)(2,1)S(1)}, bf16[64,256]{1,0:T(8,128)(2,1)S(1)}, u32[]{:S(2)}, u32[]{:S(2)}) collective-permute-start(bf16[64,256]{1,0:T(8,128)(2,1)S(1)} %get-tuple-element.52), channel_id=1, source_target_pairs={{0,128},{128,256},{256,384},{384,0},{1,129},{129,257},{257,385},{3... | collective-permute-start | bytes 98312 | tf_op jit(solution)/shard_map/reduce_y/ppermute | solution.py:204
  81.8 4.6 %collective-permute-start.5 = (bf16[64,256]{1,0:T(8,128)(2,1)S(1)}, bf16[64,256]{1,0:T(8,128)(2,1)S(1)}, u32[]{:S(2)}, u32[]{:S(2)}) collective-permute-start(bf16[64,256]{1,0:T(8,128)(2,1)S(1)} %get-tuple-element.53), channel_id=1, source_target_pairs={{0,256},{128,384},{256,0},{384,128},{1,257},{129,385},{257,1},{385... | collective-permute-start | bytes 98312 | tf_op jit(solution)/shard_map/reduce_y/ppermute | solution.py:204
  86.4 2.1 collective-permute-start.6
  88.5 0.0 collective-permute-done.5.s2
  88.5 2.9 %collective-permute-done.6.s3 = bf16[64,256]{1,0:T(8,128)(2,1)S(1)} collective-permute-done((bf16[64,256]{1,0:T(8,128)(2,1)S(1)}, bf16[64,256]{1,0:T(8,128)(2,1)S(1)}, u32[]{:S(2)}, u32[]{:S(2)}) %collective-permute-start.6) | collective-permute-done | bytes 32800 | tf_op jit(solution)/shard_map/reduce_y/ppermute | solution.py:204
  91.3 1.2 between.1
  92.5 10.6 %all-to-all-start.2 = ((bf16[32,64,256]{2,1,0:T(8,128)(2,1)}), bf16[32,64,256]{2,1,0:T(8,128)(2,1)S(1)}, u32[]{:S(2)}, u32[]{:S(2)}) async-start(bf16[32,64,256]{2,1,0:T(8,128)(2,1)} %get-tuple-element.55), calls=%async_computation.2 | async-start | bytes 2097152 | tf_op jit(solution)/shard_map/gather_plane/all_to_all | solution.py:208
  103.1 28.0 %all-gather.1 = bf16[1024,256]{1,0:T(8,128)(2,1)S(1)} all-gather(bf16[64,256]{1,0:T(8,128)(2,1)S(1)} %get-tuple-element.56), channel_id=3, replica_groups=mesh['y'=4,'x'=4,'core'=2,'far'=8,'near'=2] {'far','near'}, dimensions={0}, use_global_device_ids=true | all-gather | bytes 557056 | tf_op jit(solution)/shard_map/gather_line/all_gather | solution.py:228
  131.1 0.0 all-to-all-done.2.col_panel
  131.1 3.4 %products.3 = (bf16[16,64,256]{2,1,0:T(8,128)(2,1)}, bf16[16,64,256]{2,1,0:T(8,128)(2,1)S(1)}, bf16[16,64,256]{2,1,0:T(8,128)(2,1)S(1)}) custom-call(s32[19]{0:T(128)S(1)} %pad_add_fusion.places, bf16[16,64,256]{2,1,0:T(8,128)(2,1)S(1)} %bitcast.3, bf16[32,64,256]{2,1,0:T(8,128)(2,1)S(1)} %all-to-all-done.2.col_panel, bf16[9,512,512]{2,1,0:T(8,128)(2,1)} %tiles.3), custom_call_target="tpu_custom_call" | custom-call | flops 603979776 | bytes 4718592 | tf_op jit(solution)/shard_map/products/pallas_call | solution.py:231
  134.5 9.0 %collective-permute-start.7 = (bf16[16,64,256]{2,1,0:T(8,128)(2,1)S(1)}, bf16[16,64,256]{2,1,0:T(8,128)(2,1)S(1)}, u32[]{:S(2)}, u32[]{:S(2)}) collective-permute-start(bf16[16,64,256]{2,1,0:T(8,128)(2,1)S(1)} %get-tuple-element.60), channel_id=1, source_target_pairs={{0,16},{16,0},{1,17},{17,1},{2,18},{18,2},{3,19},{19,3},{4,20},{20... | collective-permute-start | bytes 1572872 | tf_op jit(solution)/shard_map/reduce_core/ppermute | solution.py:204
  143.5 1.5 collective-permute-done.7.got
  145.1 6.5 %all-to-all-start.3 = ((bf16[16,64,256]{2,1,0:T(8,128)(2,1)}), bf16[16,64,256]{2,1,0:T(8,128)(2,1)S(1)}, u32[]{:S(2)}, u32[]{:S(2)}) async-start(bf16[16,64,256]{2,1,0:T(8,128)(2,1)} %get-tuple-element.61), calls=%async_computation.3 | async-start | bytes 1048576 | tf_op jit(solution)/shard_map/reduce_line/all_to_all | solution.py:208
  151.6 0.1 reduce_x.3
  151.8 2.8 %collective-permute-start.8 = (bf16[4,64,256]{2,1,0:T(8,128)(2,1)S(1)}, bf16[4,64,256]{2,1,0:T(8,128)(2,1)S(1)}, u32[]{:S(2)}, u32[]{:S(2)}) collective-permute-start(bf16[4,64,256]{2,1,0:T(8,128)(2,1)S(1)} %get-tuple-element.65), channel_id=1, source_target_pairs={{0,32},{32,64},{64,96},{96,0},{1,33},{33,65},{65,97},{97,1},{2,34}... | collective-permute-start | bytes 393224 | tf_op jit(solution)/shard_map/reduce_x/ppermute | solution.py:204
  154.6 4.7 %collective-permute-start.9 = (bf16[4,64,256]{2,1,0:T(8,128)(2,1)S(1)}, bf16[4,64,256]{2,1,0:T(8,128)(2,1)S(1)}, u32[]{:S(2)}, u32[]{:S(2)}) collective-permute-start(bf16[4,64,256]{2,1,0:T(8,128)(2,1)S(1)} %get-tuple-element.66), channel_id=1, source_target_pairs={{0,64},{32,96},{64,0},{96,32},{1,65},{33,97},{65,1},{97,33},{2,66}... | collective-permute-start | bytes 393224 | tf_op jit(solution)/shard_map/reduce_x/ppermute | solution.py:204
  159.3 2.9 %collective-permute-start.10 = (bf16[4,64,256]{2,1,0:T(8,128)(2,1)S(1)}, bf16[4,64,256]{2,1,0:T(8,128)(2,1)S(1)}, u32[]{:S(2)}, u32[]{:S(2)}) collective-permute-start(bf16[4,64,256]{2,1,0:T(8,128)(2,1)S(1)} %get-tuple-element.67), channel_id=1, source_target_pairs={{0,96},{32,0},{64,32},{96,64},{1,97},{33,1},{65,33},{97,65},{2,98}... | collective-permute-start | bytes 393224 | tf_op jit(solution)/shard_map/reduce_x/ppermute | solution.py:204
  162.2 1.3 collective-permute-done.9.refs_1_
  163.4 1.9 collective-permute-done.10.refs_2_
  165.3 0.1 reduce_y.3
  165.4 2.5 %collective-permute-start.11 = (bf16[64,256]{1,0:T(8,128)(2,1)S(1)}, bf16[64,256]{1,0:T(8,128)(2,1)S(1)}, u32[]{:S(2)}, u32[]{:S(2)}) collective-permute-start(bf16[64,256]{1,0:T(8,128)(2,1)S(1)} %get-tuple-element.69), channel_id=1, source_target_pairs={{0,128},{128,256},{256,384},{384,0},{1,129},{129,257},{257,385},{3... | collective-permute-start | bytes 98312 | tf_op jit(solution)/shard_map/reduce_y/ppermute | solution.py:204
  167.9 4.9 %collective-permute-start.12 = (bf16[64,256]{1,0:T(8,128)(2,1)S(1)}, bf16[64,256]{1,0:T(8,128)(2,1)S(1)}, u32[]{:S(2)}, u32[]{:S(2)}) collective-permute-start(bf16[64,256]{1,0:T(8,128)(2,1)S(1)} %get-tuple-element.70), channel_id=1, source_target_pairs={{0,256},{128,384},{256,0},{384,128},{1,257},{129,385},{257,1},{385... | collective-permute-start | bytes 98312 | tf_op jit(solution)/shard_map/reduce_y/ppermute | solution.py:204
  172.8 2.3 %collective-permute-start.13 = (bf16[64,256]{1,0:T(8,128)(2,1)S(1)}, bf16[64,256]{1,0:T(8,128)(2,1)S(1)}, u32[]{:S(2)}, u32[]{:S(2)}) collective-permute-start(bf16[64,256]{1,0:T(8,128)(2,1)S(1)} %get-tuple-element.71), channel_id=1, source_target_pairs={{0,384},{128,0},{256,128},{384,256},{1,385},{129,1},{257,129},{385... | collective-permute-start | bytes 98312 | tf_op jit(solution)/shard_map/reduce_y/ppermute | solution.py:204
  175.1 2.6 %collective-permute-done.13.s3 = bf16[64,256]{1,0:T(8,128)(2,1)S(1)} collective-permute-done((bf16[64,256]{1,0:T(8,128)(2,1)S(1)}, bf16[64,256]{1,0:T(8,128)(2,1)S(1)}, u32[]{:S(2)}, u32[]{:S(2)}) %collective-permute-start.13) | collective-permute-done | bytes 32800 | tf_op jit(solution)/shard_map/reduce_y/ppermute | solution.py:204
  177.7 0.4 last.1
  178.1 18.4 %all_to_all.30 = f32[32,1,1152]{2,1,0:T(1,128)S(1)} all-to-all(f32[32,1,1152]{2,1,0:T(1,128)S(1)} %get-tuple-element.73), channel_id=1, replica_groups=mesh['y'=4,'x'=4,'core'=2,'far'=8,'near'=2] {'y','x','core'}, dimensions={0} | all-to-all | bytes 294912 | tf_op jit(solution)/shard_map/gram_plane/all_to_all | solution.py:208
  196.5 0.1 reduce_sum.18
  196.7 22.2 %all_to_all.31 = f32[16,1,1152]{2,1,0:T(1,128)S(1)} all-to-all(f32[16,1,1152]{2,1,0:T(1,128)S(1)} %broadcast_in_dim.16), channel_id=1, replica_groups=mesh['y'=4,'x'=4,'core'=2,'far'=8,'near'=2] {'far','near'}, dimensions={0} | all-to-all | bytes 147456 | tf_op jit(solution)/shard_map/gram_line/all_to_all | solution.py:208
  218.9 0.1 reduce_sum.19
  219.0 3.5 %all-gather.3.parts = f32[2,1,1152]{2,1,0:T(1,128)S(1)} all-gather(f32[1,1,1152]{2,1,0:T(1,128)S(1)} %reshape.16), channel_id=4, replica_groups=mesh['y'=4,'x'=4,'core'=2,'far'=8,'near'=2] {'core'}, dimensions={0}, use_global_device_ids=true | all-gather | bytes 13824 | tf_op jit(solution)/shard_map/gram_pair/all_gather | solution.py:272
  222.5 2.7 %whiten.1 = bf16[64,256]{1,0:T(8,128)(2,1)} custom-call(f32[2,1,1152]{2,1,0:T(1,128)S(1)} %all-gather.3.parts, bf16[64,256]{1,0:T(8,128)(2,1)S(1)} %get-tuple-element.74.fresh), custom_call_target="tpu_custom_call" | custom-call | tf_op jit(solution)/shard_map/whiten/pallas_call | solution.py:274
  (11 shorter events, 0.1 us)
Async XLA Ops:
  1.9 42.0 %all-to-all-start = ((bf16[32,64,256]{2,1,0:T(8,128)(2,1)}), bf16[32,64,256]{2,1,0:T(8,128)(2,1)S(1)}, u32[]{:S(2)}, u32[]{:S(2)}) async-start(bf16[32,64,256]{2,1,0:T(8,128)(2,1)} %broadcast_in_dim.6), calls=%async_computation | async-start | bytes 2097152 | tf_op jit(solution)/shard_map/gather_plane/all_to_all | solution.py:208
  13.8 77.6 %copy-start = (f32[256]{0:T(256)S(1)}, f32[256]{0:T(256)}, u32[]{:S(2)}) copy-start(f32[256]{0:T(256)} %param.7) | copy-start | bytes 3076
  47.3 11.6 %collective-permute-start = (bf16[16,64,256]{2,1,0:T(8,128)(2,1)S(1)}, bf16[16,64,256]{2,1,0:T(8,128)(2,1)S(1)}, u32[]{:S(2)}, u32[]{:S(2)}) collective-permute-start(bf16[16,64,256]{2,1,0:T(8,128)(2,1)S(1)} %get-tuple-element.43), channel_id=1, source_target_pairs={{0,16},{16,0},{1,17},{17,1},{2,18},{18,2},{3,19},{19,3},{4,20},{20... | collective-permute-start | bytes 1572872 | tf_op jit(solution)/shard_map/reduce_core/ppermute | solution.py:204
  58.9 32.4 %all-to-all-start.1 = ((bf16[16,64,256]{2,1,0:T(8,128)(2,1)}), bf16[16,64,256]{2,1,0:T(8,128)(2,1)S(1)}, u32[]{:S(2)}, u32[]{:S(2)}) async-start(bf16[16,64,256]{2,1,0:T(8,128)(2,1)} %get-tuple-element.44), calls=%async_computation.1 | async-start | bytes 1048576 | tf_op jit(solution)/shard_map/reduce_line/all_to_all | solution.py:208
  65.1 10.3 %collective-permute-start.1 = (bf16[4,64,256]{2,1,0:T(8,128)(2,1)S(1)}, bf16[4,64,256]{2,1,0:T(8,128)(2,1)S(1)}, u32[]{:S(2)}, u32[]{:S(2)}) collective-permute-start(bf16[4,64,256]{2,1,0:T(8,128)(2,1)S(1)} %get-tuple-element.48), channel_id=1, source_target_pairs={{0,32},{32,64},{64,96},{96,0},{1,33},{33,65},{65,97},{97,1},{2,34}... | collective-permute-start | bytes 393224 | tf_op jit(solution)/shard_map/reduce_x/ppermute | solution.py:204
  68.2 7.2 %collective-permute-start.2 = (bf16[4,64,256]{2,1,0:T(8,128)(2,1)S(1)}, bf16[4,64,256]{2,1,0:T(8,128)(2,1)S(1)}, u32[]{:S(2)}, u32[]{:S(2)}) collective-permute-start(bf16[4,64,256]{2,1,0:T(8,128)(2,1)S(1)} %get-tuple-element.49), channel_id=1, source_target_pairs={{0,64},{32,96},{64,0},{96,32},{1,65},{33,97},{65,1},{97,33},{2,66}... | collective-permute-start | bytes 393224 | tf_op jit(solution)/shard_map/reduce_x/ppermute | solution.py:204
  72.2 6.0 %collective-permute-start.3 = (bf16[4,64,256]{2,1,0:T(8,128)(2,1)S(1)}, bf16[4,64,256]{2,1,0:T(8,128)(2,1)S(1)}, u32[]{:S(2)}, u32[]{:S(2)}) collective-permute-start(bf16[4,64,256]{2,1,0:T(8,128)(2,1)S(1)} %get-tuple-element.50), channel_id=1, source_target_pairs={{0,96},{32,0},{64,32},{96,64},{1,97},{33,1},{65,33},{97,65},{2,98}... | collective-permute-start | bytes 393224 | tf_op jit(solution)/shard_map/reduce_x/ppermute | solution.py:204
  78.3 10.1 %collective-permute-start.4 = (bf16[64,256]{1,0:T(8,128)(2,1)S(1)}, bf16[64,256]{1,0:T(8,128)(2,1)S(1)}, u32[]{:S(2)}, u32[]{:S(2)}) collective-permute-start(bf16[64,256]{1,0:T(8,128)(2,1)S(1)} %get-tuple-element.52), channel_id=1, source_target_pairs={{0,128},{128,256},{256,384},{384,0},{1,129},{129,257},{257,385},{3... | collective-permute-start | bytes 98312 | tf_op jit(solution)/shard_map/reduce_y/ppermute | solution.py:204
  81.8 6.7 %collective-permute-start.5 = (bf16[64,256]{1,0:T(8,128)(2,1)S(1)}, bf16[64,256]{1,0:T(8,128)(2,1)S(1)}, u32[]{:S(2)}, u32[]{:S(2)}) collective-permute-start(bf16[64,256]{1,0:T(8,128)(2,1)S(1)} %get-tuple-element.53), channel_id=1, source_target_pairs={{0,256},{128,384},{256,0},{384,128},{1,257},{129,385},{257,1},{385... | collective-permute-start | bytes 98312 | tf_op jit(solution)/shard_map/reduce_y/ppermute | solution.py:204
  86.4 5.0 %collective-permute-start.6 = (bf16[64,256]{1,0:T(8,128)(2,1)S(1)}, bf16[64,256]{1,0:T(8,128)(2,1)S(1)}, u32[]{:S(2)}, u32[]{:S(2)}) collective-permute-start(bf16[64,256]{1,0:T(8,128)(2,1)S(1)} %get-tuple-element.54), channel_id=1, source_target_pairs={{0,384},{128,0},{256,128},{384,256},{1,385},{129,1},{257,129},{385... | collective-permute-start | bytes 98312 | tf_op jit(solution)/shard_map/reduce_y/ppermute | solution.py:204
  92.5 38.5 %all-to-all-start.2 = ((bf16[32,64,256]{2,1,0:T(8,128)(2,1)}), bf16[32,64,256]{2,1,0:T(8,128)(2,1)S(1)}, u32[]{:S(2)}, u32[]{:S(2)}) async-start(bf16[32,64,256]{2,1,0:T(8,128)(2,1)} %get-tuple-element.55), calls=%async_computation.2 | async-start | bytes 2097152 | tf_op jit(solution)/shard_map/gather_plane/all_to_all | solution.py:208
  134.5 10.6 %collective-permute-start.7 = (bf16[16,64,256]{2,1,0:T(8,128)(2,1)S(1)}, bf16[16,64,256]{2,1,0:T(8,128)(2,1)S(1)}, u32[]{:S(2)}, u32[]{:S(2)}) collective-permute-start(bf16[16,64,256]{2,1,0:T(8,128)(2,1)S(1)} %get-tuple-element.60), channel_id=1, source_target_pairs={{0,16},{16,0},{1,17},{17,1},{2,18},{18,2},{3,19},{19,3},{4,20},{20... | collective-permute-start | bytes 1572872 | tf_op jit(solution)/shard_map/reduce_core/ppermute | solution.py:204
  145.1 32.7 %all-to-all-start.3 = ((bf16[16,64,256]{2,1,0:T(8,128)(2,1)}), bf16[16,64,256]{2,1,0:T(8,128)(2,1)S(1)}, u32[]{:S(2)}, u32[]{:S(2)}) async-start(bf16[16,64,256]{2,1,0:T(8,128)(2,1)} %get-tuple-element.61), calls=%async_computation.3 | async-start | bytes 1048576 | tf_op jit(solution)/shard_map/reduce_line/all_to_all | solution.py:208
  151.8 10.4 %collective-permute-start.8 = (bf16[4,64,256]{2,1,0:T(8,128)(2,1)S(1)}, bf16[4,64,256]{2,1,0:T(8,128)(2,1)S(1)}, u32[]{:S(2)}, u32[]{:S(2)}) collective-permute-start(bf16[4,64,256]{2,1,0:T(8,128)(2,1)S(1)} %get-tuple-element.65), channel_id=1, source_target_pairs={{0,32},{32,64},{64,96},{96,0},{1,33},{33,65},{65,97},{97,1},{2,34}... | collective-permute-start | bytes 393224 | tf_op jit(solution)/shard_map/reduce_x/ppermute | solution.py:204
  154.6 8.8 %collective-permute-start.9 = (bf16[4,64,256]{2,1,0:T(8,128)(2,1)S(1)}, bf16[4,64,256]{2,1,0:T(8,128)(2,1)S(1)}, u32[]{:S(2)}, u32[]{:S(2)}) collective-permute-start(bf16[4,64,256]{2,1,0:T(8,128)(2,1)S(1)} %get-tuple-element.66), channel_id=1, source_target_pairs={{0,64},{32,96},{64,0},{96,32},{1,65},{33,97},{65,1},{97,33},{2,66}... | collective-permute-start | bytes 393224 | tf_op jit(solution)/shard_map/reduce_x/ppermute | solution.py:204
  159.3 6.0 %collective-permute-start.10 = (bf16[4,64,256]{2,1,0:T(8,128)(2,1)S(1)}, bf16[4,64,256]{2,1,0:T(8,128)(2,1)S(1)}, u32[]{:S(2)}, u32[]{:S(2)}) collective-permute-start(bf16[4,64,256]{2,1,0:T(8,128)(2,1)S(1)} %get-tuple-element.67), channel_id=1, source_target_pairs={{0,96},{32,0},{64,32},{96,64},{1,97},{33,1},{65,33},{97,65},{2,98}... | collective-permute-start | bytes 393224 | tf_op jit(solution)/shard_map/reduce_x/ppermute | solution.py:204
  165.4 9.7 %collective-permute-start.11 = (bf16[64,256]{1,0:T(8,128)(2,1)S(1)}, bf16[64,256]{1,0:T(8,128)(2,1)S(1)}, u32[]{:S(2)}, u32[]{:S(2)}) collective-permute-start(bf16[64,256]{1,0:T(8,128)(2,1)S(1)} %get-tuple-element.69), channel_id=1, source_target_pairs={{0,128},{128,256},{256,384},{384,0},{1,129},{129,257},{257,385},{3... | collective-permute-start | bytes 98312 | tf_op jit(solution)/shard_map/reduce_y/ppermute | solution.py:204
  167.9 7.3 %collective-permute-start.12 = (bf16[64,256]{1,0:T(8,128)(2,1)S(1)}, bf16[64,256]{1,0:T(8,128)(2,1)S(1)}, u32[]{:S(2)}, u32[]{:S(2)}) collective-permute-start(bf16[64,256]{1,0:T(8,128)(2,1)S(1)} %get-tuple-element.70), channel_id=1, source_target_pairs={{0,256},{128,384},{256,0},{384,128},{1,257},{129,385},{257,1},{385... | collective-permute-start | bytes 98312 | tf_op jit(solution)/shard_map/reduce_y/ppermute | solution.py:204
  172.8 5.0 %collective-permute-start.13 = (bf16[64,256]{1,0:T(8,128)(2,1)S(1)}, bf16[64,256]{1,0:T(8,128)(2,1)S(1)}, u32[]{:S(2)}, u32[]{:S(2)}) collective-permute-start(bf16[64,256]{1,0:T(8,128)(2,1)S(1)} %get-tuple-element.71), channel_id=1, source_target_pairs={{0,384},{128,0},{256,128},{384,256},{1,385},{129,1},{257,129},{385... | collective-permute-start | bytes 98312 | tf_op jit(solution)/shard_map/reduce_y/ppermute | solution.py:204

commit v4 on v3

--- a/solution.py
+++ b/solution.py
@@ -10,30 +10,32 @@
 F32 = jnp.float32
 BF16 = jnp.bfloat16
 ROW = ("y", "x", "core")
-LINE = ("far", "near")
+LINE = ("far", "mid", "near")
 RIDGE = 1e-06
 STEP = 8
+LONG = 1 << 44
 VMEM = pl.BlockSpec(memory_space=pltpu.VMEM)
 SMEM = pl.BlockSpec(memory_space=pltpu.SMEM)
-PARAMS = pltpu.CompilerParams(vmem_limit_bytes=48 * 1024 * 1024)
+MIB = 1024 * 1024
 NT = (((1,), (1,)), ((), ()))
 NN = (((1,), (0,)), ((), ()))
 
 
-def call(kernel, outs, ins, scratch=(), flops=0, moved=0):
+def call(kernel, outs, ins, scratch=(), flops=0, moved=0, room=16):
     return pl.pallas_call(
         kernel,
         out_shape=[jax.ShapeDtypeStruct(s, d) for s, d in outs],
         in_specs=ins,
         out_specs=[VMEM] * len(outs),
         scratch_shapes=list(scratch),
-        compiler_params=PARAMS,
+        compiler_params=pltpu.CompilerParams(vmem_limit_bytes=room * MIB),
         cost_estimate=pl.CostEstimate(flops=flops, bytes_accessed=moved, transcendentals=0),
     )
 
 
 def products_kernel(
-    places, row_panel, col_panel, tiles, direct, keep, send, blocks, row_sum, col_sum, tile_sems
+    places, row_panel, col_panel, tiles, plane_keep, plane_send, keep, send,
+    blocks, row_sum, col_sum, tile_sems,
 ):
     slots = tiles.shape[0]
     copies = [pltpu.make_async_copy(tiles.at[s], blocks.at[s], tile_sems.at[s]) for s in range(slots)]
@@ -61,32 +63,32 @@
             row_sum[low] += part[:, :half]
             row_sum[high] += part[:, half:]
 
-    direct[...] = row_sum[...].astype(BF16)
     me = lax.axis_index("core")
-    for chip in range(keep.shape[0]):
-        keep[chip] = col_sum[2 * chip + me].astype(BF16)
-        send[chip] = col_sum[2 * chip + 1 - me].astype(BF16)
-
-
-def merge_x_kernel(keep, got, *pieces):
-    me = lax.axis_index("x")
-    n = len(pieces)
-    for k, piece in enumerate(pieces):
-        to = lax.rem(me + k, n)
-        for y in range(piece.shape[0]):
-            piece[y] = (keep[y * n + to].astype(F32) + got[y * n + to].astype(F32)).astype(BF16)
-
-
-def merge_y_kernel(own, *refs):
-    n = own.shape[0]
-    got, pieces = refs[: n - 1], refs[n - 1 :]
-    me = lax.axis_index("y")
-    for k, piece in enumerate(pieces):
-        to = lax.rem(me + k, n)
-        sums = own[to].astype(F32)
-        for g in got:
-            sums += g[to].astype(F32)
-        piece[...] = sums.astype(BF16)
+    for chip in range(plane_keep.shape[0]):
+        plane_keep[chip] = col_sum[2 * chip + me].astype(BF16)
+        plane_send[chip] = col_sum[2 * chip + 1 - me].astype(BF16)
+    me = lax.axis_index("near")
+    for pair in range(keep.shape[0]):
+        keep[pair] = row_sum[2 * pair + me].astype(BF16)
+        send[pair] = row_sum[2 * pair + 1 - me].astype(BF16)
+
+
+def sum_kernel(keep, got, out):
+    out[...] = (keep[...].astype(F32) + got[...].astype(F32)).astype(BF16)
+
+
+def total_kernel(pieces, out):
+    sums = pieces[0].astype(F32)
+    for k in range(1, pieces.shape[0]):
+        sums += pieces[k].astype(F32)
+    out[...] = sums
+
+
+def halve_kernel(keep, got, stay, go):
+    me = lax.axis_index("mid")
+    for pair in range(stay.shape[0]):
+        for out, at in ((stay, 2 * pair + me), (go, 2 * pair + 1 - me)):
+            out[pair] = (keep[at].astype(F32) + got[at].astype(F32)).astype(BF16)
 
 
 def spread(value, scaled, copies):
@@ -95,17 +97,15 @@
         copies[k] = value
 
 
-def add_up(arrived, own, others, weights):
-    sums = own[...].astype(F32)
-    for other in others:
-        sums += other[...].astype(F32)
-    for k in range(arrived.shape[0]):
-        sums += arrived[k].astype(F32)
+def add_up(from_line, from_plane, weights):
+    sums = from_plane[...]
+    for k in range(from_line.shape[0]):
+        sums += from_line[k].astype(F32)
     return sums * weights[...]
 
 
-def between_kernel(arrived, own, s1, s2, s3, weights, scaled, copies, gram):
-    fresh = add_up(arrived, own, (s1, s2, s3), weights)
+def between_kernel(from_line, from_plane, weights, scaled, copies, gram):
+    fresh = add_up(from_line, from_plane, weights)
     spread((fresh * weights[...]).astype(BF16), scaled, copies)
     rounded = fresh.astype(BF16)
     gram[...] = lax.dot_general(rounded, rounded, NT, preferred_element_type=F32)
@@ -151,8 +151,8 @@
     )
 
 
-def last_kernel(scale, arrived, own, s1, s2, s3, weights, first, fresh, copies):
-    rounded = add_up(arrived, own, (s1, s2, s3), weights).astype(BF16)
+def last_kernel(scale, from_line, from_plane, weights, first, fresh, copies):
+    rounded = add_up(from_line, from_plane, weights).astype(BF16)
     fresh[...] = rounded
     gram = lax.dot_general(rounded, rounded, NT, preferred_element_type=F32)
     packed = pack((gram + RIDGE * first[...]) * scale)
@@ -211,7 +211,7 @@
 def body(x_start, weights, blocks, block_rows, block_cols, live_blocks):
     k, own = x_start.shape
     slots, tile, _ = blocks.shape
-    ny, nx, nz = lax.axis_size("y"), lax.axis_size("x"), lax.axis_size("far") * lax.axis_size("near")
+    ny, nx, nz = lax.axis_size("y"), lax.axis_size("x"), lax.axis_size(LINE)
     rows = 2 * ny * nx
     vertices = float(own * rows * nz)
     gains = weights.reshape(1, own)
@@ -228,41 +228,50 @@
             row_panel = lax.all_gather(scaled, LINE, axis=0)
         col_panel, row_panel = lax.optimization_barrier((col_panel, row_panel))
         with jax.named_scope("products"):
-            direct, keep, send = call(
+            plane_keep, plane_send, keep, send = call(
                 products_kernel,
-                [((nz, k, own), BF16)] + [((ny * nx, k, own), BF16)] * 2,
+                [((ny * nx, k, own), BF16)] * 2 + [((nz // 2, k, own), BF16)] * 2,
                 [SMEM] + [VMEM] * 2 + [any_in],
                 [pltpu.VMEM((slots, tile, tile), BF16)]
                 + [pltpu.VMEM((nz, k, own), F32), pltpu.VMEM((rows, k, own), F32)]
                 + [pltpu.SemaphoreType.DMA((slots,))],
                 4 * slots * k * tile * tile,
                 blocks.size * 2,
+                48,
             )(places, row_panel, col_panel, blocks)
-        with jax.named_scope("reduce_core"):
-            got = shift(send, "core", 1, 2)
-        direct, got = lax.optimization_barrier((direct, got))
-        with jax.named_scope("reduce_line"):
-            arrived = exchange(direct, LINE)
-        with jax.named_scope("reduce_x"):
-            pieces = call(merge_x_kernel, [((ny, k, own), BF16)] * nx, [VMEM] * 2)(keep, got)
-            moved = [pieces[0]] + [shift(pieces[s], "x", s, nx) for s in range(1, nx)]
-        with jax.named_scope("reduce_y"):
-            pieces = call(merge_y_kernel, [((k, own), BF16)] * ny, [VMEM] * nx)(*moved)
-            moved = [pieces[0]] + [shift(pieces[s], "y", s, ny) for s in range(1, ny)]
+        with jax.named_scope("reduce_near"):
+            got = shift(send, "near", 1, 2)
+        with jax.named_scope("reduce_plane"):
+            plane_got = shift(plane_send, "core", 1, 2)
+            (plane,) = call(sum_kernel, [((ny * nx, k, own), BF16)], [VMEM] * 2)(
+                plane_keep, plane_got
+            )
+            (from_plane,) = call(total_kernel, [((k, own), F32)], [VMEM])(
+                exchange(plane, ("y", "x"))
+            )
+        with jax.named_scope("reduce_mid"):
+            keep, send = call(
+                halve_kernel, [((nz // 4, k, own), BF16)] * 2, [VMEM] * 2, flops=LONG
+            )(keep, got)
+            got = shift(send, "mid", 1, 2)
+        with jax.named_scope("reduce_far"):
+            got, from_plane = lax.optimization_barrier((got, from_plane))
+            line = (keep.astype(F32) + got.astype(F32)).astype(BF16)
+            from_line = exchange(line, "far")
         if sweep == 0:
             with jax.named_scope("between"):
                 scaled, copies, gram = call(
                     between_kernel,
                     [((k, own), BF16), ((rows, k, own), BF16), ((k, k), F32)],
-                    [VMEM] * 6,
-                )(arrived, *moved, gains)
+                    [VMEM] * 3,
+                )(from_line, from_plane, gains)
         else:
             with jax.named_scope("last"):
                 fresh, copies = call(
                     functools.partial(last_kernel, 1.0 / vertices),
                     [((k, own), BF16), ((rows, 1, 9 * 128), F32)],
-                    [VMEM] * 7,
-                )(arrived, *moved, gains, gram)
+                    [VMEM] * 4,
+                )(from_line, from_plane, gains, gram)
     with jax.named_scope("gram_plane"):
         part = jnp.sum(exchange(copies, ROW), axis=0)
     with jax.named_scope("gram_line"):
@@ -282,7 +291,7 @@
 
 def solution(mesh):
     cells = ROW + LINE
-    fine = Mesh(mesh.devices.reshape(4, 4, 2, 8, 2), cells)
+    fine = Mesh(mesh.devices.reshape(4, 4, 2, 4, 2, 2), cells)
     return jax.shard_map(
         body,
         mesh=fine,

time: 226 us -> 220 us (0.973)
  starting transfers between devices: 93.1 us -> 61.2 us
  blocking collectives: 102 us -> 126 us
    ppermute x14 -> x6, starting transfers between devices: 59.6 us -> 29.5 us  [shift(): lax.ppermute(value, axis, [(i, (i + step) % size) for i in range(size)])]
    all_to_all x2 -> x4, blocking collectives: 40.6 us -> 67.9 us  [exchange(): return lax.all_to_all(value, axes, split_axis=0, concat_axis=0, tiled=True)]
    all_to_all x4, waiting for transfers between devices: 0.01 us -> 15.7 us  [exchange(): return lax.all_to_all(value, axes, split_axis=0, concat_axis=0, tiled=True)]
    ppermute x14 -> x6, waiting for transfers between devices: 14.6 us -> 0.31 us  [shift(): lax.ppermute(value, axis, [(i, (i + step) % size) for i in range(size)])]
    all_gather x2, blocking collectives: 58.1 us -> 54.2 us  [body(): row_panel = lax.all_gather(scaled, LINE, axis=0)]
    pallas_call x6 -> x8, Pallas kernels: 7.22 us -> 8.71 us  [the longest x2 4.51 us: body(): call(products_kernel, [((ny * nx, k, own), BF16)] * 2 + [((nz // 2, k, ow...]
  transfers between devices with their start and end apart: 18 -> 10, of which waited for: 8 -> 4; matrix products, arithmetic and copies ran while one was open for 0% -> 0% of each run, Pallas kernels for 0% -> 2%
where the time goes in v4:
time: 220 us; the launch traced here: 219 us
  blocking collectives  126 us (57%)
  starting transfers between devices  61.2 us (28%)
  waiting for transfers between devices  16.1 us (7%)
  Pallas kernels  12.8 us (6%)
    all_to_all x4, blocking collectives, exchange(): return lax.all_to_all(value, axes, split_axis=0, concat_axis=0, tiled=True)  67.9 us
    all_gather x2, blocking collectives, body(): row_panel = lax.all_gather(scaled, LINE, axis=0)  54.2 us
    all_to_all x4, starting transfers between devices, exchange(): return lax.all_to_all(value, axes, split_axis=0, concat_axis=0, tiled=True)  31.7 us
    ppermute x6, starting transfers between devices, shift(): lax.ppermute(value, axis, [(i, (i + step) % size) for i in range(size)])  29.5 us
    all_to_all x4, waiting for transfers between devices, exchange(): return lax.all_to_all(value, axes, split_axis=0, concat_axis=0, tiled=True)  15.7 us
    pallas_call x2, Pallas kernels, body(): call(products_kernel, [((ny * nx, k, own), BF16)] * 2 + [((nz // 2, k, ow...  4.51 us
  transfers between devices with their start and end apart: 10, of which 4 were waited for; matrix products, arithmetic and copies ran while one was open for 0% of the time, Pallas kernels for 2%

profile of v4, /device:TPU:1, one launch (start us, length us, event | category | flops | bytes accessed | tf_op | source)
XLA Modules:
  0.0 219.3 jit_solution(14140908847096929435)
XLA Ops:
  0.0 0.8 multiply_convert_fusion
  0.8 1.1 broadcast_in_dim.6
  1.9 10.5 %all-to-all-start = ((bf16[32,64,256]{2,1,0:T(8,128)(2,1)}), bf16[32,64,256]{2,1,0:T(8,128)(2,1)S(1)}, u32[]{:S(2)}, u32[]{:S(2)}) async-start(bf16[32,64,256]{2,1,0:T(8,128)(2,1)} %broadcast_in_dim.6), calls=%async_computation | async-start | bytes 2097152 | tf_op jit(solution)/shard_map/gather_plane/all_to_all | solution.py:208
  13.0 0.7 pad_add_fusion.places
  13.7 0.0 copy-start.2
  13.7 30.0 %all-gather = bf16[1024,256]{1,0:T(8,128)(2,1)S(1)} all-gather(bf16[64,256]{1,0:T(8,128)(2,1)S(1)} %multiply_convert_fusion), channel_id=2, replica_groups=mesh['y'=4,'x'=4,'core'=2,'far'=4,'mid'=2,'near'=2] {'far','mid','near'}, dimensions={0}, use_global_device_ids=true | all-gather | bytes 557056 | tf_op jit(solution)/shard_map/gather_line/all_gather | solution.py:228
  43.8 0.0 all-to-all-done.col_panel
  43.8 2.3 %products.2 = (bf16[16,64,256]{2,1,0:T(8,128)(2,1)S(1)}, bf16[16,64,256]{2,1,0:T(8,128)(2,1)S(1)}, bf16[8,64,256]{2,1,0:T(8,128)(2,1)S(1)}, bf16[8,64,256]{2,1,0:T(8,128)(2,1)S(1)}) custom-call(s32[19]{0:T(128)S(1)} %pad_add_fusion.places, bf16[16,64,256]{2,1,0:T(8,128)(2,1)S(1)} %bitcast.4, bf16[32,64,256]{2,1,0:T(8,128)(2,1)S(1)} %all-to-all-done.col_panel, ...), custom_call_target="tpu_custom_call" | custom-call | flops 603979776 | bytes 4718592 | tf_op jit(solution)/shard_map/products/pallas_call | solution.py:231
  46.0 10.0 %collective-permute-start.2 = (bf16[16,64,256]{2,1,0:T(8,128)(2,1)S(1)}, bf16[16,64,256]{2,1,0:T(8,128)(2,1)S(1)}, u32[]{:S(2)}, u32[]{:S(2)}) collective-permute-start(bf16[16,64,256]{2,1,0:T(8,128)(2,1)S(1)} %get-tuple-element.37), channel_id=1, source_target_pairs={{0,16},{16,0},{1,17},{17,1},{2,18},{18,2},{3,19},{19,3},{4,20},{20... | collective-permute-start | bytes 1572872 | tf_op jit(solution)/shard_map/reduce_plane/ppermute | solution.py:204
  56.1 1.9 collective-permute-start
  58.0 0.0 collective-permute-done.2.got
  58.0 0.9 reduce_plane.4
  58.9 0.0 copy-done.2
  58.9 6.9 %all-to-all-start.1 = ((bf16[16,64,256]{2,1,0:T(8,128)(2,1)}), bf16[16,64,256]{2,1,0:T(8,128)(2,1)}, u32[]{:S(2)}, u32[]{:S(2)}) async-start(bf16[16,64,256]{2,1,0:T(8,128)(2,1)} %reduce_plane.4), calls=%async_computation.1 | async-start | bytes 1048576 | tf_op jit(solution)/shard_map/reduce_plane/all_to_all | solution.py:208
  65.8 0.1 collective-permute-done.got
  65.9 0.1 reduce_mid.2
  66.0 2.8 %collective-permute-start.1 = (bf16[4,64,256]{2,1,0:T(8,128)(2,1)S(1)}, bf16[4,64,256]{2,1,0:T(8,128)(2,1)S(1)}, u32[]{:S(2)}, u32[]{:S(2)}) collective-permute-start(bf16[4,64,256]{2,1,0:T(8,128)(2,1)S(1)} %get-tuple-element.35), channel_id=1, source_target_pairs={{0,2},{2,0},{1,3},{3,1},{4,6},{6,4},{5,7},{7,5},{8,10},{10,8},{9,1... | collective-permute-start | bytes 393224 | tf_op jit(solution)/shard_map/reduce_mid/ppermute | solution.py:204
  68.8 8.2 %all-to-all-done.1.pieces = bf16[16,64,256]{2,1,0:T(8,128)(2,1)} async-done(((bf16[16,64,256]{2,1,0:T(8,128)(2,1)}), bf16[16,64,256]{2,1,0:T(8,128)(2,1)}, u32[]{:S(2)}, u32[]{:S(2)}) %all-to-all-start.1) | async-done | bytes 524320 | tf_op jit(solution)/shard_map/reduce_plane/all_to_all | solution.py:208
  76.9 1.1 reduce_plane.5.from_plane
  78.0 0.0 collective-permute-done.1
  78.1 19.1 %all_to_all.40.from_line = bf16[4,64,256]{2,1,0:T(8,128)(2,1)S(1)} all-to-all(bf16[4,64,256]{2,1,0:T(8,128)(2,1)S(1)} %add_convert_fusion.1), channel_id=1, replica_groups=mesh['y'=4,'x'=4,'core'=2,'far'=4,'mid'=2,'near'=2] {'far'}, dimensions={0} | all-to-all | bytes 262144 | tf_op jit(solution)/shard_map/reduce_far/all_to_all | solution.py:208
  97.2 0.0 copy-done
  97.2 1.1 between.1
  98.4 7.7 %all-to-all-start.3 = ((bf16[32,64,256]{2,1,0:T(8,128)(2,1)}), bf16[32,64,256]{2,1,0:T(8,128)(2,1)S(1)}, u32[]{:S(2)}, u32[]{:S(2)}) async-start(bf16[32,64,256]{2,1,0:T(8,128)(2,1)} %get-tuple-element.40), calls=%async_computation.3 | async-start | bytes 2097152 | tf_op jit(solution)/shard_map/gather_plane/all_to_all | solution.py:208
  106.0 24.1 %all-gather.1 = bf16[1024,256]{1,0:T(8,128)(2,1)S(1)} all-gather(bf16[64,256]{1,0:T(8,128)(2,1)S(1)} %get-tuple-element.41), channel_id=3, replica_groups=mesh['y'=4,'x'=4,'core'=2,'far'=4,'mid'=2,'near'=2] {'far','mid','near'}, dimensions={0}, use_global_device_ids=true | all-gather | bytes 557056 | tf_op jit(solution)/shard_map/gather_line/all_gather | solution.py:228
  130.2 0.0 all-to-all-done.3.col_panel
  130.2 0.0 copy-done.3
  130.2 2.3 %products.3 = (bf16[16,64,256]{2,1,0:T(8,128)(2,1)S(1)}, bf16[16,64,256]{2,1,0:T(8,128)(2,1)S(1)}, bf16[8,64,256]{2,1,0:T(8,128)(2,1)S(1)}, bf16[8,64,256]{2,1,0:T(8,128)(2,1)S(1)}) custom-call(s32[19]{0:T(128)S(1)} %copy-done.3, bf16[16,64,256]{2,1,0:T(8,128)(2,1)S(1)} %bitcast.3, bf16[32,64,256]{2,1,0:T(8,128)(2,1)S(1)} %all-to-all-done.3.col_panel, ...), custom_call_target="tpu_custom_call" | custom-call | flops 603979776 | bytes 4718592 | tf_op jit(solution)/shard_map/products/pallas_call | solution.py:231
  132.4 9.8 %collective-permute-start.5 = (bf16[16,64,256]{2,1,0:T(8,128)(2,1)S(1)}, bf16[16,64,256]{2,1,0:T(8,128)(2,1)S(1)}, u32[]{:S(2)}, u32[]{:S(2)}) collective-permute-start(bf16[16,64,256]{2,1,0:T(8,128)(2,1)S(1)} %get-tuple-element.49), channel_id=1, source_target_pairs={{0,16},{16,0},{1,17},{17,1},{2,18},{18,2},{3,19},{19,3},{4,20},{20... | collective-permute-start | bytes 1572872 | tf_op jit(solution)/shard_map/reduce_plane/ppermute | solution.py:204
  142.2 1.9 collective-permute-start.3
  144.2 0.0 collective-permute-done.5.got
  144.2 0.9 reduce_plane.6
  145.1 6.7 %all-to-all-start.4 = ((bf16[16,64,256]{2,1,0:T(8,128)(2,1)}), bf16[16,64,256]{2,1,0:T(8,128)(2,1)}, u32[]{:S(2)}, u32[]{:S(2)}) async-start(bf16[16,64,256]{2,1,0:T(8,128)(2,1)} %reduce_plane.6), calls=%async_computation.4 | async-start | bytes 1048576 | tf_op jit(solution)/shard_map/reduce_plane/all_to_all | solution.py:208
  151.8 0.2 collective-permute-done.3.got
  152.1 0.1 reduce_mid.3
  152.1 3.0 %collective-permute-start.4 = (bf16[4,64,256]{2,1,0:T(8,128)(2,1)S(1)}, bf16[4,64,256]{2,1,0:T(8,128)(2,1)S(1)}, u32[]{:S(2)}, u32[]{:S(2)}) collective-permute-start(bf16[4,64,256]{2,1,0:T(8,128)(2,1)S(1)} %get-tuple-element.47), channel_id=1, source_target_pairs={{0,2},{2,0},{1,3},{3,1},{4,6},{6,4},{5,7},{7,5},{8,10},{10,8},{9,1... | collective-permute-start | bytes 393224 | tf_op jit(solution)/shard_map/reduce_mid/ppermute | solution.py:204
  155.1 7.6 %all-to-all-done.4.pieces = bf16[16,64,256]{2,1,0:T(8,128)(2,1)} async-done(((bf16[16,64,256]{2,1,0:T(8,128)(2,1)}), bf16[16,64,256]{2,1,0:T(8,128)(2,1)}, u32[]{:S(2)}, u32[]{:S(2)}) %all-to-all-start.4) | async-done | bytes 524320 | tf_op jit(solution)/shard_map/reduce_plane/all_to_all | solution.py:208
  162.7 1.1 reduce_plane.7.from_plane
  163.8 0.0 collective-permute-done.4
  163.9 18.4 %all_to_all.41.from_line = bf16[4,64,256]{2,1,0:T(8,128)(2,1)S(1)} all-to-all(bf16[4,64,256]{2,1,0:T(8,128)(2,1)S(1)} %add_convert_fusion), channel_id=1, replica_groups=mesh['y'=4,'x'=4,'core'=2,'far'=4,'mid'=2,'near'=2] {'far'}, dimensions={0} | all-to-all | bytes 262144 | tf_op jit(solution)/shard_map/reduce_far/all_to_all | solution.py:208
  182.2 0.0 copy-done.1
  182.2 0.3 last.1
  182.6 15.3 %all_to_all.42 = f32[32,1,1152]{2,1,0:T(1,128)S(1)} all-to-all(f32[32,1,1152]{2,1,0:T(1,128)S(1)} %get-tuple-element.53), channel_id=1, replica_groups=mesh['y'=4,'x'=4,'core'=2,'far'=4,'mid'=2,'near'=2] {'y','x','core'}, dimensions={0} | all-to-all | bytes 294912 | tf_op jit(solution)/shard_map/gram_plane/all_to_all | solution.py:208
  197.9 0.1 reduce_sum.18
  198.0 15.0 %all_to_all.43 = f32[16,1,1152]{2,1,0:T(1,128)S(1)} all-to-all(f32[16,1,1152]{2,1,0:T(1,128)S(1)} %broadcast_in_dim.16), channel_id=1, replica_groups=mesh['y'=4,'x'=4,'core'=2,'far'=4,'mid'=2,'near'=2] {'far','mid','near'}, dimensions={0} | all-to-all | bytes 147456 | tf_op jit(solution)/shard_map/gram_line/all_to_all | solution.py:208
  213.1 0.1 reduce_sum.19
  213.1 3.5 %all-gather.3.parts = f32[2,1,1152]{2,1,0:T(1,128)S(1)} all-gather(f32[1,1,1152]{2,1,0:T(1,128)S(1)} %reshape.16), channel_id=4, replica_groups=mesh['y'=4,'x'=4,'core'=2,'far'=4,'mid'=2,'near'=2] {'core'}, dimensions={0}, use_global_device_ids=true | all-gather | bytes 13824 | tf_op jit(solution)/shard_map/gram_pair/all_gather | solution.py:281
  216.7 2.7 %whiten.1 = bf16[64,256]{1,0:T(8,128)(2,1)} custom-call(f32[2,1,1152]{2,1,0:T(1,128)S(1)} %all-gather.3.parts, bf16[64,256]{1,0:T(8,128)(2,1)S(1)} %get-tuple-element.54.fresh), custom_call_target="tpu_custom_call" | custom-call | tf_op jit(solution)/shard_map/whiten/pallas_call | solution.py:283
  (7 shorter events, 0.1 us)
Async XLA Ops:
  1.9 41.9 %all-to-all-start = ((bf16[32,64,256]{2,1,0:T(8,128)(2,1)}), bf16[32,64,256]{2,1,0:T(8,128)(2,1)S(1)}, u32[]{:S(2)}, u32[]{:S(2)}) async-start(bf16[32,64,256]{2,1,0:T(8,128)(2,1)} %broadcast_in_dim.6), calls=%async_computation | async-start | bytes 2097152 | tf_op jit(solution)/shard_map/gather_plane/all_to_all | solution.py:208
  13.7 45.2 %copy-start.2 = (s32[19]{0:T(128)}, s32[19]{0:T(128)S(1)}, u32[]{:S(2)}) copy-start(s32[19]{0:T(128)S(1)} %pad_add_fusion.places) | copy-start | bytes 232
  46.0 12.0 %collective-permute-start.2 = (bf16[16,64,256]{2,1,0:T(8,128)(2,1)S(1)}, bf16[16,64,256]{2,1,0:T(8,128)(2,1)S(1)}, u32[]{:S(2)}, u32[]{:S(2)}) collective-permute-start(bf16[16,64,256]{2,1,0:T(8,128)(2,1)S(1)} %get-tuple-element.37), channel_id=1, source_target_pairs={{0,16},{16,0},{1,17},{17,1},{2,18},{18,2},{3,19},{19,3},{4,20},{20... | collective-permute-start | bytes 1572872 | tf_op jit(solution)/shard_map/reduce_plane/ppermute | solution.py:204
  56.1 9.8 %collective-permute-start = (bf16[8,64,256]{2,1,0:T(8,128)(2,1)S(1)}, bf16[8,64,256]{2,1,0:T(8,128)(2,1)S(1)}, u32[]{:S(2)}, u32[]{:S(2)}) collective-permute-start(bf16[8,64,256]{2,1,0:T(8,128)(2,1)S(1)} %get-tuple-element.33), channel_id=1, source_target_pairs={{0,1},{1,0},{2,3},{3,2},{4,5},{5,4},{6,7},{7,6},{8,9},{9,8},{10,11... | collective-permute-start | bytes 786440 | tf_op jit(solution)/shard_map/reduce_near/ppermute | solution.py:204
  58.9 18.0 %all-to-all-start.1 = ((bf16[16,64,256]{2,1,0:T(8,128)(2,1)}), bf16[16,64,256]{2,1,0:T(8,128)(2,1)}, u32[]{:S(2)}, u32[]{:S(2)}) async-start(bf16[16,64,256]{2,1,0:T(8,128)(2,1)} %reduce_plane.4), calls=%async_computation.1 | async-start | bytes 1048576 | tf_op jit(solution)/shard_map/reduce_plane/all_to_all | solution.py:208
  65.9 31.4 %copy-start = (f32[256]{0:T(256)S(1)}, f32[256]{0:T(256)}, u32[]{:S(2)}) copy-start(f32[256]{0:T(256)} %param.7) | copy-start | bytes 3076
  65.9 64.3 %copy-start.3 = (s32[19]{0:T(128)S(1)}, s32[19]{0:T(128)}, u32[]{:S(2)}) copy-start(s32[19]{0:T(128)} %copy-done.2) | copy-start | bytes 232
  66.0 12.1 %collective-permute-start.1 = (bf16[4,64,256]{2,1,0:T(8,128)(2,1)S(1)}, bf16[4,64,256]{2,1,0:T(8,128)(2,1)S(1)}, u32[]{:S(2)}, u32[]{:S(2)}) collective-permute-start(bf16[4,64,256]{2,1,0:T(8,128)(2,1)S(1)} %get-tuple-element.35), channel_id=1, source_target_pairs={{0,2},{2,0},{1,3},{3,1},{4,6},{6,4},{5,7},{7,5},{8,10},{10,8},{9,1... | collective-permute-start | bytes 393224 | tf_op jit(solution)/shard_map/reduce_mid/ppermute | solution.py:204
  98.4 31.8 %all-to-all-start.3 = ((bf16[32,64,256]{2,1,0:T(8,128)(2,1)}), bf16[32,64,256]{2,1,0:T(8,128)(2,1)S(1)}, u32[]{:S(2)}, u32[]{:S(2)}) async-start(bf16[32,64,256]{2,1,0:T(8,128)(2,1)} %get-tuple-element.40), calls=%async_computation.3 | async-start | bytes 2097152 | tf_op jit(solution)/shard_map/gather_plane/all_to_all | solution.py:208
  132.4 11.7 %collective-permute-start.5 = (bf16[16,64,256]{2,1,0:T(8,128)(2,1)S(1)}, bf16[16,64,256]{2,1,0:T(8,128)(2,1)S(1)}, u32[]{:S(2)}, u32[]{:S(2)}) collective-permute-start(bf16[16,64,256]{2,1,0:T(8,128)(2,1)S(1)} %get-tuple-element.49), channel_id=1, source_target_pairs={{0,16},{16,0},{1,17},{17,1},{2,18},{18,2},{3,19},{19,3},{4,20},{20... | collective-permute-start | bytes 1572872 | tf_op jit(solution)/shard_map/reduce_plane/ppermute | solution.py:204
  142.2 9.8 %collective-permute-start.3 = (bf16[8,64,256]{2,1,0:T(8,128)(2,1)S(1)}, bf16[8,64,256]{2,1,0:T(8,128)(2,1)S(1)}, u32[]{:S(2)}, u32[]{:S(2)}) collective-permute-start(bf16[8,64,256]{2,1,0:T(8,128)(2,1)S(1)} %get-tuple-element.45), channel_id=1, source_target_pairs={{0,1},{1,0},{2,3},{3,2},{4,5},{5,4},{6,7},{7,6},{8,9},{9,8},{10,11... | collective-permute-start | bytes 786440 | tf_op jit(solution)/shard_map/reduce_near/ppermute | solution.py:204
  145.1 17.6 %all-to-all-start.4 = ((bf16[16,64,256]{2,1,0:T(8,128)(2,1)}), bf16[16,64,256]{2,1,0:T(8,128)(2,1)}, u32[]{:S(2)}, u32[]{:S(2)}) async-start(bf16[16,64,256]{2,1,0:T(8,128)(2,1)} %reduce_plane.6), calls=%async_computation.4 | async-start | bytes 1048576 | tf_op jit(solution)/shard_map/reduce_plane/all_to_all | solution.py:208
  152.1 30.2 %copy-start.1 = (f32[256]{0:T(256)S(1)}, f32[256]{0:T(256)}, u32[]{:S(2)}) copy-start(f32[256]{0:T(256)} %param.7) | copy-start | bytes 3076
  152.1 11.7 %collective-permute-start.4 = (bf16[4,64,256]{2,1,0:T(8,128)(2,1)S(1)}, bf16[4,64,256]{2,1,0:T(8,128)(2,1)S(1)}, u32[]{:S(2)}, u32[]{:S(2)}) collective-permute-start(bf16[4,64,256]{2,1,0:T(8,128)(2,1)S(1)} %get-tuple-element.47), channel_id=1, source_target_pairs={{0,2},{2,0},{1,3},{3,1},{4,6},{6,4},{5,7},{7,5},{8,10},{10,8},{9,1... | collective-permute-start | bytes 393224 | tf_op jit(solution)/shard_map/reduce_mid/ppermute | solution.py:204

commit v5 on v4

--- a/solution.py
+++ b/solution.py
@@ -34,7 +34,7 @@
 
 
 def products_kernel(
-    places, row_panel, col_panel, tiles, plane_keep, plane_send, keep, send,
+    places, row_panel, near_panel, other_panel, tiles, plane_keep, plane_send, keep, send,
     blocks, row_sum, col_sum, tile_sems,
 ):
     slots = tiles.shape[0]
@@ -44,6 +44,7 @@
     row_sum[...] = jnp.zeros_like(row_sum)
     col_sum[...] = jnp.zeros_like(col_sum)
     half = row_panel.shape[2]
+    first = lax.axis_index("core") == 0
     for s, copy in enumerate(copies):
 
         @pl.when(s < places[2 * slots])
@@ -57,9 +58,12 @@
             ) + lax.dot_general(row_panel[high], blocks[s, half:, :], NN, preferred_element_type=F32)
             col_sum[left] += part[:, :half]
             col_sum[right] += part[:, half:]
+            own, other = near_panel[c], other_panel[c]
             part = lax.dot_general(
-                col_panel[left], blocks[s, :, :half], NT, preferred_element_type=F32
-            ) + lax.dot_general(col_panel[right], blocks[s, :, half:], NT, preferred_element_type=F32)
+                jnp.where(first, own, other), blocks[s, :, :half], NT, preferred_element_type=F32
+            ) + lax.dot_general(
+                jnp.where(first, other, own), blocks[s, :, half:], NT, preferred_element_type=F32
+            )
             row_sum[low] += part[:, :half]
             row_sum[high] += part[:, half:]
 
@@ -219,26 +223,27 @@
     any_in = pl.BlockSpec(memory_space=pltpu.HBM)
     places = jnp.concatenate([block_rows, block_cols, live_blocks])
     scaled = (x_start.astype(F32) * gains).astype(BF16)
-    copies = jnp.broadcast_to(scaled[None], (rows, k, own))
+    copies = jnp.broadcast_to(scaled[None], (nz, k, own))
     gram = None
     for sweep in range(2):
+        with jax.named_scope("gather_line"):
+            row_panel = exchange(copies, LINE)
         with jax.named_scope("gather_plane"):
-            col_panel = exchange(copies, ROW)
-        with jax.named_scope("gather_line"):
-            row_panel = lax.all_gather(scaled, LINE, axis=0)
-        col_panel, row_panel = lax.optimization_barrier((col_panel, row_panel))
+            near_panel = lax.all_gather(scaled, ("y", "x"), axis=0)
+        with jax.named_scope("gather_core"):
+            other_panel = shift(near_panel, "core", 1, 2)
         with jax.named_scope("products"):
             plane_keep, plane_send, keep, send = call(
                 products_kernel,
                 [((ny * nx, k, own), BF16)] * 2 + [((nz // 2, k, own), BF16)] * 2,
-                [SMEM] + [VMEM] * 2 + [any_in],
+                [SMEM] + [VMEM] * 3 + [any_in],
                 [pltpu.VMEM((slots, tile, tile), BF16)]
                 + [pltpu.VMEM((nz, k, own), F32), pltpu.VMEM((rows, k, own), F32)]
                 + [pltpu.SemaphoreType.DMA((slots,))],
                 4 * slots * k * tile * tile,
                 blocks.size * 2,
                 48,
-            )(places, row_panel, col_panel, blocks)
+            )(places, row_panel, near_panel, other_panel, blocks)
         with jax.named_scope("reduce_near"):
             got = shift(send, "near", 1, 2)
         with jax.named_scope("reduce_plane"):
@@ -262,7 +267,7 @@
             with jax.named_scope("between"):
                 scaled, copies, gram = call(
                     between_kernel,
-                    [((k, own), BF16), ((rows, k, own), BF16), ((k, k), F32)],
+                    [((k, own), BF16), ((nz, k, own), BF16), ((k, k), F32)],
                     [VMEM] * 3,
                 )(from_line, from_plane, gains)
         else:

time: 220 us -> 221 us (level)
  starting transfers between devices: 61.2 us -> 71.7 us
  blocking collectives: 126 us -> 116 us
  waiting for transfers between devices: 16.1 us -> 13.8 us
    all_gather x2, blocking collectives: 54.2 us -> 39.1 us  [body(): near_panel = lax.all_gather(scaled, ('y', 'x'), axis=0)]
    ppermute x6 -> x8, starting transfers between devices: 29.5 us -> 37.2 us  [shift(): lax.ppermute(value, axis, [(i, (i + step) % size) for i in range(size)])]
    all_to_all x4, blocking collectives: 67.9 us -> 73.6 us  [exchange(): return lax.all_to_all(value, axes, split_axis=0, concat_axis=0, tiled=True)]
    all_to_all x4, waiting for transfers between devices: 15.7 us -> 11.7 us  [exchange(): return lax.all_to_all(value, axes, split_axis=0, concat_axis=0, tiled=True)]
    all_to_all x4, starting transfers between devices: 31.7 us -> 34.5 us  [exchange(): return lax.all_to_all(value, axes, split_axis=0, concat_axis=0, tiled=True)]
  transfers between devices with their start and end apart: 10 -> 12, of which waited for: 4 -> 5; matrix products, arithmetic and copies ran while one was open for 0% -> 0% of each run, Pallas kernels for 2% -> 2%
where the time goes in v5:
time: 221 us; the launch traced here: 220 us
  blocking collectives  116 us (52%)
  starting transfers between devices  71.7 us (32%)
  Pallas kernels  14 us (6%)
  waiting for transfers between devices  13.8 us (6%)
    all_to_all x4, blocking collectives, exchange(): return lax.all_to_all(value, axes, split_axis=0, concat_axis=0, tiled=True)  73.6 us
    all_gather x2, blocking collectives, body(): near_panel = lax.all_gather(scaled, ('y', 'x'), axis=0)  39.1 us
    ppermute x8, starting transfers between devices, shift(): lax.ppermute(value, axis, [(i, (i + step) % size) for i in range(size)])  37.2 us
    all_to_all x4, starting transfers between devices, exchange(): return lax.all_to_all(value, axes, split_axis=0, concat_axis=0, tiled=True)  34.5 us
    all_to_all x4, waiting for transfers between devices, exchange(): return lax.all_to_all(value, axes, split_axis=0, concat_axis=0, tiled=True)  11.7 us
    pallas_call x2, Pallas kernels, body(): call(products_kernel, [((ny * nx, k, own), BF16)] * 2 + [((nz // 2, k, ow...  5.93 us
  transfers between devices with their start and end apart: 12, of which 5 were waited for; matrix products, arithmetic and copies ran while one was open for 0% of the time, Pallas kernels for 2%

profile of v5, /device:TPU:1, one launch (start us, length us, event | category | flops | bytes accessed | tf_op | source)
XLA Modules:
  0.0 219.9 jit_solution(14986896300787301500)
XLA Ops:
  0.0 0.8 multiply_convert_fusion
  0.8 0.8 broadcast_in_dim.6
  1.6 15.7 %all-to-all-start = ((bf16[16,64,256]{2,1,0:T(8,128)(2,1)}), bf16[16,64,256]{2,1,0:T(8,128)(2,1)S(1)}, u32[]{:S(2)}, u32[]{:S(2)}) async-start(bf16[16,64,256]{2,1,0:T(8,128)(2,1)} %broadcast_in_dim.6), calls=%async_computation | async-start | bytes 1048576 | tf_op jit(solution)/shard_map/gather_line/all_to_all | solution.py:212
  17.4 20.2 %all-gather = bf16[1024,256]{1,0:T(8,128)(2,1)S(1)} all-gather(bf16[64,256]{1,0:T(8,128)(2,1)S(1)} %multiply_convert_fusion), channel_id=2, replica_groups=mesh['y'=4,'x'=4,'core'=2,'far'=4,'mid'=2,'near'=2] {'y','x'}, dimensions={0}, use_global_device_ids=true | all-gather | bytes 557056 | tf_op jit(solution)/shard_map/gather_plane/all_gather | solution.py:232
  37.6 7.0 %collective-permute-start = (bf16[16,64,256]{2,1,0:T(8,128)(2,1)S(1)}, bf16[16,64,256]{2,1,0:T(8,128)(2,1)S(1)}, u32[]{:S(2)}, u32[]{:S(2)}) collective-permute-start(bf16[16,64,256]{2,1,0:T(8,128)(2,1)S(1)} %bitcast.3), channel_id=1, source_target_pairs={{0,16},{16,0},{1,17},{17,1},{2,18},{18,2},{3,19},{19,3},{4,20},{20... | collective-permute-start | bytes 1572872 | tf_op jit(solution)/shard_map/gather_core/ppermute | solution.py:208
  45.3 0.7 pad_add_fusion.places
  46.0 0.1 collective-permute-done.other_panel
  46.1 0.0 all-to-all-done.row_panel
  46.1 3.0 %products.2 = (bf16[16,64,256]{2,1,0:T(8,128)(2,1)S(1)}, bf16[16,64,256]{2,1,0:T(8,128)(2,1)S(1)}, bf16[8,64,256]{2,1,0:T(8,128)(2,1)S(1)}, bf16[8,64,256]{2,1,0:T(8,128)(2,1)S(1)}) custom-call(s32[19]{0:T(128)S(1)} %pad_add_fusion.places, bf16[16,64,256]{2,1,0:T(8,128)(2,1)S(1)} %all-to-all-done.row_panel, bf16[16,64,256]{2,1,0:T(8,128)(2,1)S(1)} %bitcast.4, ...), custom_call_target="tpu_custom_call" | custom-call | flops 603979776 | bytes 4718592 | tf_op jit(solution)/shard_map/products/pallas_call | solution.py:236
  49.1 3.2 %collective-permute-start.3 = (bf16[16,64,256]{2,1,0:T(8,128)(2,1)S(1)}, bf16[16,64,256]{2,1,0:T(8,128)(2,1)S(1)}, u32[]{:S(2)}, u32[]{:S(2)}) collective-permute-start(bf16[16,64,256]{2,1,0:T(8,128)(2,1)S(1)} %get-tuple-element.31), channel_id=1, source_target_pairs={{0,16},{16,0},{1,17},{17,1},{2,18},{18,2},{3,19},{19,3},{4,20},{20... | collective-permute-start | bytes 1572872 | tf_op jit(solution)/shard_map/reduce_plane/ppermute | solution.py:208
  52.3 2.8 %collective-permute-start.1 = (bf16[8,64,256]{2,1,0:T(8,128)(2,1)S(1)}, bf16[8,64,256]{2,1,0:T(8,128)(2,1)S(1)}, u32[]{:S(2)}, u32[]{:S(2)}) collective-permute-start(bf16[8,64,256]{2,1,0:T(8,128)(2,1)S(1)} %get-tuple-element.27), channel_id=1, source_target_pairs={{0,1},{1,0},{2,3},{3,2},{4,5},{5,4},{6,7},{7,6},{8,9},{9,8},{10,11... | collective-permute-start | bytes 786440 | tf_op jit(solution)/shard_map/reduce_near/ppermute | solution.py:208
  55.1 0.0 collective-permute-done.3.got
  55.1 0.9 reduce_plane.4
  56.1 8.1 %all-to-all-start.1 = ((bf16[16,64,256]{2,1,0:T(8,128)(2,1)}), bf16[16,64,256]{2,1,0:T(8,128)(2,1)}, u32[]{:S(2)}, u32[]{:S(2)}) async-start(bf16[16,64,256]{2,1,0:T(8,128)(2,1)} %reduce_plane.4), calls=%async_computation.1 | async-start | bytes 1048576 | tf_op jit(solution)/shard_map/reduce_plane/all_to_all | solution.py:212
  64.2 0.0 copy-start
  64.2 0.1 reduce_mid.2
  64.3 3.5 %collective-permute-start.2 = (bf16[4,64,256]{2,1,0:T(8,128)(2,1)S(1)}, bf16[4,64,256]{2,1,0:T(8,128)(2,1)S(1)}, u32[]{:S(2)}, u32[]{:S(2)}) collective-permute-start(bf16[4,64,256]{2,1,0:T(8,128)(2,1)S(1)} %get-tuple-element.29), channel_id=1, source_target_pairs={{0,2},{2,0},{1,3},{3,1},{4,6},{6,4},{5,7},{7,5},{8,10},{10,8},{9,1... | collective-permute-start | bytes 393224 | tf_op jit(solution)/shard_map/reduce_mid/ppermute | solution.py:208
  67.9 7.2 %all-to-all-done.1.pieces = bf16[16,64,256]{2,1,0:T(8,128)(2,1)} async-done(((bf16[16,64,256]{2,1,0:T(8,128)(2,1)}), bf16[16,64,256]{2,1,0:T(8,128)(2,1)}, u32[]{:S(2)}, u32[]{:S(2)}) %all-to-all-start.1) | async-done | bytes 524320 | tf_op jit(solution)/shard_map/reduce_plane/all_to_all | solution.py:212
  75.1 1.1 reduce_plane.5.from_plane
  76.2 0.0 collective-permute-done.2
  76.2 19.8 %all_to_all.40.from_line = bf16[4,64,256]{2,1,0:T(8,128)(2,1)S(1)} all-to-all(bf16[4,64,256]{2,1,0:T(8,128)(2,1)S(1)} %add_convert_fusion.1), channel_id=1, replica_groups=mesh['y'=4,'x'=4,'core'=2,'far'=4,'mid'=2,'near'=2] {'far'}, dimensions={0} | all-to-all | bytes 262144 | tf_op jit(solution)/shard_map/reduce_far/all_to_all | solution.py:212
  96.1 0.9 between.1
  96.9 5.0 %all-to-all-start.3 = ((bf16[16,64,256]{2,1,0:T(8,128)(2,1)}), bf16[16,64,256]{2,1,0:T(8,128)(2,1)S(1)}, u32[]{:S(2)}, u32[]{:S(2)}) async-start(bf16[16,64,256]{2,1,0:T(8,128)(2,1)} %get-tuple-element.34), calls=%async_computation.3 | async-start | bytes 1048576 | tf_op jit(solution)/shard_map/gather_line/all_to_all | solution.py:212
  102.0 18.9 %all-gather.1 = bf16[1024,256]{1,0:T(8,128)(2,1)S(1)} all-gather(bf16[64,256]{1,0:T(8,128)(2,1)S(1)} %get-tuple-element.35), channel_id=3, replica_groups=mesh['y'=4,'x'=4,'core'=2,'far'=4,'mid'=2,'near'=2] {'y','x'}, dimensions={0}, use_global_device_ids=true | all-gather | bytes 557056 | tf_op jit(solution)/shard_map/gather_plane/all_gather | solution.py:232
  120.8 8.3 %collective-permute-start.4 = (bf16[16,64,256]{2,1,0:T(8,128)(2,1)S(1)}, bf16[16,64,256]{2,1,0:T(8,128)(2,1)S(1)}, u32[]{:S(2)}, u32[]{:S(2)}) collective-permute-start(bf16[16,64,256]{2,1,0:T(8,128)(2,1)S(1)} %bitcast.5), channel_id=1, source_target_pairs={{0,16},{16,0},{1,17},{17,1},{2,18},{18,2},{3,19},{19,3},{4,20},{20... | collective-permute-start | bytes 1572872 | tf_op jit(solution)/shard_map/gather_core/ppermute | solution.py:208
  129.2 1.5 collective-permute-done.4.other_panel
  130.7 0.7 copy-done.3
  131.3 3.0 %products.3 = (bf16[16,64,256]{2,1,0:T(8,128)(2,1)S(1)}, bf16[16,64,256]{2,1,0:T(8,128)(2,1)S(1)}, bf16[8,64,256]{2,1,0:T(8,128)(2,1)S(1)}, bf16[8,64,256]{2,1,0:T(8,128)(2,1)S(1)}) custom-call(s32[19]{0:T(128)S(1)} %copy-done.3, bf16[16,64,256]{2,1,0:T(8,128)(2,1)S(1)} %all-to-all-done.3.row_panel, bf16[16,64,256]{2,1,0:T(8,128)(2,1)S(1)} %bitcast.6, ...), custom_call_target="tpu_custom_call" | custom-call | flops 603979776 | bytes 4718592 | tf_op jit(solution)/shard_map/products/pallas_call | solution.py:236
  134.3 2.4 %collective-permute-start.7 = (bf16[16,64,256]{2,1,0:T(8,128)(2,1)S(1)}, bf16[16,64,256]{2,1,0:T(8,128)(2,1)S(1)}, u32[]{:S(2)}, u32[]{:S(2)}) collective-permute-start(bf16[16,64,256]{2,1,0:T(8,128)(2,1)S(1)} %get-tuple-element.41), channel_id=1, source_target_pairs={{0,16},{16,0},{1,17},{17,1},{2,18},{18,2},{3,19},{19,3},{4,20},{20... | collective-permute-start | bytes 1572872 | tf_op jit(solution)/shard_map/reduce_plane/ppermute | solution.py:208
  136.7 3.6 %collective-permute-start.5 = (bf16[8,64,256]{2,1,0:T(8,128)(2,1)S(1)}, bf16[8,64,256]{2,1,0:T(8,128)(2,1)S(1)}, u32[]{:S(2)}, u32[]{:S(2)}) collective-permute-start(bf16[8,64,256]{2,1,0:T(8,128)(2,1)S(1)} %get-tuple-element.37), channel_id=1, source_target_pairs={{0,1},{1,0},{2,3},{3,2},{4,5},{5,4},{6,7},{7,6},{8,9},{9,8},{10,11... | collective-permute-start | bytes 786440 | tf_op jit(solution)/shard_map/reduce_near/ppermute | solution.py:208
  140.3 0.0 collective-permute-done.7.got
  140.3 0.9 reduce_plane.6
  141.2 5.6 %all-to-all-start.4 = ((bf16[16,64,256]{2,1,0:T(8,128)(2,1)}), bf16[16,64,256]{2,1,0:T(8,128)(2,1)}, u32[]{:S(2)}, u32[]{:S(2)}) async-start(bf16[16,64,256]{2,1,0:T(8,128)(2,1)} %reduce_plane.6), calls=%async_computation.4 | async-start | bytes 1048576 | tf_op jit(solution)/shard_map/reduce_plane/all_to_all | solution.py:212
  146.9 0.0 collective-permute-done.5.got
  146.9 0.0 copy-start.1
  146.9 0.1 reduce_mid.3
  147.0 6.3 %collective-permute-start.6 = (bf16[4,64,256]{2,1,0:T(8,128)(2,1)S(1)}, bf16[4,64,256]{2,1,0:T(8,128)(2,1)S(1)}, u32[]{:S(2)}, u32[]{:S(2)}) collective-permute-start(bf16[4,64,256]{2,1,0:T(8,128)(2,1)S(1)} %get-tuple-element.39), channel_id=1, source_target_pairs={{0,2},{2,0},{1,3},{3,1},{4,6},{6,4},{5,7},{7,5},{8,10},{10,8},{9,1... | collective-permute-start | bytes 393224 | tf_op jit(solution)/shard_map/reduce_mid/ppermute | solution.py:208
  153.3 4.5 %all-to-all-done.4.pieces = bf16[16,64,256]{2,1,0:T(8,128)(2,1)} async-done(((bf16[16,64,256]{2,1,0:T(8,128)(2,1)}), bf16[16,64,256]{2,1,0:T(8,128)(2,1)}, u32[]{:S(2)}, u32[]{:S(2)}) %all-to-all-start.4) | async-done | bytes 524320 | tf_op jit(solution)/shard_map/reduce_plane/all_to_all | solution.py:212
  157.7 1.1 reduce_plane.7.from_plane
  158.9 0.5 collective-permute-done.6
  159.4 21.6 %all_to_all.41.from_line = bf16[4,64,256]{2,1,0:T(8,128)(2,1)S(1)} all-to-all(bf16[4,64,256]{2,1,0:T(8,128)(2,1)S(1)} %add_convert_fusion), channel_id=1, replica_groups=mesh['y'=4,'x'=4,'core'=2,'far'=4,'mid'=2,'near'=2] {'far'}, dimensions={0} | all-to-all | bytes 262144 | tf_op jit(solution)/shard_map/reduce_far/all_to_all | solution.py:212
  181.1 0.3 last.1
  181.4 16.1 %all_to_all.42 = f32[32,1,1152]{2,1,0:T(1,128)S(1)} all-to-all(f32[32,1,1152]{2,1,0:T(1,128)S(1)} %get-tuple-element.45), channel_id=1, replica_groups=mesh['y'=4,'x'=4,'core'=2,'far'=4,'mid'=2,'near'=2] {'y','x','core'}, dimensions={0} | all-to-all | bytes 294912 | tf_op jit(solution)/shard_map/gram_plane/all_to_all | solution.py:212
  197.5 0.1 reduce_sum.18
  197.7 16.0 %all_to_all.43 = f32[16,1,1152]{2,1,0:T(1,128)S(1)} all-to-all(f32[16,1,1152]{2,1,0:T(1,128)S(1)} %broadcast_in_dim.16), channel_id=1, replica_groups=mesh['y'=4,'x'=4,'core'=2,'far'=4,'mid'=2,'near'=2] {'far','mid','near'}, dimensions={0} | all-to-all | bytes 147456 | tf_op jit(solution)/shard_map/gram_line/all_to_all | solution.py:212
  213.7 0.1 reduce_sum.19
  213.7 3.5 %all-gather.3.parts = f32[2,1,1152]{2,1,0:T(1,128)S(1)} all-gather(f32[1,1,1152]{2,1,0:T(1,128)S(1)} %reshape.16), channel_id=4, replica_groups=mesh['y'=4,'x'=4,'core'=2,'far'=4,'mid'=2,'near'=2] {'core'}, dimensions={0}, use_global_device_ids=true | all-gather | bytes 13824 | tf_op jit(solution)/shard_map/gram_pair/all_gather | solution.py:286
  217.2 2.7 %whiten.1 = bf16[64,256]{1,0:T(8,128)(2,1)} custom-call(f32[2,1,1152]{2,1,0:T(1,128)S(1)} %all-gather.3.parts, bf16[64,256]{1,0:T(8,128)(2,1)S(1)} %get-tuple-element.46.fresh), custom_call_target="tpu_custom_call" | custom-call | tf_op jit(solution)/shard_map/whiten/pallas_call | solution.py:288
  (11 shorter events, 0.1 us)
Async XLA Ops:
  1.6 44.5 %all-to-all-start = ((bf16[16,64,256]{2,1,0:T(8,128)(2,1)}), bf16[16,64,256]{2,1,0:T(8,128)(2,1)S(1)}, u32[]{:S(2)}, u32[]{:S(2)}) async-start(bf16[16,64,256]{2,1,0:T(8,128)(2,1)} %broadcast_in_dim.6), calls=%async_computation | async-start | bytes 1048576 | tf_op jit(solution)/shard_map/gather_line/all_to_all | solution.py:212
  37.6 8.6 %collective-permute-start = (bf16[16,64,256]{2,1,0:T(8,128)(2,1)S(1)}, bf16[16,64,256]{2,1,0:T(8,128)(2,1)S(1)}, u32[]{:S(2)}, u32[]{:S(2)}) collective-permute-start(bf16[16,64,256]{2,1,0:T(8,128)(2,1)S(1)} %bitcast.3), channel_id=1, source_target_pairs={{0,16},{16,0},{1,17},{17,1},{2,18},{18,2},{3,19},{19,3},{4,20},{20... | collective-permute-start | bytes 1572872 | tf_op jit(solution)/shard_map/gather_core/ppermute | solution.py:208
  46.0 18.3 %copy-start.2 = (s32[19]{0:T(128)}, s32[19]{0:T(128)S(1)}, u32[]{:S(2)}) copy-start(s32[19]{0:T(128)S(1)} %pad_add_fusion.places) | copy-start | bytes 232
  49.1 6.0 %collective-permute-start.3 = (bf16[16,64,256]{2,1,0:T(8,128)(2,1)S(1)}, bf16[16,64,256]{2,1,0:T(8,128)(2,1)S(1)}, u32[]{:S(2)}, u32[]{:S(2)}) collective-permute-start(bf16[16,64,256]{2,1,0:T(8,128)(2,1)S(1)} %get-tuple-element.31), channel_id=1, source_target_pairs={{0,16},{16,0},{1,17},{17,1},{2,18},{18,2},{3,19},{19,3},{4,20},{20... | collective-permute-start | bytes 1572872 | tf_op jit(solution)/shard_map/reduce_plane/ppermute | solution.py:208
  52.3 11.9 %collective-permute-start.1 = (bf16[8,64,256]{2,1,0:T(8,128)(2,1)S(1)}, bf16[8,64,256]{2,1,0:T(8,128)(2,1)S(1)}, u32[]{:S(2)}, u32[]{:S(2)}) collective-permute-start(bf16[8,64,256]{2,1,0:T(8,128)(2,1)S(1)} %get-tuple-element.27), channel_id=1, source_target_pairs={{0,1},{1,0},{2,3},{3,2},{4,5},{5,4},{6,7},{7,6},{8,9},{9,8},{10,11... | collective-permute-start | bytes 786440 | tf_op jit(solution)/shard_map/reduce_near/ppermute | solution.py:208
  56.1 19.0 %all-to-all-start.1 = ((bf16[16,64,256]{2,1,0:T(8,128)(2,1)}), bf16[16,64,256]{2,1,0:T(8,128)(2,1)}, u32[]{:S(2)}, u32[]{:S(2)}) async-start(bf16[16,64,256]{2,1,0:T(8,128)(2,1)} %reduce_plane.4), calls=%async_computation.1 | async-start | bytes 1048576 | tf_op jit(solution)/shard_map/reduce_plane/all_to_all | solution.py:212
  64.2 31.9 %copy-start = (f32[256]{0:T(256)S(1)}, f32[256]{0:T(256)}, u32[]{:S(2)}) copy-start(f32[256]{0:T(256)} %param.7) | copy-start | bytes 3076
  64.3 11.9 %collective-permute-start.2 = (bf16[4,64,256]{2,1,0:T(8,128)(2,1)S(1)}, bf16[4,64,256]{2,1,0:T(8,128)(2,1)S(1)}, u32[]{:S(2)}, u32[]{:S(2)}) collective-permute-start(bf16[4,64,256]{2,1,0:T(8,128)(2,1)S(1)} %get-tuple-element.29), channel_id=1, source_target_pairs={{0,2},{2,0},{1,3},{3,1},{4,6},{6,4},{5,7},{7,5},{8,10},{10,8},{9,1... | collective-permute-start | bytes 393224 | tf_op jit(solution)/shard_map/reduce_mid/ppermute | solution.py:208
  96.9 33.8 %all-to-all-start.3 = ((bf16[16,64,256]{2,1,0:T(8,128)(2,1)}), bf16[16,64,256]{2,1,0:T(8,128)(2,1)S(1)}, u32[]{:S(2)}, u32[]{:S(2)}) async-start(bf16[16,64,256]{2,1,0:T(8,128)(2,1)} %get-tuple-element.34), calls=%async_computation.3 | async-start | bytes 1048576 | tf_op jit(solution)/shard_map/gather_line/all_to_all | solution.py:212
  120.8 9.9 %collective-permute-start.4 = (bf16[16,64,256]{2,1,0:T(8,128)(2,1)S(1)}, bf16[16,64,256]{2,1,0:T(8,128)(2,1)S(1)}, u32[]{:S(2)}, u32[]{:S(2)}) collective-permute-start(bf16[16,64,256]{2,1,0:T(8,128)(2,1)S(1)} %bitcast.5), channel_id=1, source_target_pairs={{0,16},{16,0},{1,17},{17,1},{2,18},{18,2},{3,19},{19,3},{4,20},{20... | collective-permute-start | bytes 1572872 | tf_op jit(solution)/shard_map/gather_core/ppermute | solution.py:208
  130.7 0.7 copy-start.3
  134.3 6.0 %collective-permute-start.7 = (bf16[16,64,256]{2,1,0:T(8,128)(2,1)S(1)}, bf16[16,64,256]{2,1,0:T(8,128)(2,1)S(1)}, u32[]{:S(2)}, u32[]{:S(2)}) collective-permute-start(bf16[16,64,256]{2,1,0:T(8,128)(2,1)S(1)} %get-tuple-element.41), channel_id=1, source_target_pairs={{0,16},{16,0},{1,17},{17,1},{2,18},{18,2},{3,19},{19,3},{4,20},{20... | collective-permute-start | bytes 1572872 | tf_op jit(solution)/shard_map/reduce_plane/ppermute | solution.py:208
  136.7 10.2 %collective-permute-start.5 = (bf16[8,64,256]{2,1,0:T(8,128)(2,1)S(1)}, bf16[8,64,256]{2,1,0:T(8,128)(2,1)S(1)}, u32[]{:S(2)}, u32[]{:S(2)}) collective-permute-start(bf16[8,64,256]{2,1,0:T(8,128)(2,1)S(1)} %get-tuple-element.37), channel_id=1, source_target_pairs={{0,1},{1,0},{2,3},{3,2},{4,5},{5,4},{6,7},{7,6},{8,9},{9,8},{10,11... | collective-permute-start | bytes 786440 | tf_op jit(solution)/shard_map/reduce_near/ppermute | solution.py:208
  141.2 16.5 %all-to-all-start.4 = ((bf16[16,64,256]{2,1,0:T(8,128)(2,1)}), bf16[16,64,256]{2,1,0:T(8,128)(2,1)}, u32[]{:S(2)}, u32[]{:S(2)}) async-start(bf16[16,64,256]{2,1,0:T(8,128)(2,1)} %reduce_plane.6), calls=%async_computation.4 | async-start | bytes 1048576 | tf_op jit(solution)/shard_map/reduce_plane/all_to_all | solution.py:212
  146.9 34.2 %copy-start.1 = (f32[256]{0:T(256)S(1)}, f32[256]{0:T(256)}, u32[]{:S(2)}) copy-start(f32[256]{0:T(256)} %param.7) | copy-start | bytes 3076
  147.0 12.4 %collective-permute-start.6 = (bf16[4,64,256]{2,1,0:T(8,128)(2,1)S(1)}, bf16[4,64,256]{2,1,0:T(8,128)(2,1)S(1)}, u32[]{:S(2)}, u32[]{:S(2)}) collective-permute-start(bf16[4,64,256]{2,1,0:T(8,128)(2,1)S(1)} %get-tuple-element.39), channel_id=1, source_target_pairs={{0,2},{2,0},{1,3},{3,1},{4,6},{6,4},{5,7},{7,5},{8,10},{10,8},{9,1... | collective-permute-start | bytes 393224 | tf_op jit(solution)/shard_map/reduce_mid/ppermute | solution.py:208

commit v6 on v5

--- a/solution.py
+++ b/solution.py
@@ -221,7 +221,6 @@
     gains = weights.reshape(1, own)
     any_spec = pl.BlockSpec(memory_space=pl.ANY)
     any_in = pl.BlockSpec(memory_space=pltpu.HBM)
-    places = jnp.concatenate([block_rows, block_cols, live_blocks])
     scaled = (x_start.astype(F32) * gains).astype(BF16)
     copies = jnp.broadcast_to(scaled[None], (nz, k, own))
     gram = None
@@ -232,6 +231,9 @@
             near_panel = lax.all_gather(scaled, ("y", "x"), axis=0)
         with jax.named_scope("gather_core"):
             other_panel = shift(near_panel, "core", 1, 2)
+        with jax.named_scope("places"):
+            tile_rows, near_panel = lax.optimization_barrier((block_rows, near_panel))
+            places = jnp.concatenate([tile_rows, block_cols, live_blocks])
         with jax.named_scope("products"):
             plane_keep, plane_send, keep, send = call(
                 products_kernel,

time: 221 us -> 219 us (level)
    all_to_all x4, starting transfers between devices: 34.5 us -> 31.3 us  [exchange(): return lax.all_to_all(value, axes, split_axis=0, concat_axis=0, tiled=True)]
    all_to_all x4, blocking collectives: 73.6 us -> 76.4 us  [exchange(): return lax.all_to_all(value, axes, split_axis=0, concat_axis=0, tiled=True)]
where the time goes in v6:
time: 219 us
  blocking collectives  117 us (53%)
  starting transfers between devices  69.7 us (32%)
  waiting for transfers between devices  15.2 us (7%)
  Pallas kernels  12.5 us (6%)
    all_to_all x4, blocking collectives, exchange(): return lax.all_to_all(value, axes, split_axis=0, concat_axis=0, tiled=True)  76.4 us
    ppermute x8, starting transfers between devices, shift(): lax.ppermute(value, axis, [(i, (i + step) % size) for i in range(size)])  38.4 us
    all_gather x2, blocking collectives, body(): near_panel = lax.all_gather(scaled, ('y', 'x'), axis=0)  37.6 us
    all_to_all x4, starting transfers between devices, exchange(): return lax.all_to_all(value, axes, split_axis=0, concat_axis=0, tiled=True)  31.3 us
    all_to_all x4, waiting for transfers between devices, exchange(): return lax.all_to_all(value, axes, split_axis=0, concat_axis=0, tiled=True)  12.2 us
    pallas_call x2, Pallas kernels, body(): call(products_kernel, [((ny * nx, k, own), BF16)] * 2 + [((nz // 2, k, ow...  4.49 us
  transfers between devices with their start and end apart: 12, of which 5 were waited for; matrix products, arithmetic and copies ran while one was open for 0% of the time, Pallas kernels for 2%

profile of v6, /device:TPU:1, one launch (start us, length us, event | category | flops | bytes accessed | tf_op | source)
XLA Modules:
  0.0 218.6 jit_solution(15197055955996176713)
XLA Ops:
  0.0 0.8 multiply_convert_fusion
  0.8 0.8 broadcast_in_dim.4
  1.6 15.7 %all-to-all-start = ((bf16[16,64,256]{2,1,0:T(8,128)(2,1)}), bf16[16,64,256]{2,1,0:T(8,128)(2,1)S(1)}, u32[]{:S(2)}, u32[]{:S(2)}) async-start(bf16[16,64,256]{2,1,0:T(8,128)(2,1)} %broadcast_in_dim.4), calls=%async_computation | async-start | bytes 1048576 | tf_op jit(solution)/shard_map/gather_line/all_to_all | solution.py:212
  17.4 20.2 %all-gather = bf16[1024,256]{1,0:T(8,128)(2,1)S(1)} all-gather(bf16[64,256]{1,0:T(8,128)(2,1)S(1)} %multiply_convert_fusion), channel_id=2, replica_groups=mesh['y'=4,'x'=4,'core'=2,'far'=4,'mid'=2,'near'=2] {'y','x'}, dimensions={0}, use_global_device_ids=true | all-gather | bytes 557056 | tf_op jit(solution)/shard_map/gather_plane/all_gather | solution.py:231
  37.6 7.0 %collective-permute-start = (bf16[16,64,256]{2,1,0:T(8,128)(2,1)S(1)}, bf16[16,64,256]{2,1,0:T(8,128)(2,1)S(1)}, u32[]{:S(2)}, u32[]{:S(2)}) collective-permute-start(bf16[16,64,256]{2,1,0:T(8,128)(2,1)S(1)} %bitcast.3), channel_id=1, source_target_pairs={{0,16},{16,0},{1,17},{17,1},{2,18},{18,2},{3,19},{19,3},{4,20},{20... | collective-permute-start | bytes 1572872 | tf_op jit(solution)/shard_map/gather_core/ppermute | solution.py:208
  45.3 0.7 add_add_fusion.places
  46.0 0.1 collective-permute-done.other_panel
  46.1 0.0 all-to-all-done.row_panel
  46.1 2.2 %products.2 = (bf16[16,64,256]{2,1,0:T(8,128)(2,1)S(1)}, bf16[16,64,256]{2,1,0:T(8,128)(2,1)S(1)}, bf16[8,64,256]{2,1,0:T(8,128)(2,1)S(1)}, bf16[8,64,256]{2,1,0:T(8,128)(2,1)S(1)}) custom-call(s32[19]{0:T(128)S(1)} %add_add_fusion.places, bf16[16,64,256]{2,1,0:T(8,128)(2,1)S(1)} %all-to-all-done.row_panel, bf16[16,64,256]{2,1,0:T(8,128)(2,1)S(1)} %bitcast.4, ...), custom_call_target="tpu_custom_call" | custom-call | flops 603979776 | bytes 4718592 | tf_op jit(solution)/shard_map/products/pallas_call | solution.py:238
  48.4 3.5 %collective-permute-start.3 = (bf16[16,64,256]{2,1,0:T(8,128)(2,1)S(1)}, bf16[16,64,256]{2,1,0:T(8,128)(2,1)S(1)}, u32[]{:S(2)}, u32[]{:S(2)}) collective-permute-start(bf16[16,64,256]{2,1,0:T(8,128)(2,1)S(1)} %get-tuple-element.37), channel_id=1, source_target_pairs={{0,16},{16,0},{1,17},{17,1},{2,18},{18,2},{3,19},{19,3},{4,20},{20... | collective-permute-start | bytes 1572872 | tf_op jit(solution)/shard_map/reduce_plane/ppermute | solution.py:208
  51.9 3.2 %collective-permute-start.1 = (bf16[8,64,256]{2,1,0:T(8,128)(2,1)S(1)}, bf16[8,64,256]{2,1,0:T(8,128)(2,1)S(1)}, u32[]{:S(2)}, u32[]{:S(2)}) collective-permute-start(bf16[8,64,256]{2,1,0:T(8,128)(2,1)S(1)} %get-tuple-element.33), channel_id=1, source_target_pairs={{0,1},{1,0},{2,3},{3,2},{4,5},{5,4},{6,7},{7,6},{8,9},{9,8},{10,11... | collective-permute-start | bytes 786440 | tf_op jit(solution)/shard_map/reduce_near/ppermute | solution.py:208
  55.1 0.0 collective-permute-done.3.got
  55.1 0.9 reduce_plane.4
  56.1 6.8 %all-to-all-start.1 = ((bf16[16,64,256]{2,1,0:T(8,128)(2,1)}), bf16[16,64,256]{2,1,0:T(8,128)(2,1)}, u32[]{:S(2)}, u32[]{:S(2)}) async-start(bf16[16,64,256]{2,1,0:T(8,128)(2,1)} %reduce_plane.4), calls=%async_computation.1 | async-start | bytes 1048576 | tf_op jit(solution)/shard_map/reduce_plane/all_to_all | solution.py:212
  62.9 0.0 collective-permute-done.1.got
  62.9 0.0 copy-start
  62.9 0.0 copy-start.2
  62.9 0.0 copy-start.3
  62.9 0.1 reduce_mid.2
  63.0 4.6 %collective-permute-start.2 = (bf16[4,64,256]{2,1,0:T(8,128)(2,1)S(1)}, bf16[4,64,256]{2,1,0:T(8,128)(2,1)S(1)}, u32[]{:S(2)}, u32[]{:S(2)}) collective-permute-start(bf16[4,64,256]{2,1,0:T(8,128)(2,1)S(1)} %get-tuple-element.35), channel_id=1, source_target_pairs={{0,2},{2,0},{1,3},{3,1},{4,6},{6,4},{5,7},{7,5},{8,10},{10,8},{9,1... | collective-permute-start | bytes 393224 | tf_op jit(solution)/shard_map/reduce_mid/ppermute | solution.py:208
  67.6 6.1 %all-to-all-done.1.pieces = bf16[16,64,256]{2,1,0:T(8,128)(2,1)} async-done(((bf16[16,64,256]{2,1,0:T(8,128)(2,1)}), bf16[16,64,256]{2,1,0:T(8,128)(2,1)}, u32[]{:S(2)}, u32[]{:S(2)}) %all-to-all-start.1) | async-done | bytes 524320 | tf_op jit(solution)/shard_map/reduce_plane/all_to_all | solution.py:212
  73.7 1.1 reduce_plane.5.from_plane
  74.8 0.0 collective-permute-done.2
  74.9 22.0 %all_to_all.40.from_line = bf16[4,64,256]{2,1,0:T(8,128)(2,1)S(1)} all-to-all(bf16[4,64,256]{2,1,0:T(8,128)(2,1)S(1)} %add_convert_fusion.1), channel_id=1, replica_groups=mesh['y'=4,'x'=4,'core'=2,'far'=4,'mid'=2,'near'=2] {'far'}, dimensions={0} | all-to-all | bytes 262144 | tf_op jit(solution)/shard_map/reduce_far/all_to_all | solution.py:212
  96.9 0.9 between.1
  97.8 4.5 %all-to-all-start.3 = ((bf16[16,64,256]{2,1,0:T(8,128)(2,1)}), bf16[16,64,256]{2,1,0:T(8,128)(2,1)S(1)}, u32[]{:S(2)}, u32[]{:S(2)}) async-start(bf16[16,64,256]{2,1,0:T(8,128)(2,1)} %get-tuple-element.42), calls=%async_computation.3 | async-start | bytes 1048576 | tf_op jit(solution)/shard_map/gather_line/all_to_all | solution.py:212
  102.3 17.4 %all-gather.1 = bf16[1024,256]{1,0:T(8,128)(2,1)S(1)} all-gather(bf16[64,256]{1,0:T(8,128)(2,1)S(1)} %get-tuple-element.40), channel_id=3, replica_groups=mesh['y'=4,'x'=4,'core'=2,'far'=4,'mid'=2,'near'=2] {'y','x'}, dimensions={0}, use_global_device_ids=true | all-gather | bytes 557056 | tf_op jit(solution)/shard_map/gather_plane/all_gather | solution.py:231
  119.7 9.3 %collective-permute-start.4 = (bf16[16,64,256]{2,1,0:T(8,128)(2,1)S(1)}, bf16[16,64,256]{2,1,0:T(8,128)(2,1)S(1)}, u32[]{:S(2)}, u32[]{:S(2)}) collective-permute-start(bf16[16,64,256]{2,1,0:T(8,128)(2,1)S(1)} %bitcast.5), channel_id=1, source_target_pairs={{0,16},{16,0},{1,17},{17,1},{2,18},{18,2},{3,19},{19,3},{4,20},{20... | collective-permute-start | bytes 1572872 | tf_op jit(solution)/shard_map/gather_core/ppermute | solution.py:208
  129.0 0.1 add_add_fusion.1.places
  129.1 1.4 collective-permute-done.4.other_panel
  130.5 2.2 %products.3 = (bf16[16,64,256]{2,1,0:T(8,128)(2,1)S(1)}, bf16[16,64,256]{2,1,0:T(8,128)(2,1)S(1)}, bf16[8,64,256]{2,1,0:T(8,128)(2,1)S(1)}, bf16[8,64,256]{2,1,0:T(8,128)(2,1)S(1)}) custom-call(s32[19]{0:T(128)S(1)} %add_add_fusion.1.places, bf16[16,64,256]{2,1,0:T(8,128)(2,1)S(1)} %all-to-all-done.3.row_panel, bf16[16,64,256]{2,1,0:T(8,128)(2,1)S(1)} %bitcast.6, ...), custom_call_target="tpu_custom_call" | custom-call | flops 603979776 | bytes 4718592 | tf_op jit(solution)/shard_map/products/pallas_call | solution.py:238
  132.8 3.4 %collective-permute-start.7 = (bf16[16,64,256]{2,1,0:T(8,128)(2,1)S(1)}, bf16[16,64,256]{2,1,0:T(8,128)(2,1)S(1)}, u32[]{:S(2)}, u32[]{:S(2)}) collective-permute-start(bf16[16,64,256]{2,1,0:T(8,128)(2,1)S(1)} %get-tuple-element.49), channel_id=1, source_target_pairs={{0,16},{16,0},{1,17},{17,1},{2,18},{18,2},{3,19},{19,3},{4,20},{20... | collective-permute-start | bytes 1572872 | tf_op jit(solution)/shard_map/reduce_plane/ppermute | solution.py:208
  136.2 4.2 %collective-permute-start.5 = (bf16[8,64,256]{2,1,0:T(8,128)(2,1)S(1)}, bf16[8,64,256]{2,1,0:T(8,128)(2,1)S(1)}, u32[]{:S(2)}, u32[]{:S(2)}) collective-permute-start(bf16[8,64,256]{2,1,0:T(8,128)(2,1)S(1)} %get-tuple-element.45), channel_id=1, source_target_pairs={{0,1},{1,0},{2,3},{3,2},{4,5},{5,4},{6,7},{7,6},{8,9},{9,8},{10,11... | collective-permute-start | bytes 786440 | tf_op jit(solution)/shard_map/reduce_near/ppermute | solution.py:208
  140.4 0.9 reduce_plane.6
  141.3 4.2 %all-to-all-start.4 = ((bf16[16,64,256]{2,1,0:T(8,128)(2,1)}), bf16[16,64,256]{2,1,0:T(8,128)(2,1)}, u32[]{:S(2)}, u32[]{:S(2)}) async-start(bf16[16,64,256]{2,1,0:T(8,128)(2,1)} %reduce_plane.6), calls=%async_computation.4 | async-start | bytes 1048576 | tf_op jit(solution)/shard_map/reduce_plane/all_to_all | solution.py:212
  145.5 1.5 collective-permute-done.5.got
  147.0 0.1 reduce_mid.3
  147.1 3.2 %collective-permute-start.6 = (bf16[4,64,256]{2,1,0:T(8,128)(2,1)S(1)}, bf16[4,64,256]{2,1,0:T(8,128)(2,1)S(1)}, u32[]{:S(2)}, u32[]{:S(2)}) collective-permute-start(bf16[4,64,256]{2,1,0:T(8,128)(2,1)S(1)} %get-tuple-element.47), channel_id=1, source_target_pairs={{0,2},{2,0},{1,3},{3,1},{4,6},{6,4},{5,7},{7,5},{8,10},{10,8},{9,1... | collective-permute-start | bytes 393224 | tf_op jit(solution)/shard_map/reduce_mid/ppermute | solution.py:208
  150.3 6.1 %all-to-all-done.4.pieces = bf16[16,64,256]{2,1,0:T(8,128)(2,1)} async-done(((bf16[16,64,256]{2,1,0:T(8,128)(2,1)}), bf16[16,64,256]{2,1,0:T(8,128)(2,1)}, u32[]{:S(2)}, u32[]{:S(2)}) %all-to-all-start.4) | async-done | bytes 524320 | tf_op jit(solution)/shard_map/reduce_plane/all_to_all | solution.py:212
  156.4 1.1 reduce_plane.7.from_plane
  157.5 22.3 %all_to_all.41.from_line = bf16[4,64,256]{2,1,0:T(8,128)(2,1)S(1)} all-to-all(bf16[4,64,256]{2,1,0:T(8,128)(2,1)S(1)} %add_convert_fusion), channel_id=1, replica_groups=mesh['y'=4,'x'=4,'core'=2,'far'=4,'mid'=2,'near'=2] {'far'}, dimensions={0} | all-to-all | bytes 262144 | tf_op jit(solution)/shard_map/reduce_far/all_to_all | solution.py:212
  179.8 0.3 last.1
  180.2 16.2 %all_to_all.42 = f32[32,1,1152]{2,1,0:T(1,128)S(1)} all-to-all(f32[32,1,1152]{2,1,0:T(1,128)S(1)} %get-tuple-element.53), channel_id=1, replica_groups=mesh['y'=4,'x'=4,'core'=2,'far'=4,'mid'=2,'near'=2] {'y','x','core'}, dimensions={0} | all-to-all | bytes 294912 | tf_op jit(solution)/shard_map/gram_plane/all_to_all | solution.py:212
  196.3 0.1 reduce_sum.18
  196.5 15.9 %all_to_all.43 = f32[16,1,1152]{2,1,0:T(1,128)S(1)} all-to-all(f32[16,1,1152]{2,1,0:T(1,128)S(1)} %broadcast_in_dim.5), channel_id=1, replica_groups=mesh['y'=4,'x'=4,'core'=2,'far'=4,'mid'=2,'near'=2] {'far','mid','near'}, dimensions={0} | all-to-all | bytes 147456 | tf_op jit(solution)/shard_map/gram_line/all_to_all | solution.py:212
  212.3 0.1 reduce_sum.19
  212.4 3.5 %all-gather.3.parts = f32[2,1,1152]{2,1,0:T(1,128)S(1)} all-gather(f32[1,1,1152]{2,1,0:T(1,128)S(1)} %reshape.16), channel_id=4, replica_groups=mesh['y'=4,'x'=4,'core'=2,'far'=4,'mid'=2,'near'=2] {'core'}, dimensions={0}, use_global_device_ids=true | all-gather | bytes 13824 | tf_op jit(solution)/shard_map/gram_pair/all_gather | solution.py:288
  215.9 2.7 %whiten.1 = bf16[64,256]{1,0:T(8,128)(2,1)} custom-call(f32[2,1,1152]{2,1,0:T(1,128)S(1)} %all-gather.3.parts, bf16[64,256]{1,0:T(8,128)(2,1)S(1)} %get-tuple-element.54.fresh), custom_call_target="tpu_custom_call" | custom-call | tf_op jit(solution)/shard_map/whiten/pallas_call | solution.py:290
  (12 shorter events, 0.1 us)
Async XLA Ops:
  1.6 44.5 %all-to-all-start = ((bf16[16,64,256]{2,1,0:T(8,128)(2,1)}), bf16[16,64,256]{2,1,0:T(8,128)(2,1)S(1)}, u32[]{:S(2)}, u32[]{:S(2)}) async-start(bf16[16,64,256]{2,1,0:T(8,128)(2,1)} %broadcast_in_dim.4), calls=%async_computation | async-start | bytes 1048576 | tf_op jit(solution)/shard_map/gather_line/all_to_all | solution.py:212
  37.6 8.6 %collective-permute-start = (bf16[16,64,256]{2,1,0:T(8,128)(2,1)S(1)}, bf16[16,64,256]{2,1,0:T(8,128)(2,1)S(1)}, u32[]{:S(2)}, u32[]{:S(2)}) collective-permute-start(bf16[16,64,256]{2,1,0:T(8,128)(2,1)S(1)} %bitcast.3), channel_id=1, source_target_pairs={{0,16},{16,0},{1,17},{17,1},{2,18},{18,2},{3,19},{19,3},{4,20},{20... | collective-permute-start | bytes 1572872 | tf_op jit(solution)/shard_map/gather_core/ppermute | solution.py:208
  48.4 6.7 %collective-permute-start.3 = (bf16[16,64,256]{2,1,0:T(8,128)(2,1)S(1)}, bf16[16,64,256]{2,1,0:T(8,128)(2,1)S(1)}, u32[]{:S(2)}, u32[]{:S(2)}) collective-permute-start(bf16[16,64,256]{2,1,0:T(8,128)(2,1)S(1)} %get-tuple-element.37), channel_id=1, source_target_pairs={{0,16},{16,0},{1,17},{17,1},{2,18},{18,2},{3,19},{19,3},{4,20},{20... | collective-permute-start | bytes 1572872 | tf_op jit(solution)/shard_map/reduce_plane/ppermute | solution.py:208
  51.9 10.9 %collective-permute-start.1 = (bf16[8,64,256]{2,1,0:T(8,128)(2,1)S(1)}, bf16[8,64,256]{2,1,0:T(8,128)(2,1)S(1)}, u32[]{:S(2)}, u32[]{:S(2)}) collective-permute-start(bf16[8,64,256]{2,1,0:T(8,128)(2,1)S(1)} %get-tuple-element.33), channel_id=1, source_target_pairs={{0,1},{1,0},{2,3},{3,2},{4,5},{5,4},{6,7},{7,6},{8,9},{9,8},{10,11... | collective-permute-start | bytes 786440 | tf_op jit(solution)/shard_map/reduce_near/ppermute | solution.py:208
  56.1 17.6 %all-to-all-start.1 = ((bf16[16,64,256]{2,1,0:T(8,128)(2,1)}), bf16[16,64,256]{2,1,0:T(8,128)(2,1)}, u32[]{:S(2)}, u32[]{:S(2)}) async-start(bf16[16,64,256]{2,1,0:T(8,128)(2,1)} %reduce_plane.4), calls=%async_computation.1 | async-start | bytes 1048576 | tf_op jit(solution)/shard_map/reduce_plane/all_to_all | solution.py:212
  62.9 34.0 %copy-start = (f32[256]{0:T(256)S(1)}, f32[256]{0:T(256)}, u32[]{:S(2)}) copy-start(f32[256]{0:T(256)} %param.7) | copy-start | bytes 3076
  62.9 66.1 %copy-start.2 = (s32[9]{0:T(128)S(1)}, s32[9]{0:T(128)}, u32[]{:S(2)}) copy-start(s32[9]{0:T(128)} %param.9) | copy-start | bytes 112
  62.9 66.1 %copy-start.3 = (s32[9]{0:T(128)S(1)}, s32[9]{0:T(128)}, u32[]{:S(2)}) copy-start(s32[9]{0:T(128)} %param.10) | copy-start | bytes 112
  63.0 11.9 %collective-permute-start.2 = (bf16[4,64,256]{2,1,0:T(8,128)(2,1)S(1)}, bf16[4,64,256]{2,1,0:T(8,128)(2,1)S(1)}, u32[]{:S(2)}, u32[]{:S(2)}) collective-permute-start(bf16[4,64,256]{2,1,0:T(8,128)(2,1)S(1)} %get-tuple-element.35), channel_id=1, source_target_pairs={{0,2},{2,0},{1,3},{3,1},{4,6},{6,4},{5,7},{7,5},{8,10},{10,8},{9,1... | collective-permute-start | bytes 393224 | tf_op jit(solution)/shard_map/reduce_mid/ppermute | solution.py:208
  97.8 32.7 %all-to-all-start.3 = ((bf16[16,64,256]{2,1,0:T(8,128)(2,1)}), bf16[16,64,256]{2,1,0:T(8,128)(2,1)S(1)}, u32[]{:S(2)}, u32[]{:S(2)}) async-start(bf16[16,64,256]{2,1,0:T(8,128)(2,1)} %get-tuple-element.42), calls=%async_computation.3 | async-start | bytes 1048576 | tf_op jit(solution)/shard_map/gather_line/all_to_all | solution.py:212
  119.7 10.8 %collective-permute-start.4 = (bf16[16,64,256]{2,1,0:T(8,128)(2,1)S(1)}, bf16[16,64,256]{2,1,0:T(8,128)(2,1)S(1)}, u32[]{:S(2)}, u32[]{:S(2)}) collective-permute-start(bf16[16,64,256]{2,1,0:T(8,128)(2,1)S(1)} %bitcast.5), channel_id=1, source_target_pairs={{0,16},{16,0},{1,17},{17,1},{2,18},{18,2},{3,19},{19,3},{4,20},{20... | collective-permute-start | bytes 1572872 | tf_op jit(solution)/shard_map/gather_core/ppermute | solution.py:208
  132.8 7.6 %collective-permute-start.7 = (bf16[16,64,256]{2,1,0:T(8,128)(2,1)S(1)}, bf16[16,64,256]{2,1,0:T(8,128)(2,1)S(1)}, u32[]{:S(2)}, u32[]{:S(2)}) collective-permute-start(bf16[16,64,256]{2,1,0:T(8,128)(2,1)S(1)} %get-tuple-element.49), channel_id=1, source_target_pairs={{0,16},{16,0},{1,17},{17,1},{2,18},{18,2},{3,19},{19,3},{4,20},{20... | collective-permute-start | bytes 1572872 | tf_op jit(solution)/shard_map/reduce_plane/ppermute | solution.py:208
  136.2 10.8 %collective-permute-start.5 = (bf16[8,64,256]{2,1,0:T(8,128)(2,1)S(1)}, bf16[8,64,256]{2,1,0:T(8,128)(2,1)S(1)}, u32[]{:S(2)}, u32[]{:S(2)}) collective-permute-start(bf16[8,64,256]{2,1,0:T(8,128)(2,1)S(1)} %get-tuple-element.45), channel_id=1, source_target_pairs={{0,1},{1,0},{2,3},{3,2},{4,5},{5,4},{6,7},{7,6},{8,9},{9,8},{10,11... | collective-permute-start | bytes 786440 | tf_op jit(solution)/shard_map/reduce_near/ppermute | solution.py:208
  141.3 15.1 %all-to-all-start.4 = ((bf16[16,64,256]{2,1,0:T(8,128)(2,1)}), bf16[16,64,256]{2,1,0:T(8,128)(2,1)}, u32[]{:S(2)}, u32[]{:S(2)}) async-start(bf16[16,64,256]{2,1,0:T(8,128)(2,1)} %reduce_plane.6), calls=%async_computation.4 | async-start | bytes 1048576 | tf_op jit(solution)/shard_map/reduce_plane/all_to_all | solution.py:212
  147.0 32.8 %copy-start.1 = (f32[256]{0:T(256)S(1)}, f32[256]{0:T(256)}, u32[]{:S(2)}) copy-start(f32[256]{0:T(256)} %param.7) | copy-start | bytes 3076
  147.1 10.4 %collective-permute-start.6 = (bf16[4,64,256]{2,1,0:T(8,128)(2,1)S(1)}, bf16[4,64,256]{2,1,0:T(8,128)(2,1)S(1)}, u32[]{:S(2)}, u32[]{:S(2)}) collective-permute-start(bf16[4,64,256]{2,1,0:T(8,128)(2,1)S(1)} %get-tuple-element.47), channel_id=1, source_target_pairs={{0,2},{2,0},{1,3},{3,1},{4,6},{6,4},{5,7},{7,5},{8,10},{10,8},{9,1... | collective-permute-start | bytes 393224 | tf_op jit(solution)/shard_map/reduce_mid/ppermute | solution.py:208

commit v7 on v6

--- a/solution.py
+++ b/solution.py
@@ -13,6 +13,7 @@
 LINE = ("far", "mid", "near")
 RIDGE = 1e-06
 STEP = 8
+GROUP = 3
 LONG = 1 << 44
 VMEM = pl.BlockSpec(memory_space=pltpu.VMEM)
 SMEM = pl.BlockSpec(memory_space=pltpu.SMEM)
@@ -39,33 +40,50 @@
 ):
     slots = tiles.shape[0]
     copies = [pltpu.make_async_copy(tiles.at[s], blocks.at[s], tile_sems.at[s]) for s in range(slots)]
+    live = places[2 * slots]
     for s, copy in enumerate(copies):
-        pl.when(s < places[2 * slots])(copy.start)
+        pl.when(s - s % GROUP < live)(copy.start)
     row_sum[...] = jnp.zeros_like(row_sum)
     col_sum[...] = jnp.zeros_like(col_sum)
     half = row_panel.shape[2]
-    first = lax.axis_index("core") == 0
-    for s, copy in enumerate(copies):
-
-        @pl.when(s < places[2 * slots])
+    first_core = lax.axis_index("core") == 0
+    row_spare, col_spare = row_panel.shape[0], 2 * near_panel.shape[0]
+    for start in range(0, slots, GROUP):
+
+        @pl.when(start < live)
         def _():
-            copy.wait()
-            r, c = places[s], places[slots + s]
-            low, high = 2 * r, 2 * r + 1
-            left, right = 2 * c, 2 * c + 1
-            part = lax.dot_general(
-                row_panel[low], blocks[s, :half, :], NN, preferred_element_type=F32
-            ) + lax.dot_general(row_panel[high], blocks[s, half:, :], NN, preferred_element_type=F32)
-            col_sum[left] += part[:, :half]
-            col_sum[right] += part[:, half:]
-            own, other = near_panel[c], other_panel[c]
-            part = lax.dot_general(
-                jnp.where(first, own, other), blocks[s, :, :half], NT, preferred_element_type=F32
-            ) + lax.dot_general(
-                jnp.where(first, other, own), blocks[s, :, half:], NT, preferred_element_type=F32
-            )
-            row_sum[low] += part[:, :half]
-            row_sum[high] += part[:, half:]
+            group = range(start, min(start + GROUP, slots))
+            for s in group:
+                copies[s].wait()
+            terms = []
+            for s in group:
+                r, c = places[s], places[slots + s]
+                low, high = 2 * r, 2 * r + 1
+                down = lax.dot_general(
+                    row_panel[low], blocks[s, :half, :], NN, preferred_element_type=F32
+                ) + lax.dot_general(
+                    row_panel[high], blocks[s, half:, :], NN, preferred_element_type=F32
+                )
+                own, other = near_panel[c], other_panel[c]
+                across = lax.dot_general(
+                    jnp.where(first_core, own, other),
+                    blocks[s, :, :half],
+                    NT,
+                    preferred_element_type=F32,
+                ) + lax.dot_general(
+                    jnp.where(first_core, other, own),
+                    blocks[s, :, half:],
+                    NT,
+                    preferred_element_type=F32,
+                )
+                rows = [jnp.where(s < live, at, row_spare) for at in (low, high)]
+                cols = [jnp.where(s < live, at, col_spare) for at in (2 * c, 2 * c + 1)]
+                terms.append((rows, cols, down, across))
+            for rows, cols, down, across in terms:
+                col_sum[cols[0]] += down[:, :half]
+                col_sum[cols[1]] += down[:, half:]
+                row_sum[rows[0]] += across[:, :half]
+                row_sum[rows[1]] += across[:, half:]
 
     me = lax.axis_index("core")
     for chip in range(plane_keep.shape[0]):
@@ -240,7 +258,7 @@
                 [((ny * nx, k, own), BF16)] * 2 + [((nz // 2, k, own), BF16)] * 2,
                 [SMEM] + [VMEM] * 3 + [any_in],
                 [pltpu.VMEM((slots, tile, tile), BF16)]
-                + [pltpu.VMEM((nz, k, own), F32), pltpu.VMEM((rows, k, own), F32)]
+                + [pltpu.VMEM((nz + 1, k, own), F32), pltpu.VMEM((rows + 1, k, own), F32)]
                 + [pltpu.SemaphoreType.DMA((slots,))],
                 4 * slots * k * tile * tile,
                 blocks.size * 2,

time: 219 us -> 220 us (level)
  no operation moved by 1% of the time
where the time goes in v7:
time: 220 us; the launch traced here: 219 us
  blocking collectives  118 us (54%)
  starting transfers between devices  69.5 us (32%)
  Pallas kernels  14.1 us (6%)
  waiting for transfers between devices  13.9 us (6%)
    all_to_all x4, blocking collectives, exchange(): return lax.all_to_all(value, axes, split_axis=0, concat_axis=0, tiled=True)  76.6 us
    all_gather x2, blocking collectives, body(): near_panel = lax.all_gather(scaled, ('y', 'x'), axis=0)  38.2 us
    ppermute x8, starting transfers between devices, shift(): lax.ppermute(value, axis, [(i, (i + step) % size) for i in range(size)])  38.1 us
    all_to_all x4, starting transfers between devices, exchange(): return lax.all_to_all(value, axes, split_axis=0, concat_axis=0, tiled=True)  31.4 us
    all_to_all x4, waiting for transfers between devices, exchange(): return lax.all_to_all(value, axes, split_axis=0, concat_axis=0, tiled=True)  11 us
    pallas_call x2, Pallas kernels, body(): call(products_kernel, [((ny * nx, k, own), BF16)] * 2 + [((nz // 2, k, ow...  6.01 us
  transfers between devices with their start and end apart: 12, of which 5 were waited for; matrix products, arithmetic and copies ran while one was open for 0% of the time, Pallas kernels for 2%

profile of v7, /device:TPU:1, one launch (start us, length us, event | category | flops | bytes accessed | tf_op | source)
XLA Modules:
  0.0 219.5 jit_solution(17344350236686707998)
XLA Ops:
  0.0 0.8 multiply_convert_fusion
  0.8 0.8 broadcast_in_dim.4
  1.6 15.7 %all-to-all-start = ((bf16[16,64,256]{2,1,0:T(8,128)(2,1)}), bf16[16,64,256]{2,1,0:T(8,128)(2,1)S(1)}, u32[]{:S(2)}, u32[]{:S(2)}) async-start(bf16[16,64,256]{2,1,0:T(8,128)(2,1)} %broadcast_in_dim.4), calls=%async_computation | async-start | bytes 1048576 | tf_op jit(solution)/shard_map/gather_line/all_to_all | solution.py:230
  17.4 20.2 %all-gather = bf16[1024,256]{1,0:T(8,128)(2,1)S(1)} all-gather(bf16[64,256]{1,0:T(8,128)(2,1)S(1)} %multiply_convert_fusion), channel_id=2, replica_groups=mesh['y'=4,'x'=4,'core'=2,'far'=4,'mid'=2,'near'=2] {'y','x'}, dimensions={0}, use_global_device_ids=true | all-gather | bytes 557056 | tf_op jit(solution)/shard_map/gather_plane/all_gather | solution.py:249
  37.6 7.0 %collective-permute-start = (bf16[16,64,256]{2,1,0:T(8,128)(2,1)S(1)}, bf16[16,64,256]{2,1,0:T(8,128)(2,1)S(1)}, u32[]{:S(2)}, u32[]{:S(2)}) collective-permute-start(bf16[16,64,256]{2,1,0:T(8,128)(2,1)S(1)} %bitcast.3), channel_id=1, source_target_pairs={{0,16},{16,0},{1,17},{17,1},{2,18},{18,2},{3,19},{19,3},{4,20},{20... | collective-permute-start | bytes 1572872 | tf_op jit(solution)/shard_map/gather_core/ppermute | solution.py:226
  45.3 0.7 add_add_fusion.places
  46.0 0.1 collective-permute-done.other_panel
  46.1 0.0 all-to-all-done.row_panel
  46.1 3.0 %products.2 = (bf16[16,64,256]{2,1,0:T(8,128)(2,1)S(1)}, bf16[16,64,256]{2,1,0:T(8,128)(2,1)S(1)}, bf16[8,64,256]{2,1,0:T(8,128)(2,1)S(1)}, bf16[8,64,256]{2,1,0:T(8,128)(2,1)S(1)}) custom-call(s32[19]{0:T(128)S(1)} %add_add_fusion.places, bf16[16,64,256]{2,1,0:T(8,128)(2,1)S(1)} %all-to-all-done.row_panel, bf16[16,64,256]{2,1,0:T(8,128)(2,1)S(1)} %bitcast.4, ...), custom_call_target="tpu_custom_call" | custom-call | flops 603979776 | bytes 4718592 | tf_op jit(solution)/shard_map/products/pallas_call | solution.py:256
  49.2 4.1 %collective-permute-start.3 = (bf16[16,64,256]{2,1,0:T(8,128)(2,1)S(1)}, bf16[16,64,256]{2,1,0:T(8,128)(2,1)S(1)}, u32[]{:S(2)}, u32[]{:S(2)}) collective-permute-start(bf16[16,64,256]{2,1,0:T(8,128)(2,1)S(1)} %get-tuple-element.37), channel_id=1, source_target_pairs={{0,16},{16,0},{1,17},{17,1},{2,18},{18,2},{3,19},{19,3},{4,20},{20... | collective-permute-start | bytes 1572872 | tf_op jit(solution)/shard_map/reduce_plane/ppermute | solution.py:226
  53.2 2.5 %collective-permute-start.1 = (bf16[8,64,256]{2,1,0:T(8,128)(2,1)S(1)}, bf16[8,64,256]{2,1,0:T(8,128)(2,1)S(1)}, u32[]{:S(2)}, u32[]{:S(2)}) collective-permute-start(bf16[8,64,256]{2,1,0:T(8,128)(2,1)S(1)} %get-tuple-element.33), channel_id=1, source_target_pairs={{0,1},{1,0},{2,3},{3,2},{4,5},{5,4},{6,7},{7,6},{8,9},{9,8},{10,11... | collective-permute-start | bytes 786440 | tf_op jit(solution)/shard_map/reduce_near/ppermute | solution.py:226
  55.7 0.0 collective-permute-done.3.got
  55.7 0.9 reduce_plane.4
  56.6 7.0 %all-to-all-start.1 = ((bf16[16,64,256]{2,1,0:T(8,128)(2,1)}), bf16[16,64,256]{2,1,0:T(8,128)(2,1)}, u32[]{:S(2)}, u32[]{:S(2)}) async-start(bf16[16,64,256]{2,1,0:T(8,128)(2,1)} %reduce_plane.4), calls=%async_computation.1 | async-start | bytes 1048576 | tf_op jit(solution)/shard_map/reduce_plane/all_to_all | solution.py:230
  63.7 0.0 collective-permute-done.1.got
  63.7 0.0 copy-start
  63.7 0.0 copy-start.2
  63.7 0.0 copy-start.3
  63.7 0.1 reduce_mid.2
  63.8 4.8 %collective-permute-start.2 = (bf16[4,64,256]{2,1,0:T(8,128)(2,1)S(1)}, bf16[4,64,256]{2,1,0:T(8,128)(2,1)S(1)}, u32[]{:S(2)}, u32[]{:S(2)}) collective-permute-start(bf16[4,64,256]{2,1,0:T(8,128)(2,1)S(1)} %get-tuple-element.35), channel_id=1, source_target_pairs={{0,2},{2,0},{1,3},{3,1},{4,6},{6,4},{5,7},{7,5},{8,10},{10,8},{9,1... | collective-permute-start | bytes 393224 | tf_op jit(solution)/shard_map/reduce_mid/ppermute | solution.py:226
  68.6 6.0 %all-to-all-done.1.pieces = bf16[16,64,256]{2,1,0:T(8,128)(2,1)} async-done(((bf16[16,64,256]{2,1,0:T(8,128)(2,1)}), bf16[16,64,256]{2,1,0:T(8,128)(2,1)}, u32[]{:S(2)}, u32[]{:S(2)}) %all-to-all-start.1) | async-done | bytes 524320 | tf_op jit(solution)/shard_map/reduce_plane/all_to_all | solution.py:230
  74.5 1.1 reduce_plane.5.from_plane
  75.7 21.6 %all_to_all.40.from_line = bf16[4,64,256]{2,1,0:T(8,128)(2,1)S(1)} all-to-all(bf16[4,64,256]{2,1,0:T(8,128)(2,1)S(1)} %add_convert_fusion.1), channel_id=1, replica_groups=mesh['y'=4,'x'=4,'core'=2,'far'=4,'mid'=2,'near'=2] {'far'}, dimensions={0} | all-to-all | bytes 262144 | tf_op jit(solution)/shard_map/reduce_far/all_to_all | solution.py:230
  97.3 0.9 between.1
  98.2 4.2 %all-to-all-start.3 = ((bf16[16,64,256]{2,1,0:T(8,128)(2,1)}), bf16[16,64,256]{2,1,0:T(8,128)(2,1)S(1)}, u32[]{:S(2)}, u32[]{:S(2)}) async-start(bf16[16,64,256]{2,1,0:T(8,128)(2,1)} %get-tuple-element.42), calls=%async_computation.3 | async-start | bytes 1048576 | tf_op jit(solution)/shard_map/gather_line/all_to_all | solution.py:230
  102.4 18.0 %all-gather.1 = bf16[1024,256]{1,0:T(8,128)(2,1)S(1)} all-gather(bf16[64,256]{1,0:T(8,128)(2,1)S(1)} %get-tuple-element.40), channel_id=3, replica_groups=mesh['y'=4,'x'=4,'core'=2,'far'=4,'mid'=2,'near'=2] {'y','x'}, dimensions={0}, use_global_device_ids=true | all-gather | bytes 557056 | tf_op jit(solution)/shard_map/gather_plane/all_gather | solution.py:249
  120.4 9.3 %collective-permute-start.4 = (bf16[16,64,256]{2,1,0:T(8,128)(2,1)S(1)}, bf16[16,64,256]{2,1,0:T(8,128)(2,1)S(1)}, u32[]{:S(2)}, u32[]{:S(2)}) collective-permute-start(bf16[16,64,256]{2,1,0:T(8,128)(2,1)S(1)} %bitcast.5), channel_id=1, source_target_pairs={{0,16},{16,0},{1,17},{17,1},{2,18},{18,2},{3,19},{19,3},{4,20},{20... | collective-permute-start | bytes 1572872 | tf_op jit(solution)/shard_map/gather_core/ppermute | solution.py:226
  129.8 0.1 add_add_fusion.1.places
  129.8 1.4 collective-permute-done.4.other_panel
  131.3 3.0 %products.3 = (bf16[16,64,256]{2,1,0:T(8,128)(2,1)S(1)}, bf16[16,64,256]{2,1,0:T(8,128)(2,1)S(1)}, bf16[8,64,256]{2,1,0:T(8,128)(2,1)S(1)}, bf16[8,64,256]{2,1,0:T(8,128)(2,1)S(1)}) custom-call(s32[19]{0:T(128)S(1)} %add_add_fusion.1.places, bf16[16,64,256]{2,1,0:T(8,128)(2,1)S(1)} %all-to-all-done.3.row_panel, bf16[16,64,256]{2,1,0:T(8,128)(2,1)S(1)} %bitcast.6, ...), custom_call_target="tpu_custom_call" | custom-call | flops 603979776 | bytes 4718592 | tf_op jit(solution)/shard_map/products/pallas_call | solution.py:256
  134.3 3.3 %collective-permute-start.7 = (bf16[16,64,256]{2,1,0:T(8,128)(2,1)S(1)}, bf16[16,64,256]{2,1,0:T(8,128)(2,1)S(1)}, u32[]{:S(2)}, u32[]{:S(2)}) collective-permute-start(bf16[16,64,256]{2,1,0:T(8,128)(2,1)S(1)} %get-tuple-element.49), channel_id=1, source_target_pairs={{0,16},{16,0},{1,17},{17,1},{2,18},{18,2},{3,19},{19,3},{4,20},{20... | collective-permute-start | bytes 1572872 | tf_op jit(solution)/shard_map/reduce_plane/ppermute | solution.py:226
  137.6 3.1 %collective-permute-start.5 = (bf16[8,64,256]{2,1,0:T(8,128)(2,1)S(1)}, bf16[8,64,256]{2,1,0:T(8,128)(2,1)S(1)}, u32[]{:S(2)}, u32[]{:S(2)}) collective-permute-start(bf16[8,64,256]{2,1,0:T(8,128)(2,1)S(1)} %get-tuple-element.45), channel_id=1, source_target_pairs={{0,1},{1,0},{2,3},{3,2},{4,5},{5,4},{6,7},{7,6},{8,9},{9,8},{10,11... | collective-permute-start | bytes 786440 | tf_op jit(solution)/shard_map/reduce_near/ppermute | solution.py:226
  140.7 0.0 collective-permute-done.7.got
  140.7 0.9 reduce_plane.6
  141.6 4.4 %all-to-all-start.4 = ((bf16[16,64,256]{2,1,0:T(8,128)(2,1)}), bf16[16,64,256]{2,1,0:T(8,128)(2,1)}, u32[]{:S(2)}, u32[]{:S(2)}) async-start(bf16[16,64,256]{2,1,0:T(8,128)(2,1)} %reduce_plane.6), calls=%async_computation.4 | async-start | bytes 1048576 | tf_op jit(solution)/shard_map/reduce_plane/all_to_all | solution.py:230
  146.0 1.4 collective-permute-done.5.got
  147.4 0.1 reduce_mid.3
  147.5 4.1 %collective-permute-start.6 = (bf16[4,64,256]{2,1,0:T(8,128)(2,1)S(1)}, bf16[4,64,256]{2,1,0:T(8,128)(2,1)S(1)}, u32[]{:S(2)}, u32[]{:S(2)}) collective-permute-start(bf16[4,64,256]{2,1,0:T(8,128)(2,1)S(1)} %get-tuple-element.47), channel_id=1, source_target_pairs={{0,2},{2,0},{1,3},{3,1},{4,6},{6,4},{5,7},{7,5},{8,10},{10,8},{9,1... | collective-permute-start | bytes 393224 | tf_op jit(solution)/shard_map/reduce_mid/ppermute | solution.py:226
  151.6 5.0 %all-to-all-done.4.pieces = bf16[16,64,256]{2,1,0:T(8,128)(2,1)} async-done(((bf16[16,64,256]{2,1,0:T(8,128)(2,1)}), bf16[16,64,256]{2,1,0:T(8,128)(2,1)}, u32[]{:S(2)}, u32[]{:S(2)}) %all-to-all-start.4) | async-done | bytes 524320 | tf_op jit(solution)/shard_map/reduce_plane/all_to_all | solution.py:230
  156.6 1.1 reduce_plane.7.from_plane
  157.8 24.7 %all_to_all.41.from_line = bf16[4,64,256]{2,1,0:T(8,128)(2,1)S(1)} all-to-all(bf16[4,64,256]{2,1,0:T(8,128)(2,1)S(1)} %add_convert_fusion), channel_id=1, replica_groups=mesh['y'=4,'x'=4,'core'=2,'far'=4,'mid'=2,'near'=2] {'far'}, dimensions={0} | all-to-all | bytes 262144 | tf_op jit(solution)/shard_map/reduce_far/all_to_all | solution.py:230
  182.5 0.3 last.1
  182.8 15.1 %all_to_all.42 = f32[32,1,1152]{2,1,0:T(1,128)S(1)} all-to-all(f32[32,1,1152]{2,1,0:T(1,128)S(1)} %get-tuple-element.53), channel_id=1, replica_groups=mesh['y'=4,'x'=4,'core'=2,'far'=4,'mid'=2,'near'=2] {'y','x','core'}, dimensions={0} | all-to-all | bytes 294912 | tf_op jit(solution)/shard_map/gram_plane/all_to_all | solution.py:230
  197.9 0.1 reduce_sum.18
  198.0 15.2 %all_to_all.43 = f32[16,1,1152]{2,1,0:T(1,128)S(1)} all-to-all(f32[16,1,1152]{2,1,0:T(1,128)S(1)} %broadcast_in_dim.5), channel_id=1, replica_groups=mesh['y'=4,'x'=4,'core'=2,'far'=4,'mid'=2,'near'=2] {'far','mid','near'}, dimensions={0} | all-to-all | bytes 147456 | tf_op jit(solution)/shard_map/gram_line/all_to_all | solution.py:230
  213.2 0.1 reduce_sum.19
  213.3 3.5 %all-gather.3.parts = f32[2,1,1152]{2,1,0:T(1,128)S(1)} all-gather(f32[1,1,1152]{2,1,0:T(1,128)S(1)} %reshape.16), channel_id=4, replica_groups=mesh['y'=4,'x'=4,'core'=2,'far'=4,'mid'=2,'near'=2] {'core'}, dimensions={0}, use_global_device_ids=true | all-gather | bytes 13824 | tf_op jit(solution)/shard_map/gram_pair/all_gather | solution.py:306
  216.8 2.7 %whiten.1 = bf16[64,256]{1,0:T(8,128)(2,1)} custom-call(f32[2,1,1152]{2,1,0:T(1,128)S(1)} %all-gather.3.parts, bf16[64,256]{1,0:T(8,128)(2,1)S(1)} %get-tuple-element.54.fresh), custom_call_target="tpu_custom_call" | custom-call | tf_op jit(solution)/shard_map/whiten/pallas_call | solution.py:308
  (12 shorter events, 0.1 us)
Async XLA Ops:
  1.6 44.5 %all-to-all-start = ((bf16[16,64,256]{2,1,0:T(8,128)(2,1)}), bf16[16,64,256]{2,1,0:T(8,128)(2,1)S(1)}, u32[]{:S(2)}, u32[]{:S(2)}) async-start(bf16[16,64,256]{2,1,0:T(8,128)(2,1)} %broadcast_in_dim.4), calls=%async_computation | async-start | bytes 1048576 | tf_op jit(solution)/shard_map/gather_line/all_to_all | solution.py:230
  37.6 8.6 %collective-permute-start = (bf16[16,64,256]{2,1,0:T(8,128)(2,1)S(1)}, bf16[16,64,256]{2,1,0:T(8,128)(2,1)S(1)}, u32[]{:S(2)}, u32[]{:S(2)}) collective-permute-start(bf16[16,64,256]{2,1,0:T(8,128)(2,1)S(1)} %bitcast.3), channel_id=1, source_target_pairs={{0,16},{16,0},{1,17},{17,1},{2,18},{18,2},{3,19},{19,3},{4,20},{20... | collective-permute-start | bytes 1572872 | tf_op jit(solution)/shard_map/gather_core/ppermute | solution.py:226
  49.2 6.5 %collective-permute-start.3 = (bf16[16,64,256]{2,1,0:T(8,128)(2,1)S(1)}, bf16[16,64,256]{2,1,0:T(8,128)(2,1)S(1)}, u32[]{:S(2)}, u32[]{:S(2)}) collective-permute-start(bf16[16,64,256]{2,1,0:T(8,128)(2,1)S(1)} %get-tuple-element.37), channel_id=1, source_target_pairs={{0,16},{16,0},{1,17},{17,1},{2,18},{18,2},{3,19},{19,3},{4,20},{20... | collective-permute-start | bytes 1572872 | tf_op jit(solution)/shard_map/reduce_plane/ppermute | solution.py:226
  53.2 10.4 %collective-permute-start.1 = (bf16[8,64,256]{2,1,0:T(8,128)(2,1)S(1)}, bf16[8,64,256]{2,1,0:T(8,128)(2,1)S(1)}, u32[]{:S(2)}, u32[]{:S(2)}) collective-permute-start(bf16[8,64,256]{2,1,0:T(8,128)(2,1)S(1)} %get-tuple-element.33), channel_id=1, source_target_pairs={{0,1},{1,0},{2,3},{3,2},{4,5},{5,4},{6,7},{7,6},{8,9},{9,8},{10,11... | collective-permute-start | bytes 786440 | tf_op jit(solution)/shard_map/reduce_near/ppermute | solution.py:226
  56.6 17.9 %all-to-all-start.1 = ((bf16[16,64,256]{2,1,0:T(8,128)(2,1)}), bf16[16,64,256]{2,1,0:T(8,128)(2,1)}, u32[]{:S(2)}, u32[]{:S(2)}) async-start(bf16[16,64,256]{2,1,0:T(8,128)(2,1)} %reduce_plane.4), calls=%async_computation.1 | async-start | bytes 1048576 | tf_op jit(solution)/shard_map/reduce_plane/all_to_all | solution.py:230
  63.7 33.6 %copy-start = (f32[256]{0:T(256)S(1)}, f32[256]{0:T(256)}, u32[]{:S(2)}) copy-start(f32[256]{0:T(256)} %param.7) | copy-start | bytes 3076
  63.7 66.0 %copy-start.2 = (s32[9]{0:T(128)S(1)}, s32[9]{0:T(128)}, u32[]{:S(2)}) copy-start(s32[9]{0:T(128)} %param.9) | copy-start | bytes 112
  63.7 66.0 %copy-start.3 = (s32[9]{0:T(128)S(1)}, s32[9]{0:T(128)}, u32[]{:S(2)}) copy-start(s32[9]{0:T(128)} %param.10) | copy-start | bytes 112
  63.8 11.9 %collective-permute-start.2 = (bf16[4,64,256]{2,1,0:T(8,128)(2,1)S(1)}, bf16[4,64,256]{2,1,0:T(8,128)(2,1)S(1)}, u32[]{:S(2)}, u32[]{:S(2)}) collective-permute-start(bf16[4,64,256]{2,1,0:T(8,128)(2,1)S(1)} %get-tuple-element.35), channel_id=1, source_target_pairs={{0,2},{2,0},{1,3},{3,1},{4,6},{6,4},{5,7},{7,5},{8,10},{10,8},{9,1... | collective-permute-start | bytes 393224 | tf_op jit(solution)/shard_map/reduce_mid/ppermute | solution.py:226
  98.2 33.1 %all-to-all-start.3 = ((bf16[16,64,256]{2,1,0:T(8,128)(2,1)}), bf16[16,64,256]{2,1,0:T(8,128)(2,1)S(1)}, u32[]{:S(2)}, u32[]{:S(2)}) async-start(bf16[16,64,256]{2,1,0:T(8,128)(2,1)} %get-tuple-element.42), calls=%async_computation.3 | async-start | bytes 1048576 | tf_op jit(solution)/shard_map/gather_line/all_to_all | solution.py:230
  120.4 10.8 %collective-permute-start.4 = (bf16[16,64,256]{2,1,0:T(8,128)(2,1)S(1)}, bf16[16,64,256]{2,1,0:T(8,128)(2,1)S(1)}, u32[]{:S(2)}, u32[]{:S(2)}) collective-permute-start(bf16[16,64,256]{2,1,0:T(8,128)(2,1)S(1)} %bitcast.5), channel_id=1, source_target_pairs={{0,16},{16,0},{1,17},{17,1},{2,18},{18,2},{3,19},{19,3},{4,20},{20... | collective-permute-start | bytes 1572872 | tf_op jit(solution)/shard_map/gather_core/ppermute | solution.py:226
  134.3 6.4 %collective-permute-start.7 = (bf16[16,64,256]{2,1,0:T(8,128)(2,1)S(1)}, bf16[16,64,256]{2,1,0:T(8,128)(2,1)S(1)}, u32[]{:S(2)}, u32[]{:S(2)}) collective-permute-start(bf16[16,64,256]{2,1,0:T(8,128)(2,1)S(1)} %get-tuple-element.49), channel_id=1, source_target_pairs={{0,16},{16,0},{1,17},{17,1},{2,18},{18,2},{3,19},{19,3},{4,20},{20... | collective-permute-start | bytes 1572872 | tf_op jit(solution)/shard_map/reduce_plane/ppermute | solution.py:226
  137.6 9.8 %collective-permute-start.5 = (bf16[8,64,256]{2,1,0:T(8,128)(2,1)S(1)}, bf16[8,64,256]{2,1,0:T(8,128)(2,1)S(1)}, u32[]{:S(2)}, u32[]{:S(2)}) collective-permute-start(bf16[8,64,256]{2,1,0:T(8,128)(2,1)S(1)} %get-tuple-element.45), channel_id=1, source_target_pairs={{0,1},{1,0},{2,3},{3,2},{4,5},{5,4},{6,7},{7,6},{8,9},{9,8},{10,11... | collective-permute-start | bytes 786440 | tf_op jit(solution)/shard_map/reduce_near/ppermute | solution.py:226
  141.6 15.0 %all-to-all-start.4 = ((bf16[16,64,256]{2,1,0:T(8,128)(2,1)}), bf16[16,64,256]{2,1,0:T(8,128)(2,1)}, u32[]{:S(2)}, u32[]{:S(2)}) async-start(bf16[16,64,256]{2,1,0:T(8,128)(2,1)} %reduce_plane.6), calls=%async_computation.4 | async-start | bytes 1048576 | tf_op jit(solution)/shard_map/reduce_plane/all_to_all | solution.py:230
  147.4 35.1 %copy-start.1 = (f32[256]{0:T(256)S(1)}, f32[256]{0:T(256)}, u32[]{:S(2)}) copy-start(f32[256]{0:T(256)} %param.7) | copy-start | bytes 3076
  147.5 10.3 %collective-permute-start.6 = (bf16[4,64,256]{2,1,0:T(8,128)(2,1)S(1)}, bf16[4,64,256]{2,1,0:T(8,128)(2,1)S(1)}, u32[]{:S(2)}, u32[]{:S(2)}) collective-permute-start(bf16[4,64,256]{2,1,0:T(8,128)(2,1)S(1)} %get-tuple-element.47), channel_id=1, source_target_pairs={{0,2},{2,0},{1,3},{3,1},{4,6},{6,4},{5,7},{7,5},{8,10},{10,8},{9,1... | collective-permute-start | bytes 393224 | tf_op jit(solution)/shard_map/reduce_mid/ppermute | solution.py:226
